TPU v7x, 128 devices: a whole 4x4x4 slice. The times are simulated.
128 devices in a mesh: trans: 16 (over z_lo, x, core), pw: 8 (over z_hi, y).
Axes of the slice: x: 4, y: 4, z: 4 (z_hi: 2, z_lo: 2; z = z_hi * 2 + z_lo), core: 2. Of those that a mesh axis runs over, the one named last changes fastest.
Arguments:
- densities: bfloat16 [65536, 5120], P('trans', 'pw'), may hold values from -1.75 to 1.75
- coulomb: float32 [5120], P('pw'), may hold values from 0.25 to 4
- pairs: int32 [288, 2], replicated, may hold values from 0 to 127, as said below
- owner: int32 [128], replicated, may hold values from 0 to 127, as said below
Outputs:
- kernel: float32 [512, 288, 512], P('pw', 'trans')
- kernel_t: float32 [512, 288, 512], P('pw', 'trans')
Inputs may be any that keep to these rules, and one draw needn't show every extreme that they name: `pairs`: pair p lists its first block at owner p // 18. Write s_q for (owner of the second block minus owner of the first) taken modulo 16 into -2 to 2; it depends only on the list position q = p % 18, the same for every owner. The value 0 is taken by 6 positions, each other value by exactly 3 positions. `owner`: A permutation of the 128 storage slots.
All inputs are finite; a program needn't handle non-finite values.
Results may differ from a plain program's by a relative error of at most 0.0027.
Values may be sent and summed in bfloat16 or wider, within the bound.
No kernel may reach another device: no remote copies, remote signals or barrier semaphores. Data moves between devices by JAX's collectives and lax.ppermute only.
A program may use at most 192 MiB of HBM per device.

v0:
```python
import jax
import jax.numpy as jnp
from jax import lax
from jax.sharding import PartitionSpec as P

BLK = 512
SPAN = 2
MULT = 3


def shifted(value, axis, steps):
    count = lax.axis_size(axis)
    pairs = [(source, (source + steps) % count) for source in range(count)]
    return lax.ppermute(value, axis, pairs)


def body(densities, coulomb, pairs, owner):
    ntrans = lax.axis_size("trans")
    device = lax.axis_index("trans")
    width = densities.shape[1]
    stored = densities.shape[0] // BLK
    listed = pairs.shape[0] // ntrans
    local = densities.reshape(stored, BLK, width)
    mine = lax.dynamic_slice_in_dim(pairs, device * listed, listed, 0)
    first_slot = owner[mine[:, 0]] % stored
    second_slot = owner[mine[:, 1]] % stored
    second_owner = owner[mine[:, 1]] // stored
    distance = (second_owner - device + SPAN) % ntrans - SPAN
    position = jnp.arange(listed, dtype=jnp.int32)
    weighted = (local.astype(jnp.float32) * coulomb).astype(jnp.bfloat16)
    left = weighted[first_slot]
    neighbours = []
    for step in range(-SPAN, SPAN + 1):
        if step == 0:
            neighbours.append(local)
        else:
            neighbours.append(shifted(local, "trans", -step))
    gathered = jnp.stack(neighbours, axis=0)
    right = gathered[distance + SPAN, second_slot]
    kernel = lax.psum_scatter(
        jnp.einsum("qrg,qcg->rqc", left, right, preferred_element_type=jnp.float32),
        "pw",
        scatter_dimension=0,
        tiled=True,
    )
    columns = lax.all_to_all(kernel, "pw", split_axis=2, concat_axis=0, tiled=True)
    flipped = jnp.transpose(columns, (2, 1, 0))
    mirrored = flipped
    for step in range(-SPAN, SPAN + 1):
        if step != 0:
            keyed = jnp.where(distance == step, 0, 1).astype(jnp.int32) * listed + position
            chosen = jnp.argsort(keyed)[:MULT]
            arrived = shifted(flipped[:, chosen], "trans", step)
            mirrored = mirrored.at[:, chosen].set(arrived)
    return (kernel, mirrored)


def solution(mesh):
    in_specs = (P("trans", "pw"), P("pw"), P(), P())
    out_specs = (P("pw", "trans", None), P("pw", "trans", None))
    return jax.shard_map(body, mesh=mesh, in_specs=in_specs, out_specs=out_specs, check_vma=False)
```

profile of v0, /device:TPU:6, one launch (start us, length us, event | category | flops | bytes accessed | tf_op | source)
XLA Modules:
  0.0 622.1 jit_solution(14603613552837608487)
XLA Ops:
  7.2 0.0 copy-start
  7.2 0.0 reduce-scatter.2.cloned.1.call-start
  7.2 1.9 collective-permute-start
  9.1 0.0 collective-permute-start.1
  9.1 1.7 collective-permute-start.2
  10.9 0.2 collective-permute-start.3
  11.1 0.0 copy-done
  11.1 0.1 constant_dynamic-slice_fusion
  11.2 1.4 gather_fusion
  12.5 1.4 gather_fusion.2
  13.9 5.8 multiply_convert_fusion
  19.7 8.9 %gather_fusion.3 = bf16[18,512,640]{2,1,0:T(8,128)(2,1)} fusion(bf16[8,512,640]{2,1,0:T(8,128)(2,1)} %multiply_convert_fusion, s32[1024]{0:T(1024)S(1)} %pad_clamp_fusion.4), kind=kCustom, calls=%fused_computation.3 | custom fusion | bytes 23593032 | tf_op jit(solution)/shard_map/gather | solution.py:31
  28.5 95.0 %collective-permute-done = bf16[8,512,640]{2,1,0:T(8,128)(2,1)} collective-permute-done((bf16[8,512,640]{2,1,0:T(8,128)(2,1)}, bf16[8,512,640]{2,1,0:T(8,128)(2,1)}, u32[]{:S(2)}, u32[]{:S(2)}) %collective-permute-start) | collective-permute-done | bytes 5242912 | tf_op jit(solution)/shard_map/ppermute | solution.py:14
  123.5 0.0 slice-start
  123.5 5.5 bitcast_dynamic-update-slice_fusion.3
  129.0 49.5 %collective-permute-done.1 = bf16[8,512,640]{2,1,0:T(8,128)(2,1)} collective-permute-done((bf16[8,512,640]{2,1,0:T(8,128)(2,1)}, bf16[8,512,640]{2,1,0:T(8,128)(2,1)}, u32[]{:S(2)}, u32[]{:S(2)}) %collective-permute-start.1) | collective-permute-done | bytes 5242912 | tf_op jit(solution)/shard_map/ppermute | solution.py:14
  178.6 5.4 bitcast_dynamic-update-slice_fusion.2
  183.9 0.0 slice-done
  184.0 0.0 slice-done.1
  184.0 2.8 constant_dynamic-update-slice_fusion
  186.8 0.0 collective-permute-done.2
  186.8 5.4 bitcast_dynamic-update-slice_fusion.1
  192.2 0.0 collective-permute-done.3
  192.2 5.3 bitcast_dynamic-update-slice_fusion
  197.5 14.9 %gather_fusion.1 = bf16[18,512,640]{2,1,0:T(8,128)(2,1)} fusion(bf16[5,8,512,640]{3,2,1,0:T(8,128)(2,1)} %bitcast_dynamic-update-slice_fusion, s32[18]{0:T(128)S(1)} %fusion.20), kind=kCustom, calls=%fused_computation.1 | custom fusion | bytes 23593104 | tf_op jit(solution)/shard_map/gather | solution.py:39
  212.5 15.8 %convolution_bitcast_fusion = f32[512,18,512]{0,2,1:T(8,128)} fusion(bf16[18,512,640]{2,1,0:T(8,128)(2,1)} %gather_fusion.1, bf16[18,512,640]{2,1,0:T(8,128)(2,1)} %gather_fusion.3), kind=kOutput, calls=%fused_computation.13 | convolution fusion | flops 6039797760 | bytes 42467328 | tf_op jit(solution)/shard_map/qrg,qcg->rqc/dot_general | solution.py:41
  228.3 22.7 %copy.10 = f32[512,18,512]{2,1,0:T(8,128)} copy(f32[512,18,512]{0,2,1:T(8,128)} %convolution_bitcast_fusion) | data formatting | bytes 37748736 | tf_op jit(solution)/shard_map/qrg,qcg->rqc/transpose | solution.py:41
  251.0 0.0 reduce-scatter.2.cloned.1.call-update
  251.1 265.6 %reduce-scatter.2.cloned.1.call-done = f32[64,18,512]{2,1,0:T(8,128)} async-done(((f32[512,18,512]{2,1,0:T(8,128)}), f32[64,18,512]{2,1,0:T(8,128)}) %reduce-scatter.2.cloned.1.call-update) | async-done | bytes 2359312 | tf_op jit(solution)/shard_map/reduce_scatter | solution.py:40
  516.6 6.4 %copy.11 = f32[64,18,512]{0,1,2:T(8,128)} copy(f32[64,18,512]{2,1,0:T(8,128)} %reduce-scatter.2.cloned.1.call-done) | data formatting | bytes 4718592 | tf_op jit(solution)/shard_map/reduce_scatter | solution.py:40
  523.1 7.9 %reshape.287 = f32[8,1,73728]{2,1,0:T(1,128)} reshape(f32[512,18,64]{2,1,0:T(8,128)} %bitcast.58) | data formatting | bytes 4718592
  530.9 4.9 all-to-all-start
  535.8 1.6 sort.62
  537.4 1.6 sort.61
  539.0 1.6 sort.60
  540.6 1.6 sort.59
  542.3 0.0 copy-start.3
  542.4 23.1 %all-to-all-done = f32[8,1,73728]{2,1,0:T(1,128)S(1)} async-done(((f32[8,1,73728]{2,1,0:T(1,128)}), f32[8,1,73728]{2,1,0:T(1,128)S(1)}, u32[]{:S(2)}, u32[]{:S(2)}) %all-to-all-start) | async-done | bytes 2359328 | tf_op jit(solution)/shard_map/all_to_all | solution.py:46
  565.5 0.5 broadcast.350
  566.0 8.7 %reduce = f32[8,73728]{1,0:T(8,128)} reduce(f32[8,1,73728]{2,1,0:T(1,128)S(1)} %all-to-all-done, f32[]{:T(128)} %broadcast.350), dimensions={1}, to_apply=%all_to_all.13.reduce_sub_computation | reduce | bytes 4718596 | tf_op jit(solution)/shard_map/all_to_all | solution.py:46
  574.7 7.0 %reshape.288 = f32[512,18,64]{2,1,0:T(8,128)} reshape(f32[8,73728]{1,0:T(8,128)} %reduce) | data formatting | bytes 4718592
  581.7 0.0 copy-done.3
  581.7 8.0 %copy.15 = f32[64,18,8,64]{0,2,3,1:T(8,128)} copy(f32[64,18,8,64]{0,1,3,2:T(8,128)} %bitcast.59) | data formatting | bytes 4718592 | tf_op jit(solution)/shard_map/all_to_all | solution.py:46
  589.7 3.6 all_to_all.16
  593.4 1.3 gather_fusion.4
  594.7 1.0 collective-permute-start.4
  595.7 1.3 gather_fusion.5
  597.0 0.0 collective-permute-start.5
  597.0 1.3 gather_fusion.6
  598.3 0.5 collective-permute-start.6
  598.9 1.3 gather_fusion.7
  600.2 3.1 collective-permute-start.7
  603.3 4.7 copy.13
  607.9 0.0 collective-permute-done.4
  607.9 1.8 scatter_fusion
  609.7 0.0 collective-permute-done.5
  609.7 0.7 scatter_fusion.1
  610.4 0.0 collective-permute-done.6
  610.4 0.7 scatter_fusion.2
  611.1 2.0 collective-permute-done.7
  613.2 0.7 scatter_fusion.3
  613.9 0.0 copy-start.2
  613.9 1.4 copy-done.2
  615.3 0.0 copy-done.1
  (22 shorter events, 0.1 us)
Async XLA Ops:
  7.2 3.9 copy-start
  7.2 509.4 %reduce-scatter.2.cloned.1.call-start = ((), (), s32[]{:S(2)}) async-start(), calls=%async_computation.2 | async-start | bytes 28311552 | tf_op jit(solution)/shard_map/reduce_scatter | solution.py:40
  7.2 116.3 %collective-permute-start = (bf16[8,512,640]{2,1,0:T(8,128)(2,1)}, bf16[8,512,640]{2,1,0:T(8,128)(2,1)}, u32[]{:S(2)}, u32[]{:S(2)}) collective-permute-start(bf16[8,512,640]{2,1,0:T(8,128)(2,1)} %bitcast.60), channel_id=1, source_target_pairs={{0,16},{8,24},{16,32},{24,40},{32,48},{40,56},{48,64},{56,72},{64,... | collective-permute-start | bytes 15728648 | tf_op jit(solution)/shard_map/ppermute | solution.py:14
  9.1 169.4 %collective-permute-start.1 = (bf16[8,512,640]{2,1,0:T(8,128)(2,1)}, bf16[8,512,640]{2,1,0:T(8,128)(2,1)}, u32[]{:S(2)}, u32[]{:S(2)}) collective-permute-start(bf16[8,512,640]{2,1,0:T(8,128)(2,1)} %bitcast.61), channel_id=1, source_target_pairs={{0,8},{8,16},{16,24},{24,32},{32,40},{40,48},{48,56},{56,64},{64,7... | collective-permute-start | bytes 15728648 | tf_op jit(solution)/shard_map/ppermute | solution.py:14
  9.1 177.6 %collective-permute-start.2 = (bf16[8,512,640]{2,1,0:T(8,128)(2,1)}, bf16[8,512,640]{2,1,0:T(8,128)(2,1)}, u32[]{:S(2)}, u32[]{:S(2)}) collective-permute-start(bf16[8,512,640]{2,1,0:T(8,128)(2,1)} %bitcast.62), channel_id=1, source_target_pairs={{0,120},{8,0},{16,8},{24,16},{32,24},{40,32},{48,40},{56,48},{64,5... | collective-permute-start | bytes 15728648 | tf_op jit(solution)/shard_map/ppermute | solution.py:14
  10.9 181.3 %collective-permute-start.3 = (bf16[8,512,640]{2,1,0:T(8,128)(2,1)}, bf16[8,512,640]{2,1,0:T(8,128)(2,1)}, u32[]{:S(2)}, u32[]{:S(2)}) collective-permute-start(bf16[8,512,640]{2,1,0:T(8,128)(2,1)} %bitcast.63), channel_id=1, source_target_pairs={{0,112},{8,120},{16,0},{24,8},{32,16},{40,24},{48,32},{56,40},{64,... | collective-permute-start | bytes 15728648 | tf_op jit(solution)/shard_map/ppermute | solution.py:14
  123.5 60.4 %slice-start = ((s8[5242880]{0:T(1024)(128)(4,1)}), s8[4194304]{0:T(1024)(128)(4,1)S(1)}, s32[]{:S(2)}) async-start(s8[5242880]{0:T(1024)(128)(4,1)} %bitcast.65), calls=%async_computation.3 | async-start | bytes 8388608
  129.0 54.9 %slice-start.1 = ((s8[5242880]{0:T(1024)(128)(4,1)}), s8[1048576]{0:T(1024)(128)(4,1)S(1)}, s32[]{:S(2)}) async-start(s8[5242880]{0:T(1024)(128)(4,1)} %bitcast.65), calls=%async_computation.4 | async-start | bytes 2097152
  530.9 34.6 %all-to-all-start = ((f32[8,1,73728]{2,1,0:T(1,128)}), f32[8,1,73728]{2,1,0:T(1,128)S(1)}, u32[]{:S(2)}, u32[]{:S(2)}) async-start(f32[8,1,73728]{2,1,0:T(1,128)} %reshape.287), calls=%async_computation.1 | async-start | bytes 4718592 | tf_op jit(solution)/shard_map/all_to_all | solution.py:46
  542.3 39.4 %copy-start.3 = (s32[3]{0:T(128)}, s32[3]{0:T(128)S(1)}, u32[]{:S(2)}) copy-start(s32[3]{0:T(128)S(1)} %compare_select_fusion.3) | copy-start | bytes 40
  594.7 13.3 %collective-permute-start.4 = (f32[64,3,512]{2,0,1:T(8,128)}, f32[64,3,512]{2,0,1:T(8,128)}, u32[]{:S(2)}, u32[]{:S(2)}) collective-permute-start(f32[64,3,512]{2,0,1:T(8,128)} %bitcast.16), channel_id=1, source_target_pairs={{0,112},{8,120},{16,0},{24,8},{32,16},{40,24},{48,32},{56,40},{64,... | collective-permute-start | bytes 1179656 | tf_op jit(solution)/shard_map/ppermute | solution.py:14
  597.0 12.7 %collective-permute-start.5 = (f32[64,3,512]{2,0,1:T(8,128)}, f32[64,3,512]{2,0,1:T(8,128)S(1)}, u32[]{:S(2)}, u32[]{:S(2)}) collective-permute-start(f32[64,3,512]{2,0,1:T(8,128)} %bitcast.18), channel_id=1, source_target_pairs={{0,120},{8,0},{16,8},{24,16},{32,24},{40,32},{48,40},{56,48},{64,5... | collective-permute-start | bytes 1179656 | tf_op jit(solution)/shard_map/ppermute | solution.py:14
  598.3 16.9 %copy-start.1 = (s32[288,2]{0,1:T(2,128)S(1)}, s32[288,2]{0,1:T(2,128)}, u32[]{:S(2)}) copy-start(s32[288,2]{0,1:T(2,128)} %param.6) | copy-start | bytes 6916
  598.3 12.1 %collective-permute-start.6 = (f32[64,3,512]{2,0,1:T(8,128)}, f32[64,3,512]{2,0,1:T(8,128)S(1)}, u32[]{:S(2)}, u32[]{:S(2)}) collective-permute-start(f32[64,3,512]{2,0,1:T(8,128)} %bitcast.20), channel_id=1, source_target_pairs={{0,8},{8,16},{16,24},{24,32},{32,40},{40,48},{48,56},{56,64},{64,7... | collective-permute-start | bytes 1179656 | tf_op jit(solution)/shard_map/ppermute | solution.py:14
  600.2 13.0 %collective-permute-start.7 = (f32[64,3,512]{2,0,1:T(8,128)}, f32[64,3,512]{2,0,1:T(8,128)S(1)}, u32[]{:S(2)}, u32[]{:S(2)}) collective-permute-start(f32[64,3,512]{2,0,1:T(8,128)} %bitcast.77), channel_id=1, source_target_pairs={{0,16},{8,24},{16,32},{24,40},{32,48},{40,56},{48,64},{56,72},{64,... | collective-permute-start | bytes 1179656 | tf_op jit(solution)/shard_map/ppermute | solution.py:14
  613.9 1.4 copy-start.2
Sparse Core Ops, SparseCore 0:
  251.2 265.3 reduce-scatter.1
where the time goes:
time: 630 us; the launch traced here: 622 us
  waiting for transfers between devices  435 us (69%)
  local copies, waits for them, and re-layouts  122 us (19%)
  other arithmetic  21 us (3%)
  matrix products  15.8 us (3%)
  between operations  14.2 us (2%)
  starting transfers between devices  13.4 us (2%)
    reduce_scatter x1, waiting for transfers between devices, body(): lax.psum_scatter(jnp.einsum('qrg,qcg->rqc', left, right, preferred_elemen...  266 us
    ppermute x8, waiting for transfers between devices, shifted(): return lax.ppermute(value, axis, pairs)  147 us
    unnamed x19, local copies, waits for them, and re-layouts  40.1 us
    all_to_all x1, waiting for transfers between devices, body(): lax.all_to_all(kernel, 'pw', split_axis=2, concat_axis=0, tiled=True)  23.1 us
    transpose x1, local copies, waits for them, and re-layouts, body(): jnp.einsum('qrg,qcg->rqc', left, right, preferred_element_type=jnp.float32)  22.7 us
    dot_general x1, matrix products, body(): jnp.einsum('qrg,qcg->rqc', left, right, preferred_element_type=jnp.float32)  15.8 us
    gather x1, local copies, waits for them, and re-layouts, body(): right = gathered[distance + SPAN, second_slot]  14.9 us
  transfers between devices with their start and end apart: 10, of which 5 were waited for; matrix products, arithmetic and copies ran while one was open for 9% of the time, Pallas kernels for 0%

commit v1 on v0

v1 whole, which is shorter than its diff:
```python
import jax
import jax.numpy as jnp
from jax import lax
from jax.experimental import pallas as pl
from jax.experimental.pallas import tpu as pltpu
from jax.sharding import PartitionSpec as P

BLK = 512
SPAN = 2
MULT = 3
STORED = 8
LISTED = 18
LOCAL = 6
NTRANS = 16
NPW = 8
ROWS = BLK // NPW
HALF = ROWS // 2
STEPS = (1, -1, 2, -2)
ORDER, FIRST, SECOND, TABLE = 0, LISTED, 2 * LISTED, 3 * LISTED


def shifted(value, axis, steps):
    count = lax.axis_size(axis)
    pairs = [(source, (source + steps) % count) for source in range(count)]
    return lax.ppermute(value, axis, pairs)


def start_of(step):
    return 0 if step == 0 else LOCAL + MULT * STEPS.index(step)


def prepare_kernel(device_ref, pairs_ref, owner_ref, blocks_ref, table_ref, *rest):
    sends, sems = rest[: len(STEPS)], rest[len(STEPS)]
    device = device_ref[0]
    filled = {step: start_of(step) for step in (0, *STEPS)}
    for q in range(LISTED):
        pair = device * LISTED + q
        first = owner_ref[pairs_ref[0, pair]]
        second = owner_ref[pairs_ref[1, pair]]
        distance = (((second >> 3) - device + SPAN + NTRANS) & (NTRANS - 1)) - SPAN
        place = jnp.int32(0)
        for step in filled:
            here = distance == step
            place = jnp.where(here, filled[step], place)
            filled[step] = jnp.where(here, filled[step] + 1, filled[step])
        table_ref[ORDER + place] = jnp.int32(q)
        table_ref[FIRST + place] = first & (STORED - 1)
        table_ref[SECOND + place] = second & (STORED - 1)
    copies = []
    for at, step in enumerate(STEPS):
        target = (device - step + NTRANS) & (NTRANS - 1)
        for j in range(MULT):
            q = table_ref[ORDER + start_of(step) + j]
            slot = owner_ref[pairs_ref[1, target * LISTED + q]] & (STORED - 1)
            copies.append(pltpu.make_async_copy(blocks_ref.at[slot], sends[at].at[j], sems.at[at * MULT + j]))
            copies[-1].start()
    for copy in copies:
        copy.wait()


def prepare(device, pairs, owner, blocks):
    width = blocks.shape[2]
    smem = pl.BlockSpec(memory_space=pltpu.SMEM)
    anywhere = pl.BlockSpec(memory_space=pl.ANY)
    return pl.pallas_call(
        prepare_kernel,
        out_shape=[jax.ShapeDtypeStruct((TABLE,), jnp.int32)]
        + [jax.ShapeDtypeStruct((MULT, BLK, width), jnp.bfloat16)] * len(STEPS),
        in_specs=[smem, smem, smem, anywhere],
        out_specs=[smem] + [anywhere] * len(STEPS),
        scratch_shapes=[pltpu.SemaphoreType.DMA((MULT * len(STEPS),))],
        name="prepare",
    )(device, pairs, owner, blocks)


def products_kernel(count, table_ref, left_ref, coulomb_ref, *refs):
    rights, out_ref = refs[:-1], refs[-1]
    each = count // len(rights)
    weighted = (left_ref[0].astype(jnp.float32) * coulomb_ref[...]).astype(jnp.bfloat16)
    for at, right_ref in enumerate(rights):

        @pl.when(pl.program_id(0) // each == at)
        def _():
            part = lax.dot_general(
                weighted, right_ref[0], (((1,), (1,)), ((), ())), preferred_element_type=jnp.float32
            )
            out_ref[...] = part.astype(jnp.bfloat16).reshape(out_ref.shape)


def products(table, blocks, coulomb, rights, start, count):
    width = blocks.shape[2]
    each = count // len(rights)
    if rights[0].shape[0] == STORED:
        right_specs = [pl.BlockSpec((1, BLK, width), lambda i, table: (table[SECOND + start + i], 0, 0))]
    else:
        right_specs = [
            pl.BlockSpec((1, BLK, width), lambda i, table, at=at: (jnp.clip(i - at * each, 0, each - 1), 0, 0))
            for at in range(len(rights))
        ]
    return pl.pallas_call(
        lambda *refs: products_kernel(count, *refs),
        out_shape=jax.ShapeDtypeStruct((NPW, count, ROWS, BLK), jnp.bfloat16),
        grid_spec=pltpu.PrefetchScalarGridSpec(
            num_scalar_prefetch=1,
            grid=(count,),
            in_specs=[
                pl.BlockSpec((1, BLK, width), lambda i, table: (table[FIRST + start + i], 0, 0)),
                pl.BlockSpec((1, width), lambda i, table: (0, 0)),
                *right_specs,
            ],
            out_specs=pl.BlockSpec((NPW, 1, ROWS, BLK), lambda i, table: (0, i, 0, 0)),
        ),
        cost_estimate=pl.CostEstimate(
            flops=2 * count * BLK * BLK * width, bytes_accessed=count * (4 * BLK * width + 2 * BLK * BLK), transcendentals=0
        ),
        name="products",
    )(table, blocks, coulomb, *rights)


def total_kernel(table_ref, *refs):
    parts_ref, (kernel_ref, cut_ref) = refs[0], refs[-2:]
    total = jnp.sum(parts_ref[...].astype(jnp.float32), axis=0)[0]
    kernel_ref[0] = total
    both = jnp.concatenate([total, pltpu.roll(total, BLK - HALF, 1)], axis=0)
    columns = jnp.transpose(both, (1, 0))
    for target in range(NPW):
        cut_ref[target, 0] = columns[target * ROWS : target * ROWS + HALF].astype(cut_ref.dtype)


def totals(table, parts, kernel, start):
    count = parts.shape[1]
    carried = [] if kernel is None else [kernel]
    return pl.pallas_call(
        total_kernel,
        out_shape=[
            jax.ShapeDtypeStruct((LISTED, ROWS, BLK), jnp.float32),
            jax.ShapeDtypeStruct((NPW, count, HALF, 2 * ROWS), jnp.bfloat16),
        ],
        grid_spec=pltpu.PrefetchScalarGridSpec(
            num_scalar_prefetch=1,
            grid=(count,),
            in_specs=[pl.BlockSpec((NPW, 1, ROWS, BLK), lambda i, table: (0, i, 0, 0))]
            + [pl.BlockSpec(memory_space=pl.ANY)] * len(carried),
            out_specs=[
                pl.BlockSpec((1, ROWS, BLK), lambda i, table: (table[ORDER + start + i], 0, 0)),
                pl.BlockSpec((NPW, 1, HALF, 2 * ROWS), lambda i, table: (0, i, 0, 0)),
            ],
        ),
        input_output_aliases={2: 0} if carried else {},
        cost_estimate=pl.CostEstimate(
            flops=count * NPW * ROWS * BLK, bytes_accessed=count * 22 * ROWS * BLK, transcendentals=0
        ),
        name="totals",
    )(table, parts, *carried)


def mirror_kernel(table_ref, cut_ref, *refs):
    out_ref = refs[-1]
    low = lax.broadcasted_iota(jnp.int32, (HALF, 2 * ROWS), 1) < ROWS
    for at in range(NPW // 2):
        even = cut_ref[2 * at, 0].astype(jnp.float32)
        odd = cut_ref[2 * at + 1, 0].astype(jnp.float32)
        lanes = pl.ds(2 * ROWS * at, 2 * ROWS)
        out_ref[0, :HALF, lanes] = jnp.where(low, even, pltpu.roll(odd, ROWS, 1))
        out_ref[0, HALF:, lanes] = jnp.where(low, pltpu.roll(even, ROWS, 1), odd)


def mirrored(table, cut, kernel_t, start):
    count = cut.shape[1]
    carried = [] if kernel_t is None else [kernel_t]
    return pl.pallas_call(
        mirror_kernel,
        out_shape=jax.ShapeDtypeStruct((LISTED, ROWS, BLK), jnp.float32),
        grid_spec=pltpu.PrefetchScalarGridSpec(
            num_scalar_prefetch=1,
            grid=(count,),
            in_specs=[pl.BlockSpec((NPW, 1, HALF, 2 * ROWS), lambda i, table: (0, i, 0, 0))]
            + [pl.BlockSpec(memory_space=pl.ANY)] * len(carried),
            out_specs=pl.BlockSpec((1, ROWS, BLK), lambda i, table: (table[ORDER + start + i], 0, 0)),
        ),
        input_output_aliases={2: 0} if carried else {},
        cost_estimate=pl.CostEstimate(
            flops=count * ROWS * BLK, bytes_accessed=count * 6 * ROWS * BLK, transcendentals=0
        ),
        name="mirrored",
    )(table, cut, *carried)


def exchanged(value):
    return lax.all_to_all(value, "pw", split_axis=0, concat_axis=0, tiled=True)


def body(densities, coulomb, pairs, owner):
    blocks = densities.reshape(STORED, BLK, densities.shape[1])
    weight = coulomb.reshape(1, -1)
    device = lax.axis_index("trans").astype(jnp.int32).reshape(1)
    table, *sends = prepare(device, pairs.T, owner, blocks)
    arrived = [shifted(send, "trans", -step) for step, send in zip(STEPS, sends)]
    groups = [(0, LOCAL, [blocks])]
    for at in range(0, len(STEPS), 2):
        groups.append((start_of(STEPS[at]), 2 * MULT, arrived[at : at + 2]))
    kernel, kernel_t = None, None
    for start, count, rights in groups:
        parts = exchanged(products(table, blocks, weight, rights, start, count))
        kernel, cut = totals(table, parts, kernel, start)
        if start > 0:
            at = (start - LOCAL) // MULT
            cut = jnp.concatenate(
                [shifted(cut[:, :MULT], "trans", STEPS[at]), shifted(cut[:, MULT:], "trans", STEPS[at + 1])], axis=1
            )
        kernel_t = mirrored(table, exchanged(cut), kernel_t, start)
    return jnp.transpose(kernel, (1, 0, 2)), jnp.transpose(kernel_t, (1, 0, 2))


def solution(mesh):
    in_specs = (P("trans", "pw"), P("pw"), P(), P())
    out_specs = (P("pw", "trans", None), P("pw", "trans", None))
    return jax.shard_map(body, mesh=mesh, in_specs=in_specs, out_specs=out_specs, check_vma=False)
```

time: 630 us -> 512 us (0.81)
  Pallas kernels: 0 us -> 301 us
  waiting for transfers between devices: 435 us -> 151 us
  local copies, waits for them, and re-layouts: 122 us -> 7.81 us
  starting transfers between devices: 13.4 us -> 46.8 us
  other arithmetic: 21 us -> 2.62 us
  matrix products: 15.8 us -> 0 us
  between operations: 14.2 us -> 0.69 us
    pallas_call x0 -> x10, Pallas kernels: none -> 301 us  [the longest x1 241 us: prepare(): pl.pallas_call(prepare_kernel, out_shape=[jax.ShapeDtypeStruct((TABLE,),...]
    reduce_scatter x1 -> x0, waiting for transfers between devices: 266 us -> none  [body(): lax.psum_scatter(jnp.einsum('qrg,qcg->rqc', left, right, preferred_elemen...]
    ppermute x8, waiting for transfers between devices: 147 us -> 99.7 us  [shifted(): return lax.ppermute(value, axis, pairs)]
    unnamed x19 -> x12, local copies, waits for them, and re-layouts: 40.1 us -> 3.74 us
    all_to_all x1 -> x6, starting transfers between devices: 4.86 us -> 37.8 us  [exchanged(): return lax.all_to_all(value, 'pw', split_axis=0, concat_axis=0, tiled=True)]
    gather x8 -> x0, local copies, waits for them, and re-layouts: 31.8 us -> none  [the longest x1 14.9 us: body(): right = gathered[distance + SPAN, second_slot]]
    all_to_all x1 -> x6, waiting for transfers between devices: 23.1 us -> 50.8 us  [exchanged(): return lax.all_to_all(value, 'pw', split_axis=0, concat_axis=0, tiled=True)]
    transpose x1 -> x0, local copies, waits for them, and re-layouts: 22.7 us -> none  [body(): jnp.einsum('qrg,qcg->rqc', left, right, preferred_element_type=jnp.float32)]
  transfers between devices with their start and end apart: 10 -> 14, of which waited for: 5 -> 7; matrix products, arithmetic and copies ran while one was open for 9% -> 1% of each run, Pallas kernels for 0% -> 9%
where the time goes in v1:
time: 512 us; the launch traced here: 510 us
  Pallas kernels  301 us (59%)
  waiting for transfers between devices  151 us (29%)
  starting transfers between devices  46.8 us (9%)
  local copies, waits for them, and re-layouts  7.81 us (2%)
    pallas_call x1, Pallas kernels, prepare(): pl.pallas_call(prepare_kernel, out_shape=[jax.ShapeDtypeStruct((TABLE,),...  241 us
    ppermute x8, waiting for transfers between devices, shifted(): return lax.ppermute(value, axis, pairs)  99.7 us
    all_to_all x6, waiting for transfers between devices, exchanged(): return lax.all_to_all(value, 'pw', split_axis=0, concat_axis=0, tiled=True)  50.8 us
    all_to_all x6, starting transfers between devices, exchanged(): return lax.all_to_all(value, 'pw', split_axis=0, concat_axis=0, tiled=True)  37.8 us
    pallas_call x3, Pallas kernels, products(): pl.pallas_call(lambda *refs: products_kernel(count, *refs), out_shape=jax...  28.2 us
    pallas_call x3, Pallas kernels, totals(): pl.pallas_call(total_kernel, out_shape=[jax.ShapeDtypeStruct((LISTED, ROW...  17.5 us
    pallas_call x3, Pallas kernels, mirrored(): pl.pallas_call(mirror_kernel, out_shape=jax.ShapeDtypeStruct((LISTED, ROW...  14.5 us
  transfers between devices with their start and end apart: 14, of which 7 were waited for; matrix products, arithmetic and copies ran while one was open for 1% of the time, Pallas kernels for 9%

profile of v1, /device:TPU:6, one launch (start us, length us, event | category | flops | bytes accessed | tf_op | source)
XLA Modules:
  0.0 509.6 jit_solution(11842575727689334653)
XLA Ops:
  0.6 1.2 reshape.15.refs_2_
  1.9 240.9 %prepare.1 = (s32[54]{0:T(128)}, bf16[3,512,640]{2,1,0:T(8,128)(2,1)}, bf16[3,512,640]{2,1,0:T(8,128)(2,1)}, bf16[3,512,640]{2,1,0:T(8,128)(2,1)}, bf16[3,512,640]{2,1,0:T(8,128)(2,1)}) custom-call(s32[1]{0:T(128)} %bitcast.device_ref, s32[2,288]{1,0:T(2,128)} %bitcast.12, s32[128]{0:T(128)} %owner_ref.1, bf16[8,512,640]{2,1,0:T(8,128)(2,1)} %bitcast.5), custom_call_target="tpu_custom_call" | custom-call | tf_op jit(solution)/shard_map/prepare/pallas_call | solution.py:65
  242.8 9.4 %products.5 = bf16[8,6,64,512]{3,2,1,0:T(8,128)(2,1)} custom-call(s32[54]{0:T(128)} %get-tuple-element.13.refs_0_.table_ref, bf16[8,512,640]{2,1,0:T(8,128)(2,1)} %bitcast.6, f32[1,640]{1,0:T(1,128)} %reshape.15.refs_2_, bf16[8,512,640]{2,1,0:T(8,128)(2,1)} %bitcast.7), custom_call_target="tpu_custom_call" | custom-call | flops 2013265920 | bytes 11010048 | tf_op jit(solution)/shard_map/products/pallas_call | solution.py:100
  252.2 7.8 %all-to-all-start.2 = ((bf16[8,6,64,512]{3,2,1,0:T(8,128)(2,1)}), bf16[8,6,64,512]{3,2,1,0:T(8,128)(2,1)S(1)}, u32[]{:S(2)}, u32[]{:S(2)}) async-start(bf16[8,6,64,512]{3,2,1,0:T(8,128)(2,1)} %products.5), calls=%async_computation.2 | async-start | bytes 6291456 | tf_op jit(solution)/shard_map/all_to_all | solution.py:190
  260.0 0.0 collective-permute-start.2
  260.0 0.5 collective-permute-start.3
  260.5 22.0 %collective-permute-done.2.refs_3_ = bf16[3,512,640]{2,1,0:T(8,128)(2,1)} collective-permute-done((bf16[3,512,640]{2,1,0:T(8,128)(2,1)}, bf16[3,512,640]{2,1,0:T(8,128)(2,1)}, u32[]{:S(2)}, u32[]{:S(2)}) %collective-permute-start.2) | collective-permute-done | bytes 1966112 | tf_op jit(solution)/shard_map/ppermute | solution.py:25
  282.5 2.0 collective-permute-done.3.refs_4_
  284.5 9.4 %products.4 = bf16[8,6,64,512]{3,2,1,0:T(8,128)(2,1)} custom-call(s32[54]{0:T(128)} %get-tuple-element.13.refs_0_.table_ref, bf16[8,512,640]{2,1,0:T(8,128)(2,1)} %bitcast.8, f32[1,640]{1,0:T(1,128)} %reshape.15.refs_2_, bf16[3,512,640]{2,1,0:T(8,128)(2,1)} %collective-permute-done.2.refs_3_, bf16[3,512,640]{2,1,0:T(8,128)(2,1)} %collective-permute-done.3.refs_4_), custom_call_target="tpu_custom_call" | custom-call | flops 2013265920 | bytes 11010048 | tf_op jit(solution)/shard_map/products/pallas_call | solution.py:100
  293.9 24.6 %all-to-all-done.2.refs_0_ = bf16[8,6,64,512]{3,2,1,0:T(8,128)(2,1)S(1)} async-done(((bf16[8,6,64,512]{3,2,1,0:T(8,128)(2,1)}), bf16[8,6,64,512]{3,2,1,0:T(8,128)(2,1)S(1)}, u32[]{:S(2)}, u32[]{:S(2)}) %all-to-all-start.2) | async-done | bytes 3145760 | tf_op jit(solution)/shard_map/all_to_all | solution.py:190
  318.5 0.0 copy-start
  318.5 1.7 copy-done
  320.2 5.9 %all-to-all-start.1 = ((bf16[8,6,64,512]{3,2,1,0:T(8,128)(2,1)}), bf16[8,6,64,512]{3,2,1,0:T(8,128)(2,1)}, u32[]{:S(2)}, u32[]{:S(2)}) async-start(bf16[8,6,64,512]{3,2,1,0:T(8,128)(2,1)} %products.4), calls=%async_computation.1 | async-start | bytes 6291456 | tf_op jit(solution)/shard_map/all_to_all | solution.py:190
  326.1 0.0 collective-permute-start
  326.1 4.6 collective-permute-start.1
  330.7 68.0 %collective-permute-done.refs_3_ = bf16[3,512,640]{2,1,0:T(8,128)(2,1)S(1)} collective-permute-done((bf16[3,512,640]{2,1,0:T(8,128)(2,1)}, bf16[3,512,640]{2,1,0:T(8,128)(2,1)S(1)}, u32[]{:S(2)}, u32[]{:S(2)}) %collective-permute-start) | collective-permute-done | bytes 1966112 | tf_op jit(solution)/shard_map/ppermute | solution.py:25
  398.7 0.0 copy-start.2
  398.7 0.0 collective-permute-done.1.refs_4_
  398.7 1.3 copy-done.2
  400.0 9.4 %products.3 = bf16[8,6,64,512]{3,2,1,0:T(8,128)(2,1)} custom-call(s32[54]{0:T(128)} %get-tuple-element.13.refs_0_.table_ref, bf16[8,512,640]{2,1,0:T(8,128)(2,1)} %bitcast.9, f32[1,640]{1,0:T(1,128)} %reshape.15.refs_2_, bf16[3,512,640]{2,1,0:T(8,128)(2,1)} %copy-done.2, bf16[3,512,640]{2,1,0:T(8,128)(2,1)} %collective-permute-done.1.refs_4_), custom_call_target="tpu_custom_call" | custom-call | flops 2013265920 | bytes 11010048 | tf_op jit(solution)/shard_map/products/pallas_call | solution.py:100
  409.4 0.0 all-to-all-done.1.refs_0_
  409.4 5.4 %all-to-all-start = ((bf16[8,6,64,512]{3,2,1,0:T(8,128)(2,1)}), bf16[8,6,64,512]{3,2,1,0:T(8,128)(2,1)S(1)}, u32[]{:S(2)}, u32[]{:S(2)}) async-start(bf16[8,6,64,512]{3,2,1,0:T(8,128)(2,1)} %products.3), calls=%async_computation | async-start | bytes 6291456 | tf_op jit(solution)/shard_map/all_to_all | solution.py:190
  414.8 5.8 %totals.3 = (f32[18,64,512]{2,1,0:T(8,128)}, bf16[8,6,32,128]{3,2,1,0:T(8,128)(2,1)}) custom-call(s32[54]{0:T(128)} %get-tuple-element.13.refs_0_.table_ref, bf16[8,6,64,512]{3,2,1,0:T(8,128)(2,1)} %copy-done), custom_call_target="tpu_custom_call" | custom-call | flops 1572864 | bytes 4325376 | tf_op jit(solution)/shard_map/totals/pallas_call | solution.py:133
  420.6 5.8 %totals.4 = (f32[18,64,512]{2,1,0:T(8,128)}, bf16[8,6,32,128]{3,2,1,0:T(8,128)(2,1)}) custom-call(s32[54]{0:T(128)} %get-tuple-element.13.refs_0_.table_ref, bf16[8,6,64,512]{3,2,1,0:T(8,128)(2,1)} %all-to-all-done.1.refs_0_, f32[18,64,512]{2,1,0:T(8,128)} %get-tuple-element.18.refs_1_), custom_call_target="tpu_custom_call", output_to_operand_aliasing={{0}: (2, {})} | custom-call | flops 1572864 | bytes 4325376 | tf_op jit(solution)/shard_map/totals/pallas_call | solution.py:133
  426.5 26.2 %all-to-all-done.refs_0_ = bf16[8,6,64,512]{3,2,1,0:T(8,128)(2,1)S(1)} async-done(((bf16[8,6,64,512]{3,2,1,0:T(8,128)(2,1)}), bf16[8,6,64,512]{3,2,1,0:T(8,128)(2,1)S(1)}, u32[]{:S(2)}, u32[]{:S(2)}) %all-to-all-start) | async-done | bytes 3145760 | tf_op jit(solution)/shard_map/all_to_all | solution.py:190
  452.6 0.0 copy-start.1
  452.6 4.6 all-to-all-start.5
  457.2 1.8 fusion
  459.0 0.0 collective-permute-start.6
  459.0 1.7 collective-permute-start.7
  460.8 0.0 copy-done.1
  460.8 5.8 %totals.5 = (f32[18,64,512]{2,1,0:T(8,128)}, bf16[8,6,32,128]{3,2,1,0:T(8,128)(2,1)}) custom-call(s32[54]{0:T(128)} %get-tuple-element.13.refs_0_.table_ref, bf16[8,6,64,512]{3,2,1,0:T(8,128)(2,1)} %copy-done.1, f32[18,64,512]{2,1,0:T(8,128)} %get-tuple-element.19.refs_1_), custom_call_target="tpu_custom_call", output_to_operand_aliasing={{0}: (2, {})} | custom-call | flops 1572864 | bytes 4325376 | tf_op jit(solution)/shard_map/totals/pallas_call | solution.py:133
  466.6 0.0 collective-permute-done.6
  466.6 0.0 collective-permute-done.7
  466.6 1.8 pad_maximum_fusion.1
  468.4 0.0 all-to-all-done.5.cut_ref
  468.4 0.0 copy-start.3
  468.4 7.2 %all-to-all-start.4 = ((bf16[8,6,32,128]{3,2,1,0:T(8,128)(2,1)}), bf16[8,6,32,128]{3,2,1,0:T(8,128)(2,1)S(1)}, u32[]{:S(2)}, u32[]{:S(2)}) async-start(bf16[8,6,32,128]{3,2,1,0:T(8,128)(2,1)} %pad_maximum_fusion.1), calls=%async_computation.4 | async-start | bytes 786432 | tf_op jit(solution)/shard_map/all_to_all | solution.py:190
  475.7 1.0 fusion.1
  476.7 1.2 collective-permute-start.4
  477.9 0.9 collective-permute-start.5
  478.8 4.1 collective-permute-done.4
  482.9 3.6 collective-permute-done.5
  486.6 0.8 pad_maximum_fusion
  487.3 0.0 all-to-all-done.4.cut_ref
  487.4 0.0 copy-start.4
  487.4 6.9 %all-to-all-start.3 = ((bf16[8,6,32,128]{3,2,1,0:T(8,128)(2,1)}), bf16[8,6,32,128]{3,2,1,0:T(8,128)(2,1)S(1)}, u32[]{:S(2)}, u32[]{:S(2)}) async-start(bf16[8,6,32,128]{3,2,1,0:T(8,128)(2,1)} %pad_maximum_fusion), calls=%async_computation.3 | async-start | bytes 786432 | tf_op jit(solution)/shard_map/all_to_all | solution.py:190
  494.3 0.0 copy-done.3
  494.3 4.8 mirrored.3.refs_0_
  499.1 0.0 copy-done.4
  499.1 4.8 mirrored.4.refs_0_
  504.0 0.0 all-to-all-done.3.cut_ref
  504.0 0.0 copy-start.5
  504.0 0.8 copy-done.5
  504.7 4.8 mirrored.5
Async XLA Ops:
  252.2 66.3 %all-to-all-start.2 = ((bf16[8,6,64,512]{3,2,1,0:T(8,128)(2,1)}), bf16[8,6,64,512]{3,2,1,0:T(8,128)(2,1)S(1)}, u32[]{:S(2)}, u32[]{:S(2)}) async-start(bf16[8,6,64,512]{3,2,1,0:T(8,128)(2,1)} %products.5), calls=%async_computation.2 | async-start | bytes 6291456 | tf_op jit(solution)/shard_map/all_to_all | solution.py:190
  260.0 22.5 %collective-permute-start.2 = (bf16[3,512,640]{2,1,0:T(8,128)(2,1)}, bf16[3,512,640]{2,1,0:T(8,128)(2,1)}, u32[]{:S(2)}, u32[]{:S(2)}) collective-permute-start(bf16[3,512,640]{2,1,0:T(8,128)(2,1)} %get-tuple-element.16), channel_id=1, source_target_pairs={{0,120},{8,0},{16,8},{24,16},{32,24},{40,32},{48,40},{56,48},{64,5... | collective-permute-start | bytes 5898248 | tf_op jit(solution)/shard_map/ppermute | solution.py:25
  260.0 24.4 %collective-permute-start.3 = (bf16[3,512,640]{2,1,0:T(8,128)(2,1)}, bf16[3,512,640]{2,1,0:T(8,128)(2,1)}, u32[]{:S(2)}, u32[]{:S(2)}) collective-permute-start(bf16[3,512,640]{2,1,0:T(8,128)(2,1)} %get-tuple-element.17), channel_id=1, source_target_pairs={{0,8},{8,16},{16,24},{24,32},{32,40},{40,48},{48,56},{56,64},{64,7... | collective-permute-start | bytes 5898248 | tf_op jit(solution)/shard_map/ppermute | solution.py:25
  318.5 1.7 copy-start
  320.2 89.1 %all-to-all-start.1 = ((bf16[8,6,64,512]{3,2,1,0:T(8,128)(2,1)}), bf16[8,6,64,512]{3,2,1,0:T(8,128)(2,1)}, u32[]{:S(2)}, u32[]{:S(2)}) async-start(bf16[8,6,64,512]{3,2,1,0:T(8,128)(2,1)} %products.4), calls=%async_computation.1 | async-start | bytes 6291456 | tf_op jit(solution)/shard_map/all_to_all | solution.py:190
  326.1 72.6 %collective-permute-start = (bf16[3,512,640]{2,1,0:T(8,128)(2,1)}, bf16[3,512,640]{2,1,0:T(8,128)(2,1)S(1)}, u32[]{:S(2)}, u32[]{:S(2)}) collective-permute-start(bf16[3,512,640]{2,1,0:T(8,128)(2,1)} %get-tuple-element.14), channel_id=1, source_target_pairs={{0,112},{8,120},{16,0},{24,8},{32,16},{40,24},{48,32},{56,40},{64,... | collective-permute-start | bytes 5898248 | tf_op jit(solution)/shard_map/ppermute | solution.py:25
  326.1 72.6 %collective-permute-start.1 = (bf16[3,512,640]{2,1,0:T(8,128)(2,1)}, bf16[3,512,640]{2,1,0:T(8,128)(2,1)}, u32[]{:S(2)}, u32[]{:S(2)}) collective-permute-start(bf16[3,512,640]{2,1,0:T(8,128)(2,1)} %get-tuple-element.15), channel_id=1, source_target_pairs={{0,16},{8,24},{16,32},{24,40},{32,48},{40,56},{48,64},{56,72},{64,... | collective-permute-start | bytes 5898248 | tf_op jit(solution)/shard_map/ppermute | solution.py:25
  398.7 1.3 copy-start.2
  409.4 43.3 %all-to-all-start = ((bf16[8,6,64,512]{3,2,1,0:T(8,128)(2,1)}), bf16[8,6,64,512]{3,2,1,0:T(8,128)(2,1)S(1)}, u32[]{:S(2)}, u32[]{:S(2)}) async-start(bf16[8,6,64,512]{3,2,1,0:T(8,128)(2,1)} %products.3), calls=%async_computation | async-start | bytes 6291456 | tf_op jit(solution)/shard_map/all_to_all | solution.py:190
  452.6 8.2 %copy-start.1 = (bf16[8,6,64,512]{3,2,1,0:T(8,128)(2,1)}, bf16[8,6,64,512]{3,2,1,0:T(8,128)(2,1)S(1)}, u32[]{:S(2)}) copy-start(bf16[8,6,64,512]{3,2,1,0:T(8,128)(2,1)S(1)} %all-to-all-done.refs_0_) | copy-start | bytes 9437188
  452.6 15.8 %all-to-all-start.5 = ((bf16[8,6,32,128]{3,2,1,0:T(8,128)(2,1)}), bf16[8,6,32,128]{3,2,1,0:T(8,128)(2,1)S(1)}, u32[]{:S(2)}, u32[]{:S(2)}) async-start(bf16[8,6,32,128]{3,2,1,0:T(8,128)(2,1)} %get-tuple-element.23), calls=%async_computation.5 | async-start | bytes 786432 | tf_op jit(solution)/shard_map/all_to_all | solution.py:190
  459.0 7.6 %collective-permute-start.6 = (bf16[8,3,32,128]{3,2,1,0:T(8,128)(2,1)}, bf16[8,3,32,128]{3,2,1,0:T(8,128)(2,1)}, u32[]{:S(2)}, u32[]{:S(2)}) collective-permute-start(bf16[8,3,32,128]{3,2,1,0:T(8,128)(2,1)} %get-tuple-element.24), channel_id=1, source_target_pairs={{0,8},{8,16},{16,24},{24,32},{32,40},{40,48},{48,56},{56,64},{64,7... | collective-permute-start | bytes 589832 | tf_op jit(solution)/shard_map/ppermute | solution.py:25
  459.0 7.6 %collective-permute-start.7 = (bf16[8,3,32,128]{3,2,1,0:T(8,128)(2,1)}, bf16[8,3,32,128]{3,2,1,0:T(8,128)(2,1)}, u32[]{:S(2)}, u32[]{:S(2)}) collective-permute-start(bf16[8,3,32,128]{3,2,1,0:T(8,128)(2,1)} %get-tuple-element.25), channel_id=1, source_target_pairs={{0,120},{8,0},{16,8},{24,16},{32,24},{40,32},{48,40},{56,48},{64,5... | collective-permute-start | bytes 589832 | tf_op jit(solution)/shard_map/ppermute | solution.py:25
  468.4 25.8 %copy-start.3 = (bf16[8,6,32,128]{3,2,1,0:T(8,128)(2,1)}, bf16[8,6,32,128]{3,2,1,0:T(8,128)(2,1)S(1)}, u32[]{:S(2)}) copy-start(bf16[8,6,32,128]{3,2,1,0:T(8,128)(2,1)S(1)} %all-to-all-done.5.cut_ref) | copy-start | bytes 1179652
  468.4 18.9 %all-to-all-start.4 = ((bf16[8,6,32,128]{3,2,1,0:T(8,128)(2,1)}), bf16[8,6,32,128]{3,2,1,0:T(8,128)(2,1)S(1)}, u32[]{:S(2)}, u32[]{:S(2)}) async-start(bf16[8,6,32,128]{3,2,1,0:T(8,128)(2,1)} %pad_maximum_fusion.1), calls=%async_computation.4 | async-start | bytes 786432 | tf_op jit(solution)/shard_map/all_to_all | solution.py:190
  476.7 6.2 %collective-permute-start.4 = (bf16[8,3,32,128]{3,2,1,0:T(8,128)(2,1)S(1)}, bf16[8,3,32,128]{3,2,1,0:T(8,128)(2,1)S(1)}, u32[]{:S(2)}, u32[]{:S(2)}) collective-permute-start(bf16[8,3,32,128]{3,2,1,0:T(8,128)(2,1)S(1)} %get-tuple-element.26), channel_id=1, source_target_pairs={{0,16},{8,24},{16,32},{24,40},{32,48},{40,56},{48,64},{56,72},{64,... | collective-permute-start | bytes 589832 | tf_op jit(solution)/shard_map/ppermute | solution.py:25
  477.9 8.7 %collective-permute-start.5 = (bf16[8,3,32,128]{3,2,1,0:T(8,128)(2,1)S(1)}, bf16[8,3,32,128]{3,2,1,0:T(8,128)(2,1)S(1)}, u32[]{:S(2)}, u32[]{:S(2)}) collective-permute-start(bf16[8,3,32,128]{3,2,1,0:T(8,128)(2,1)S(1)} %get-tuple-element.27), channel_id=1, source_target_pairs={{0,112},{8,120},{16,0},{24,8},{32,16},{40,24},{48,32},{56,40},{64,... | collective-permute-start | bytes 589832 | tf_op jit(solution)/shard_map/ppermute | solution.py:25
  487.4 11.8 %copy-start.4 = (bf16[8,6,32,128]{3,2,1,0:T(8,128)(2,1)}, bf16[8,6,32,128]{3,2,1,0:T(8,128)(2,1)S(1)}, u32[]{:S(2)}) copy-start(bf16[8,6,32,128]{3,2,1,0:T(8,128)(2,1)S(1)} %all-to-all-done.4.cut_ref) | copy-start | bytes 1179652
  487.4 16.6 %all-to-all-start.3 = ((bf16[8,6,32,128]{3,2,1,0:T(8,128)(2,1)}), bf16[8,6,32,128]{3,2,1,0:T(8,128)(2,1)S(1)}, u32[]{:S(2)}, u32[]{:S(2)}) async-start(bf16[8,6,32,128]{3,2,1,0:T(8,128)(2,1)} %pad_maximum_fusion), calls=%async_computation.3 | async-start | bytes 786432 | tf_op jit(solution)/shard_map/all_to_all | solution.py:190
  504.0 0.8 copy-start.5

commit v2 on v1

v2 whole, which is shorter than its diff:
```python
import jax
import jax.numpy as jnp
from jax import lax
from jax.experimental import pallas as pl
from jax.experimental.pallas import tpu as pltpu
from jax.sharding import PartitionSpec as P

BLK = 512
SPAN = 2
MULT = 3
STORED = 8
LISTED = 18
LOCAL = 6
NTRANS = 16
NPW = 8
NY = 4
NZ = 2
ROWS = BLK // NPW
HALF = ROWS // 2
STEPS = (1, -1, 2, -2)
ORDER, FIRST, SECOND, YAT, ZAT, TABLE = 0, LISTED, 2 * LISTED, 3 * LISTED, 3 * LISTED + 1, 3 * LISTED + 2
VMEM_BYTES = 24 * 2**20


def shifted(value, steps):
    pairs = [(source, (source + steps) % NTRANS) for source in range(NTRANS)]
    return lax.ppermute(value, "trans", pairs)


def along_y(value, steps):
    pairs = [(z * NY + y, z * NY + (y + steps) % NY) for z in range(NZ) for y in range(NY)]
    return lax.ppermute(value, "pw", pairs)


def across_z(value):
    return lax.ppermute(value, "pw", [(source, (source + NY) % NPW) for source in range(NPW)])


def exchanged(value):
    return lax.all_to_all(value, "pw", split_axis=0, concat_axis=0, tiled=True)


def start_of(step):
    return 0 if step == 0 else LOCAL + MULT * STEPS.index(step)


def params():
    return pltpu.CompilerParams(vmem_limit_bytes=VMEM_BYTES)


def select(steps, device, table_ref, pairs_ref, owner_ref, blocks_ref, sends, held, in_sems, out_sems):
    loads, stores = [], []
    for at, step in enumerate(steps):
        target = (device - step + NTRANS) & (NTRANS - 1)
        for j in range(MULT):
            n = at * MULT + j
            q = table_ref[ORDER + start_of(step) + j]
            slot = owner_ref[pairs_ref[1, target * LISTED + q]] & (STORED - 1)
            loads.append(pltpu.make_async_copy(blocks_ref.at[slot], held.at[n], in_sems.at[n]))
            stores.append(pltpu.make_async_copy(held.at[n], sends[at].at[j], out_sems.at[n]))
            loads[-1].start()
    for load, store in zip(loads, stores):
        load.wait()
        store.start()
    for store in stores:
        store.wait()


def prepare_kernel(steps, place_ref, pairs_ref, owner_ref, blocks_ref, table_ref, *rest):
    sends, scratch = rest[: len(steps)], rest[len(steps) :]
    device = place_ref[0]
    table_ref[YAT] = place_ref[1] & (NY - 1)
    table_ref[ZAT] = place_ref[1] >> 2
    filled = {step: start_of(step) for step in (0, *STEPS)}
    for q in range(LISTED):
        pair = device * LISTED + q
        first = owner_ref[pairs_ref[0, pair]]
        second = owner_ref[pairs_ref[1, pair]]
        distance = (((second >> 3) - device + SPAN + NTRANS) & (NTRANS - 1)) - SPAN
        place = jnp.int32(0)
        for step in filled:
            here = distance == step
            place = jnp.where(here, filled[step], place)
            filled[step] = jnp.where(here, filled[step] + 1, filled[step])
        table_ref[ORDER + place] = jnp.int32(q)
        table_ref[FIRST + place] = first & (STORED - 1)
        table_ref[SECOND + place] = second & (STORED - 1)
    select(steps, device, table_ref, pairs_ref, owner_ref, blocks_ref, sends, *scratch)


def select_kernel(steps, table_ref, place_ref, pairs_ref, owner_ref, blocks_ref, *rest):
    sends, scratch = rest[: len(steps)], rest[len(steps) :]
    select(steps, place_ref[0], table_ref, pairs_ref, owner_ref, blocks_ref, sends, *scratch)


def prepare(steps, table, place, pairs, owner, blocks):
    width = blocks.shape[2]
    count = MULT * len(steps)
    smem = pl.BlockSpec(memory_space=pltpu.SMEM)
    anywhere = pl.BlockSpec(memory_space=pl.ANY)
    sends = [jax.ShapeDtypeStruct((MULT, BLK, width), jnp.bfloat16)] * len(steps)
    scratch = [
        pltpu.VMEM((count, BLK, width), jnp.bfloat16),
        pltpu.SemaphoreType.DMA((count,)),
        pltpu.SemaphoreType.DMA((count,)),
    ]
    if table is None:
        return pl.pallas_call(
            lambda *refs: prepare_kernel(steps, *refs),
            out_shape=[jax.ShapeDtypeStruct((TABLE,), jnp.int32)] + sends,
            in_specs=[smem, smem, smem, anywhere],
            out_specs=[smem] + [anywhere] * len(steps),
            scratch_shapes=scratch,
            compiler_params=params(),
            name="prepare",
        )(place, pairs, owner, blocks)
    return pl.pallas_call(
        lambda *refs: select_kernel(steps, *refs),
        out_shape=sends,
        in_specs=[smem, smem, smem, smem, anywhere],
        out_specs=[anywhere] * len(steps),
        scratch_shapes=scratch,
        compiler_params=params(),
        name="select",
    )(table, place, pairs, owner, blocks)


def products_kernel(count, table_ref, left_ref, coulomb_ref, *refs):
    rights, (own_ref, *send_refs), weighted_ref = refs[:-5], refs[-5:-1], refs[-1]
    each = count // len(rights)
    y = table_ref[YAT]
    for dy in range(NY):
        for z in range(NZ):
            at = (dy * NZ + z) * ROWS
            source = z * (NY * ROWS) + ((y + dy) & (NY - 1)) * ROWS
            rows = left_ref[0, pl.ds(pl.multiple_of(source, ROWS), ROWS), :]
            weighted_ref[at : at + ROWS, :] = (rows.astype(jnp.float32) * coulomb_ref[...]).astype(jnp.bfloat16)
    for at, right_ref in enumerate(rights):

        @pl.when(pl.program_id(0) // each == at)
        def _():
            part = lax.dot_general(
                weighted_ref[...], right_ref[0], (((1,), (1,)), ((), ())), preferred_element_type=jnp.float32
            ).reshape(NY, NZ, 1, ROWS, BLK)
            own_ref[...] = part[0]
            for dy, send_ref in zip(range(1, NY), send_refs):
                send_ref[...] = part[dy].astype(jnp.bfloat16)


def products(table, blocks, coulomb, rights, start, count):
    width = blocks.shape[2]
    each = count // len(rights)
    if rights[0].shape[0] == STORED:
        right_specs = [pl.BlockSpec((1, BLK, width), lambda i, table: (table[SECOND + start + i], 0, 0))]
    else:
        right_specs = [
            pl.BlockSpec((1, BLK, width), lambda i, table, at=at: (jnp.clip(i - at * each, 0, each - 1), 0, 0))
            for at in range(len(rights))
        ]
    return pl.pallas_call(
        lambda *refs: products_kernel(count, *refs),
        out_shape=[
            jax.ShapeDtypeStruct((NZ, count, ROWS, BLK), jnp.bfloat16 if dy else jnp.float32) for dy in range(NY)
        ],
        grid_spec=pltpu.PrefetchScalarGridSpec(
            num_scalar_prefetch=1,
            grid=(count,),
            in_specs=[
                pl.BlockSpec((1, BLK, width), lambda i, table: (table[FIRST + start + i], 0, 0)),
                pl.BlockSpec((1, width), lambda i, table: (0, 0)),
                *right_specs,
            ],
            out_specs=[pl.BlockSpec((NZ, 1, ROWS, BLK), lambda i, table: (0, i, 0, 0))] * NY,
            scratch_shapes=[pltpu.VMEM((BLK, width), jnp.bfloat16)],
        ),
        compiler_params=params(),
        name="products",
    )(table, blocks, coulomb, *rights)


def plane_kernel(table_ref, own_ref, up_ref, two_ref, down_ref, keep_ref, give_ref):
    z = table_ref[ZAT]

    def total(at):
        return (
            own_ref[at] + up_ref[at].astype(jnp.float32) + two_ref[at].astype(jnp.float32) + down_ref[at].astype(jnp.float32)
        )

    keep_ref[...] = total(z)
    give_ref[...] = total(1 - z).astype(jnp.bfloat16)


def plane_sums(table, parts, per):
    count = parts[0].shape[1]
    return pl.pallas_call(
        plane_kernel,
        out_shape=[
            jax.ShapeDtypeStruct((count, ROWS, BLK), jnp.float32),
            jax.ShapeDtypeStruct((count, ROWS, BLK), jnp.bfloat16),
        ],
        grid_spec=pltpu.PrefetchScalarGridSpec(
            num_scalar_prefetch=1,
            grid=(count // per,),
            in_specs=[pl.BlockSpec((NZ, per, ROWS, BLK), lambda i, table: (0, i, 0, 0))] * NY,
            out_specs=[pl.BlockSpec((per, ROWS, BLK), lambda i, table: (i, 0, 0))] * 2,
        ),
        compiler_params=params(),
        name="plane_sums",
    )(table, *parts)


def total_kernel(table_ref, keep_ref, got_ref, *refs):
    kernel_ref, cut_refs = refs[-3], refs[-2:]
    total = keep_ref[0] + got_ref[0].astype(jnp.float32)
    kernel_ref[0] = total
    both = jnp.concatenate([total, pltpu.roll(total, BLK - HALF, 1)], axis=0)
    columns = jnp.transpose(both, (1, 0))
    for at, cut_ref in enumerate(cut_refs):

        @pl.when(pl.program_id(0) // MULT == at)
        def _():
            for target in range(NPW):
                cut_ref[target, 0] = columns[target * ROWS : target * ROWS + HALF].astype(cut_ref.dtype)


def totals(table, keep, got, kernel, start):
    count = keep.shape[0]
    carried = [] if kernel is None else [kernel]
    return pl.pallas_call(
        total_kernel,
        out_shape=[jax.ShapeDtypeStruct((LISTED, ROWS, BLK), jnp.float32)]
        + [jax.ShapeDtypeStruct((NPW, MULT, HALF, 2 * ROWS), jnp.bfloat16)] * 2,
        grid_spec=pltpu.PrefetchScalarGridSpec(
            num_scalar_prefetch=1,
            grid=(count,),
            in_specs=[pl.BlockSpec((1, ROWS, BLK), lambda i, table: (i, 0, 0))] * 2
            + [pl.BlockSpec(memory_space=pl.ANY)] * len(carried),
            out_specs=[pl.BlockSpec((1, ROWS, BLK), lambda i, table: (table[ORDER + start + i], 0, 0))]
            + [
                pl.BlockSpec(
                    (NPW, 1, HALF, 2 * ROWS), lambda i, table, at=at: (0, jnp.clip(i - at * MULT, 0, MULT - 1), 0, 0)
                )
                for at in range(2)
            ],
        ),
        input_output_aliases={3: 0} if carried else {},
        compiler_params=params(),
        name="totals",
    )(table, keep, got, *carried)


def mirror_kernel(table_ref, cut_ref, *refs):
    out_ref = refs[-1]
    low = lax.broadcasted_iota(jnp.int32, (HALF, 2 * ROWS), 1) < ROWS
    for at in range(NPW // 2):
        even = cut_ref[2 * at, 0].astype(jnp.float32)
        odd = cut_ref[2 * at + 1, 0].astype(jnp.float32)
        lanes = pl.ds(2 * ROWS * at, 2 * ROWS)
        out_ref[0, :HALF, lanes] = jnp.where(low, even, pltpu.roll(odd, ROWS, 1))
        out_ref[0, HALF:, lanes] = jnp.where(low, pltpu.roll(even, ROWS, 1), odd)


def mirrored(table, cut, kernel_t, start):
    count = cut.shape[1]
    carried = [] if kernel_t is None else [kernel_t]
    return pl.pallas_call(
        mirror_kernel,
        out_shape=jax.ShapeDtypeStruct((LISTED, ROWS, BLK), jnp.float32),
        grid_spec=pltpu.PrefetchScalarGridSpec(
            num_scalar_prefetch=1,
            grid=(count,),
            in_specs=[pl.BlockSpec((NPW, 1, HALF, 2 * ROWS), lambda i, table: (0, i, 0, 0))]
            + [pl.BlockSpec(memory_space=pl.ANY)] * len(carried),
            out_specs=pl.BlockSpec((1, ROWS, BLK), lambda i, table: (table[ORDER + start + i], 0, 0)),
        ),
        input_output_aliases={2: 0} if carried else {},
        compiler_params=params(),
        name="mirrored",
    )(table, cut, *carried)


def body(densities, coulomb, pairs, owner):
    blocks = densities.reshape(STORED, BLK, densities.shape[1])
    weight = coulomb.reshape(1, -1)
    place = jnp.stack([lax.axis_index("trans"), lax.axis_index("pw")]).astype(jnp.int32)
    table, *near = prepare(STEPS[:2], None, place, pairs.T, owner, blocks)
    far = prepare(STEPS[2:], table, place, pairs.T, owner, blocks)
    near = [shifted(send, -step) for step, send in zip(STEPS[:2], near)]
    *far, near[0], near[1] = lax.optimization_barrier((*far, *near))
    far = [shifted(send, -step) for step, send in zip(STEPS[2:], far)]
    groups = [(0, LOCAL, [blocks]), (start_of(STEPS[0]), 2 * MULT, near), (start_of(STEPS[2]), 2 * MULT, far)]
    kernel, kernel_t = None, None
    for start, count, rights in groups:
        own, up, two, down = products(table, blocks, weight, rights, start, count)
        parts = (own, along_y(up, 1), along_y(two, 2), along_y(down, 3))
        keep, give = plane_sums(table, parts, MULT)
        kernel, *cuts = totals(table, keep, across_z(give), kernel, start)
        if start > 0:
            at = (start - LOCAL) // MULT
            cuts = [shifted(cut, step) for cut, step in zip(cuts, STEPS[at : at + 2])]
        kernel_t = mirrored(table, exchanged(jnp.concatenate(cuts, axis=1)), kernel_t, start)
    return jnp.transpose(kernel, (1, 0, 2)), jnp.transpose(kernel_t, (1, 0, 2))


def solution(mesh):
    in_specs = (P("trans", "pw"), P("pw"), P(), P())
    out_specs = (P("pw", "trans", None), P("pw", "trans", None))
    return jax.shard_map(body, mesh=mesh, in_specs=in_specs, out_specs=out_specs, check_vma=False)
```

time: 512 us -> 214 us (0.42)
  Pallas kernels: 301 us -> 45.4 us
  waiting for transfers between devices: 151 us -> 108 us
  starting transfers between devices: 46.8 us -> 52.6 us
    pallas_call x4 -> x8, Pallas kernels: 269 us -> 26.8 us  [the longest x3 15.8 us: products(): pl.pallas_call(lambda *refs: products_kernel(count, *refs), out_shape=[ja...]
    all_to_all x6 -> x3, waiting for transfers between devices: 50.8 us -> 4.57 us  [exchanged(): return lax.all_to_all(value, 'pw', split_axis=0, concat_axis=0, tiled=True)]
    ppermute x8 -> x20, starting transfers between devices: 8.96 us -> 35.1 us  [the longest x9 14 us: along_y(): return lax.ppermute(value, 'pw', pairs)]
    all_to_all x6 -> x3, starting transfers between devices: 37.8 us -> 17.5 us  [exchanged(): return lax.all_to_all(value, 'pw', split_axis=0, concat_axis=0, tiled=True)]
    pallas_call x3, Pallas kernels: 17.5 us -> 9.83 us  [totals(): pl.pallas_call(total_kernel, out_shape=[jax.ShapeDtypeStruct((LISTED, ROW...]
    pallas_call x3, Pallas kernels: 14.5 us -> 8.77 us  [mirrored(): pl.pallas_call(mirror_kernel, out_shape=jax.ShapeDtypeStruct((LISTED, ROW...]
    ppermute x8 -> x20, waiting for transfers between devices: 99.7 us -> 104 us  [the longest x9 50.7 us: along_y(): return lax.ppermute(value, 'pw', pairs)]
  transfers between devices with their start and end apart: 14 -> 23, of which waited for: 7 -> 14; matrix products, arithmetic and copies ran while one was open for 1% -> 1% of each run, Pallas kernels for 9% -> 18%
where the time goes in v2:
time: 214 us; the launch traced here: 213 us
  waiting for transfers between devices  108 us (50%)
  starting transfers between devices  52.6 us (25%)
  Pallas kernels  45.4 us (21%)
  local copies, waits for them, and re-layouts  3.83 us (2%)
  other arithmetic  2.42 us (1%)
    ppermute x9, waiting for transfers between devices, along_y(): return lax.ppermute(value, 'pw', pairs)  50.7 us
    ppermute x8, waiting for transfers between devices, shifted(): return lax.ppermute(value, 'trans', pairs)  47.6 us
    all_to_all x3, starting transfers between devices, exchanged(): return lax.all_to_all(value, 'pw', split_axis=0, concat_axis=0, tiled=True)  17.5 us
    pallas_call x3, Pallas kernels, products(): pl.pallas_call(lambda *refs: products_kernel(count, *refs), out_shape=[ja...  15.8 us
    ppermute x9, starting transfers between devices, along_y(): return lax.ppermute(value, 'pw', pairs)  14 us
    ppermute x3, starting transfers between devices, across_z(): lax.ppermute(value, 'pw', [(source, (source + NY) % NPW) for source in ra...  11.4 us
    pallas_call x3, Pallas kernels, totals(): pl.pallas_call(total_kernel, out_shape=[jax.ShapeDtypeStruct((LISTED, ROW...  9.83 us
    ppermute x8, starting transfers between devices, shifted(): return lax.ppermute(value, 'trans', pairs)  9.77 us
  transfers between devices with their start and end apart: 23, of which 14 were waited for; matrix products, arithmetic and copies ran while one was open for 1% of the time, Pallas kernels for 18%

profile of v2, /device:TPU:6, one launch (start us, length us, event | category | flops | bytes accessed | tf_op | source)
XLA Modules:
  0.0 213.2 jit_solution(6961894455150561116)
XLA Ops:
  0.6 0.1 pad_add_fusion.refs_0_.refs_1_
  0.7 2.5 %copy-done = bf16[4096,640]{1,0:T(8,128)(2,1)S(1)} copy-done((bf16[4096,640]{1,0:T(8,128)(2,1)S(1)}, bf16[4096,640]{1,0:T(8,128)(2,1)}, u32[]{:S(2)}) %copy-start) | copy-done | bytes 5242904
  3.2 0.7 copy-done.2
  3.9 0.7 copy-done.3
  4.5 4.2 %prepare.1 = (s32[56]{0:T(128)S(1)}, bf16[3,512,640]{2,1,0:T(8,128)(2,1)S(1)}, bf16[3,512,640]{2,1,0:T(8,128)(2,1)S(1)}) custom-call(s32[2]{0:T(128)S(1)} %pad_add_fusion.refs_0_.refs_1_, s32[2,288]{1,0:T(2,128)S(1)} %bitcast.12, s32[128]{0:T(128)S(1)} %copy-done.3, bf16[8,512,640]{2,1,0:T(8,128)(2,1)S(1)} %bitcast.6), custom_call_target="tpu_custom_call" | custom-call | tf_op jit(solution)/shard_map/prepare/pallas_call | solution.py:108
  8.7 0.3 collective-permute-start
  9.1 0.2 collective-permute-start.1
  9.3 3.3 %select.1 = (bf16[3,512,640]{2,1,0:T(8,128)(2,1)S(1)}, bf16[3,512,640]{2,1,0:T(8,128)(2,1)S(1)}) custom-call(s32[56]{0:T(128)S(1)} %get-tuple-element.38.refs_0_.table_ref, s32[2]{0:T(128)S(1)} %pad_add_fusion.refs_0_.refs_1_, s32[2,288]{1,0:T(2,128)S(1)} %bitcast.13, s32[128]{0:T(128)S(1)} %copy-done.3, bf16[8,512,640]{2,1,0:T(8,128)(2,1)S(1)} %bitcast.7), custom_call_target="tpu_custom_call" | custom-call | tf_op jit(solution)/shard_map/select/pallas_call | solution.py:117
  12.6 18.6 %collective-permute-done.refs_3_ = bf16[3,512,640]{2,1,0:T(8,128)(2,1)S(1)} collective-permute-done((bf16[3,512,640]{2,1,0:T(8,128)(2,1)S(1)}, bf16[3,512,640]{2,1,0:T(8,128)(2,1)S(1)}, u32[]{:S(2)}, u32[]{:S(2)}) %collective-permute-start) | collective-permute-done | bytes 1966112 | tf_op jit(solution)/shard_map/ppermute | solution.py:27
  31.2 1.9 collective-permute-done.1.refs_4_
  33.1 0.6 collective-permute-start.2
  33.8 4.8 %collective-permute-start.3 = (bf16[3,512,640]{2,1,0:T(8,128)(2,1)S(1)}, bf16[3,512,640]{2,1,0:T(8,128)(2,1)S(1)}, u32[]{:S(2)}, u32[]{:S(2)}) collective-permute-start(bf16[3,512,640]{2,1,0:T(8,128)(2,1)S(1)} %get-tuple-element.44), channel_id=1, source_target_pairs={{0,16},{8,24},{16,32},{24,40},{32,48},{40,56},{48,64},{56,72},{64,... | collective-permute-start | bytes 5898248 | tf_op jit(solution)/shard_map/ppermute | solution.py:27
  38.6 5.2 %products.5 = (f32[2,6,64,512]{3,2,1,0:T(8,128)S(1)}, bf16[2,6,64,512]{3,2,1,0:T(8,128)(2,1)S(1)}, bf16[2,6,64,512]{3,2,1,0:T(8,128)(2,1)S(1)}, bf16[2,6,64,512]{3,2,1,0:T(8,128)(2,1)S(1)}) custom-call(s32[56]{0:T(128)S(1)} %get-tuple-element.38.refs_0_.table_ref, bf16[8,512,640]{2,1,0:T(8,128)(2,1)S(1)} %bitcast.8, f32[1,640]{1,0:T(1,128)S(1)} %reshape.11.refs_2_, ...), custom_call_target="tpu_custom_call" | custom-call | tf_op jit(solution)/shard_map/products/pallas_call | solution.py:160
  43.8 1.6 collective-permute-start.12
  45.4 2.9 %collective-permute-start.13 = (bf16[2,6,64,512]{3,2,1,0:T(8,128)(2,1)S(1)}, bf16[2,6,64,512]{3,2,1,0:T(8,128)(2,1)S(1)}, u32[]{:S(2)}, u32[]{:S(2)}) collective-permute-start(bf16[2,6,64,512]{3,2,1,0:T(8,128)(2,1)S(1)} %get-tuple-element.61), channel_id=1, source_target_pairs={{0,2},{1,3},{2,0},{3,1},{4,6},{5,7},{6,4},{7,5},{8,10},{9,11},{10,... | collective-permute-start | bytes 2359304 | tf_op jit(solution)/shard_map/ppermute | solution.py:32
  48.3 1.3 collective-permute-start.14
  49.7 5.3 %products.4 = (f32[2,6,64,512]{3,2,1,0:T(8,128)S(1)}, bf16[2,6,64,512]{3,2,1,0:T(8,128)(2,1)S(1)}, bf16[2,6,64,512]{3,2,1,0:T(8,128)(2,1)S(1)}, bf16[2,6,64,512]{3,2,1,0:T(8,128)(2,1)S(1)}) custom-call(s32[56]{0:T(128)S(1)} %get-tuple-element.38.refs_0_.table_ref, bf16[8,512,640]{2,1,0:T(8,128)(2,1)S(1)} %bitcast.10, f32[1,640]{1,0:T(1,128)S(1)} %reshape.11.refs_2_, ...), custom_call_target="tpu_custom_call" | custom-call | tf_op jit(solution)/shard_map/products/pallas_call | solution.py:160
  55.0 9.5 %collective-permute-done.12.up_ref = bf16[2,6,64,512]{3,2,1,0:T(8,128)(2,1)S(1)} collective-permute-done((bf16[2,6,64,512]{3,2,1,0:T(8,128)(2,1)S(1)}, bf16[2,6,64,512]{3,2,1,0:T(8,128)(2,1)S(1)}, u32[]{:S(2)}, u32[]{:S(2)}) %collective-permute-start.12) | collective-permute-done | bytes 786464 | tf_op jit(solution)/shard_map/ppermute | solution.py:32
  64.4 1.5 collective-permute-start.8
  65.9 15.8 %collective-permute-done.2.refs_3_ = bf16[3,512,640]{2,1,0:T(8,128)(2,1)S(1)} collective-permute-done((bf16[3,512,640]{2,1,0:T(8,128)(2,1)S(1)}, bf16[3,512,640]{2,1,0:T(8,128)(2,1)S(1)}, u32[]{:S(2)}, u32[]{:S(2)}) %collective-permute-start.2) | collective-permute-done | bytes 1966112 | tf_op jit(solution)/shard_map/ppermute | solution.py:27
  81.6 3.2 %collective-permute-start.9 = (bf16[2,6,64,512]{3,2,1,0:T(8,128)(2,1)S(1)}, bf16[2,6,64,512]{3,2,1,0:T(8,128)(2,1)S(1)}, u32[]{:S(2)}, u32[]{:S(2)}) collective-permute-start(bf16[2,6,64,512]{3,2,1,0:T(8,128)(2,1)S(1)} %get-tuple-element.55), channel_id=1, source_target_pairs={{0,2},{1,3},{2,0},{3,1},{4,6},{5,7},{6,4},{7,5},{8,10},{9,11},{10,... | collective-permute-start | bytes 2359304 | tf_op jit(solution)/shard_map/ppermute | solution.py:32
  84.8 0.0 collective-permute-done.3.refs_4_
  84.8 1.1 collective-permute-start.10
  85.9 5.3 %products.3 = (f32[2,6,64,512]{3,2,1,0:T(8,128)S(1)}, bf16[2,6,64,512]{3,2,1,0:T(8,128)(2,1)S(1)}, bf16[2,6,64,512]{3,2,1,0:T(8,128)(2,1)S(1)}, bf16[2,6,64,512]{3,2,1,0:T(8,128)(2,1)S(1)}) custom-call(s32[56]{0:T(128)S(1)} %get-tuple-element.38.refs_0_.table_ref, bf16[8,512,640]{2,1,0:T(8,128)(2,1)S(1)} %bitcast.11, f32[1,640]{1,0:T(1,128)S(1)} %reshape.11.refs_2_, ...), custom_call_target="tpu_custom_call" | custom-call | tf_op jit(solution)/shard_map/products/pallas_call | solution.py:160
  91.2 1.0 collective-permute-start.4
  92.2 0.0 collective-permute-done.14.down_ref
  92.2 0.8 collective-permute-start.5
  93.0 7.5 %collective-permute-done.8.up_ref = bf16[2,6,64,512]{3,2,1,0:T(8,128)(2,1)S(1)} collective-permute-done((bf16[2,6,64,512]{3,2,1,0:T(8,128)(2,1)S(1)}, bf16[2,6,64,512]{3,2,1,0:T(8,128)(2,1)S(1)}, u32[]{:S(2)}, u32[]{:S(2)}) %collective-permute-start.8) | collective-permute-done | bytes 786464 | tf_op jit(solution)/shard_map/ppermute | solution.py:32
  100.6 0.5 collective-permute-start.6
  101.1 1.2 plane_sums.5
  102.3 15.1 %collective-permute-done.9.two_ref = bf16[2,6,64,512]{3,2,1,0:T(8,128)(2,1)S(1)} collective-permute-done((bf16[2,6,64,512]{3,2,1,0:T(8,128)(2,1)S(1)}, bf16[2,6,64,512]{3,2,1,0:T(8,128)(2,1)S(1)}, u32[]{:S(2)}, u32[]{:S(2)}) %collective-permute-start.9) | collective-permute-done | bytes 786464 | tf_op jit(solution)/shard_map/ppermute | solution.py:32
  117.4 3.9 %collective-permute-start.15 = (bf16[6,64,512]{2,1,0:T(8,128)(2,1)S(1)}, bf16[6,64,512]{2,1,0:T(8,128)(2,1)S(1)}, u32[]{:S(2)}, u32[]{:S(2)}) collective-permute-start(bf16[6,64,512]{2,1,0:T(8,128)(2,1)S(1)} %get-tuple-element.64), channel_id=1, source_target_pairs={{0,4},{1,5},{2,6},{3,7},{4,0},{5,1},{6,2},{7,3},{8,12},{9,13},{10,... | collective-permute-start | bytes 1179656 | tf_op jit(solution)/shard_map/ppermute | solution.py:36
  121.3 0.0 collective-permute-done.10.down_ref
  121.3 1.2 plane_sums.4
  122.5 3.5 %collective-permute-start.11 = (bf16[6,64,512]{2,1,0:T(8,128)(2,1)S(1)}, bf16[6,64,512]{2,1,0:T(8,128)(2,1)S(1)}, u32[]{:S(2)}, u32[]{:S(2)}) collective-permute-start(bf16[6,64,512]{2,1,0:T(8,128)(2,1)S(1)} %get-tuple-element.58), channel_id=1, source_target_pairs={{0,4},{1,5},{2,6},{3,7},{4,0},{5,1},{6,2},{7,3},{8,12},{9,13},{10,... | collective-permute-start | bytes 1179656 | tf_op jit(solution)/shard_map/ppermute | solution.py:36
  126.0 5.3 %collective-permute-done.15.got_ref = bf16[6,64,512]{2,1,0:T(8,128)(2,1)S(1)} collective-permute-done((bf16[6,64,512]{2,1,0:T(8,128)(2,1)S(1)}, bf16[6,64,512]{2,1,0:T(8,128)(2,1)S(1)}, u32[]{:S(2)}, u32[]{:S(2)}) %collective-permute-start.15) | collective-permute-done | bytes 393248 | tf_op jit(solution)/shard_map/ppermute | solution.py:36
  131.3 3.3 %totals.3 = (f32[18,64,512]{2,1,0:T(8,128)}, bf16[8,3,32,128]{3,2,1,0:T(8,128)(2,1)S(1)}, bf16[8,3,32,128]{3,2,1,0:T(8,128)(2,1)S(1)}) custom-call(s32[56]{0:T(128)S(1)} %get-tuple-element.38.refs_0_.table_ref, f32[6,64,512]{2,1,0:T(8,128)S(1)} %get-tuple-element.63.keep_ref, bf16[6,64,512]{2,1,0:T(8,128)(2,1)S(1)} %collective-permute-done.15.got_ref), custom_call_target="tpu_custom_call" | custom-call | tf_op jit(solution)/shard_map/totals/pallas_call | solution.py:229
  134.6 0.0 collective-permute-done.4.up_ref
  134.6 15.4 %collective-permute-done.5.two_ref = bf16[2,6,64,512]{3,2,1,0:T(8,128)(2,1)S(1)} collective-permute-done((bf16[2,6,64,512]{3,2,1,0:T(8,128)(2,1)S(1)}, bf16[2,6,64,512]{3,2,1,0:T(8,128)(2,1)S(1)}, u32[]{:S(2)}, u32[]{:S(2)}) %collective-permute-start.5) | collective-permute-done | bytes 786464 | tf_op jit(solution)/shard_map/ppermute | solution.py:32
  149.9 3.2 %collective-permute-done.6.down_ref = bf16[2,6,64,512]{3,2,1,0:T(8,128)(2,1)S(1)} collective-permute-done((bf16[2,6,64,512]{3,2,1,0:T(8,128)(2,1)S(1)}, bf16[2,6,64,512]{3,2,1,0:T(8,128)(2,1)S(1)}, u32[]{:S(2)}, u32[]{:S(2)}) %collective-permute-start.6) | collective-permute-done | bytes 786464 | tf_op jit(solution)/shard_map/ppermute | solution.py:32
  153.2 1.2 plane_sums.3
  154.4 4.0 %collective-permute-start.7 = (bf16[6,64,512]{2,1,0:T(8,128)(2,1)S(1)}, bf16[6,64,512]{2,1,0:T(8,128)(2,1)S(1)}, u32[]{:S(2)}, u32[]{:S(2)}) collective-permute-start(bf16[6,64,512]{2,1,0:T(8,128)(2,1)S(1)} %get-tuple-element.50), channel_id=1, source_target_pairs={{0,4},{1,5},{2,6},{3,7},{4,0},{5,1},{6,2},{7,3},{8,12},{9,13},{10,... | collective-permute-start | bytes 1179656 | tf_op jit(solution)/shard_map/ppermute | solution.py:36
  158.3 0.8 pad_maximum_fusion.2
  159.1 3.9 %all-to-all-start.2 = ((bf16[8,6,32,128]{3,2,1,0:T(8,128)(2,1)}), bf16[8,6,32,128]{3,2,1,0:T(8,128)(2,1)S(1)}, u32[]{:S(2)}, u32[]{:S(2)}) async-start(bf16[8,6,32,128]{3,2,1,0:T(8,128)(2,1)} %pad_maximum_fusion.2), calls=%async_computation.2 | async-start | bytes 786432 | tf_op jit(solution)/shard_map/all_to_all | solution.py:40
  163.0 0.0 collective-permute-done.11.got_ref
  163.0 3.3 %totals.4 = (f32[18,64,512]{2,1,0:T(8,128)}, bf16[8,3,32,128]{3,2,1,0:T(8,128)(2,1)S(1)}, bf16[8,3,32,128]{3,2,1,0:T(8,128)(2,1)S(1)}) custom-call(s32[56]{0:T(128)S(1)} %get-tuple-element.38.refs_0_.table_ref, f32[6,64,512]{2,1,0:T(8,128)S(1)} %get-tuple-element.57.keep_ref, ...), custom_call_target="tpu_custom_call", output_to_operand_aliasing={{0}: (3, {})} | custom-call | tf_op jit(solution)/shard_map/totals/pallas_call | solution.py:229
  166.3 0.0 collective-permute-start.18
  166.3 1.7 collective-permute-start.19
  168.0 3.3 %collective-permute-done.18 = bf16[8,3,32,128]{3,2,1,0:T(8,128)(2,1)S(1)} collective-permute-done((bf16[8,3,32,128]{3,2,1,0:T(8,128)(2,1)S(1)}, bf16[8,3,32,128]{3,2,1,0:T(8,128)(2,1)S(1)}, u32[]{:S(2)}, u32[]{:S(2)}) %collective-permute-start.18) | collective-permute-done | bytes 196640 | tf_op jit(solution)/shard_map/ppermute | solution.py:27
  171.4 0.0 collective-permute-done.19
  171.4 0.8 pad_maximum_fusion.1
  172.2 0.9 all-to-all-done.2.cut_ref
  173.1 7.4 %all-to-all-start.1 = ((bf16[8,6,32,128]{3,2,1,0:T(8,128)(2,1)}), bf16[8,6,32,128]{3,2,1,0:T(8,128)(2,1)S(1)}, u32[]{:S(2)}, u32[]{:S(2)}) async-start(bf16[8,6,32,128]{3,2,1,0:T(8,128)(2,1)} %pad_maximum_fusion.1), calls=%async_computation.1 | async-start | bytes 786432 | tf_op jit(solution)/shard_map/all_to_all | solution.py:40
  180.5 0.0 collective-permute-done.7.got_ref
  180.5 3.3 %totals.5 = (f32[18,64,512]{2,1,0:T(8,128)}, bf16[8,3,32,128]{3,2,1,0:T(8,128)(2,1)S(1)}, bf16[8,3,32,128]{3,2,1,0:T(8,128)(2,1)S(1)}) custom-call(s32[56]{0:T(128)S(1)} %get-tuple-element.38.refs_0_.table_ref, f32[6,64,512]{2,1,0:T(8,128)S(1)} %get-tuple-element.49.keep_ref, ...), custom_call_target="tpu_custom_call", output_to_operand_aliasing={{0}: (3, {})} | custom-call | tf_op jit(solution)/shard_map/totals/pallas_call | solution.py:229
  183.8 2.0 collective-permute-start.17
  185.8 5.1 %collective-permute-done.16 = bf16[8,3,32,128]{3,2,1,0:T(8,128)(2,1)S(1)} collective-permute-done((bf16[8,3,32,128]{3,2,1,0:T(8,128)(2,1)S(1)}, bf16[8,3,32,128]{3,2,1,0:T(8,128)(2,1)S(1)}, u32[]{:S(2)}, u32[]{:S(2)}) %collective-permute-start.16) | collective-permute-done | bytes 196640 | tf_op jit(solution)/shard_map/ppermute | solution.py:27
  190.9 2.8 %collective-permute-done.17 = bf16[8,3,32,128]{3,2,1,0:T(8,128)(2,1)S(1)} collective-permute-done((bf16[8,3,32,128]{3,2,1,0:T(8,128)(2,1)S(1)}, bf16[8,3,32,128]{3,2,1,0:T(8,128)(2,1)S(1)}, u32[]{:S(2)}, u32[]{:S(2)}) %collective-permute-start.17) | collective-permute-done | bytes 196640 | tf_op jit(solution)/shard_map/ppermute | solution.py:27
  193.7 0.8 pad_maximum_fusion
  194.5 6.2 %all-to-all-start = ((bf16[8,6,32,128]{3,2,1,0:T(8,128)(2,1)}), bf16[8,6,32,128]{3,2,1,0:T(8,128)(2,1)S(1)}, u32[]{:S(2)}, u32[]{:S(2)}) async-start(bf16[8,6,32,128]{3,2,1,0:T(8,128)(2,1)} %pad_maximum_fusion), calls=%async_computation | async-start | bytes 786432 | tf_op jit(solution)/shard_map/all_to_all | solution.py:40
  200.8 2.9 %mirrored.3.refs_0_ = f32[18,64,512]{2,1,0:T(8,128)} custom-call(s32[56]{0:T(128)S(1)} %get-tuple-element.38.refs_0_.table_ref, bf16[8,6,32,128]{3,2,1,0:T(8,128)(2,1)S(1)} %all-to-all-done.2.cut_ref), custom_call_target="tpu_custom_call" | custom-call | tf_op jit(solution)/shard_map/mirrored/pallas_call | solution.py:266
  203.7 2.9 %mirrored.4.refs_0_ = f32[18,64,512]{2,1,0:T(8,128)} custom-call(s32[56]{0:T(128)S(1)} %get-tuple-element.38.refs_0_.table_ref, bf16[8,6,32,128]{3,2,1,0:T(8,128)(2,1)S(1)} %all-to-all-done.1.cut_ref, f32[18,64,512]{2,1,0:T(8,128)} %mirrored.3.refs_0_), custom_call_target="tpu_custom_call", output_to_operand_aliasing={{}: (2, {})} | custom-call | tf_op jit(solution)/shard_map/mirrored/pallas_call | solution.py:266
  206.6 3.6 %all-to-all-done.cut_ref = bf16[8,6,32,128]{3,2,1,0:T(8,128)(2,1)S(1)} async-done(((bf16[8,6,32,128]{3,2,1,0:T(8,128)(2,1)}), bf16[8,6,32,128]{3,2,1,0:T(8,128)(2,1)S(1)}, u32[]{:S(2)}, u32[]{:S(2)}) %all-to-all-start) | async-done | bytes 393248 | tf_op jit(solution)/shard_map/all_to_all | solution.py:40
  210.2 2.9 %mirrored.5 = f32[18,64,512]{2,1,0:T(8,128)} custom-call(s32[56]{0:T(128)S(1)} %get-tuple-element.38.refs_0_.table_ref, bf16[8,6,32,128]{3,2,1,0:T(8,128)(2,1)S(1)} %all-to-all-done.cut_ref, f32[18,64,512]{2,1,0:T(8,128)} %mirrored.4.refs_0_), custom_call_target="tpu_custom_call", output_to_operand_aliasing={{}: (2, {})} | custom-call | tf_op jit(solution)/shard_map/mirrored/pallas_call | solution.py:266
  (11 shorter events, 0.0 us)
Async XLA Ops:
  0.7 2.5 %copy-start = (bf16[4096,640]{1,0:T(8,128)(2,1)S(1)}, bf16[4096,640]{1,0:T(8,128)(2,1)}, u32[]{:S(2)}) copy-start(bf16[4096,640]{1,0:T(8,128)(2,1)} %param.4) | copy-start | bytes 15728644
  3.2 0.7 copy-start.2
  3.9 0.7 copy-start.3
  8.7 22.5 %collective-permute-start = (bf16[3,512,640]{2,1,0:T(8,128)(2,1)S(1)}, bf16[3,512,640]{2,1,0:T(8,128)(2,1)S(1)}, u32[]{:S(2)}, u32[]{:S(2)}) collective-permute-start(bf16[3,512,640]{2,1,0:T(8,128)(2,1)S(1)} %get-tuple-element.41), channel_id=1, source_target_pairs={{0,120},{8,0},{16,8},{24,16},{32,24},{40,32},{48,40},{56,48},{64,5... | collective-permute-start | bytes 5898248 | tf_op jit(solution)/shard_map/ppermute | solution.py:27
  9.1 24.1 %collective-permute-start.1 = (bf16[3,512,640]{2,1,0:T(8,128)(2,1)S(1)}, bf16[3,512,640]{2,1,0:T(8,128)(2,1)S(1)}, u32[]{:S(2)}, u32[]{:S(2)}) collective-permute-start(bf16[3,512,640]{2,1,0:T(8,128)(2,1)S(1)} %get-tuple-element.42), channel_id=1, source_target_pairs={{0,8},{8,16},{16,24},{24,32},{32,40},{40,48},{48,56},{56,64},{64,7... | collective-permute-start | bytes 5898248 | tf_op jit(solution)/shard_map/ppermute | solution.py:27
  9.3 29.2 %copy-start.4 = (f32[640]{0:T(1024)S(1)}, f32[640]{0:T(1024)}, u32[]{:S(2)}) copy-start(f32[640]{0:T(1024)} %param.5) | copy-start | bytes 7684
  9.3 29.2 %copy-start.1 = (bf16[4096,640]{1,0:T(8,128)(2,1)S(1)}, bf16[4096,640]{1,0:T(8,128)(2,1)}, u32[]{:S(2)}) copy-start(bf16[4096,640]{1,0:T(8,128)(2,1)} %param.4) | copy-start | bytes 15728644
  33.1 48.5 %collective-permute-start.2 = (bf16[3,512,640]{2,1,0:T(8,128)(2,1)S(1)}, bf16[3,512,640]{2,1,0:T(8,128)(2,1)S(1)}, u32[]{:S(2)}, u32[]{:S(2)}) collective-permute-start(bf16[3,512,640]{2,1,0:T(8,128)(2,1)S(1)} %get-tuple-element.43), channel_id=1, source_target_pairs={{0,112},{8,120},{16,0},{24,8},{32,16},{40,24},{48,32},{56,40},{64,... | collective-permute-start | bytes 5898248 | tf_op jit(solution)/shard_map/ppermute | solution.py:27
  33.8 51.1 %collective-permute-start.3 = (bf16[3,512,640]{2,1,0:T(8,128)(2,1)S(1)}, bf16[3,512,640]{2,1,0:T(8,128)(2,1)S(1)}, u32[]{:S(2)}, u32[]{:S(2)}) collective-permute-start(bf16[3,512,640]{2,1,0:T(8,128)(2,1)S(1)} %get-tuple-element.44), channel_id=1, source_target_pairs={{0,16},{8,24},{16,32},{24,40},{32,48},{40,56},{48,64},{56,72},{64,... | collective-permute-start | bytes 5898248 | tf_op jit(solution)/shard_map/ppermute | solution.py:27
  43.8 20.6 %collective-permute-start.12 = (bf16[2,6,64,512]{3,2,1,0:T(8,128)(2,1)S(1)}, bf16[2,6,64,512]{3,2,1,0:T(8,128)(2,1)S(1)}, u32[]{:S(2)}, u32[]{:S(2)}) collective-permute-start(bf16[2,6,64,512]{3,2,1,0:T(8,128)(2,1)S(1)} %get-tuple-element.60), channel_id=1, source_target_pairs={{0,1},{1,2},{2,3},{3,0},{4,5},{5,6},{6,7},{7,4},{8,9},{9,10},{10,1... | collective-permute-start | bytes 2359304 | tf_op jit(solution)/shard_map/ppermute | solution.py:32
  45.4 45.7 %collective-permute-start.13 = (bf16[2,6,64,512]{3,2,1,0:T(8,128)(2,1)S(1)}, bf16[2,6,64,512]{3,2,1,0:T(8,128)(2,1)S(1)}, u32[]{:S(2)}, u32[]{:S(2)}) collective-permute-start(bf16[2,6,64,512]{3,2,1,0:T(8,128)(2,1)S(1)} %get-tuple-element.61), channel_id=1, source_target_pairs={{0,2},{1,3},{2,0},{3,1},{4,6},{5,7},{6,4},{7,5},{8,10},{9,11},{10,... | collective-permute-start | bytes 2359304 | tf_op jit(solution)/shard_map/ppermute | solution.py:32
  48.3 43.9 %collective-permute-start.14 = (bf16[2,6,64,512]{3,2,1,0:T(8,128)(2,1)S(1)}, bf16[2,6,64,512]{3,2,1,0:T(8,128)(2,1)S(1)}, u32[]{:S(2)}, u32[]{:S(2)}) collective-permute-start(bf16[2,6,64,512]{3,2,1,0:T(8,128)(2,1)S(1)} %get-tuple-element.62), channel_id=1, source_target_pairs={{0,3},{1,0},{2,1},{3,2},{4,7},{5,4},{6,5},{7,6},{8,11},{9,8},{10,9... | collective-permute-start | bytes 2359304 | tf_op jit(solution)/shard_map/ppermute | solution.py:32
  64.4 36.1 %collective-permute-start.8 = (bf16[2,6,64,512]{3,2,1,0:T(8,128)(2,1)S(1)}, bf16[2,6,64,512]{3,2,1,0:T(8,128)(2,1)S(1)}, u32[]{:S(2)}, u32[]{:S(2)}) collective-permute-start(bf16[2,6,64,512]{3,2,1,0:T(8,128)(2,1)S(1)} %get-tuple-element.54), channel_id=1, source_target_pairs={{0,1},{1,2},{2,3},{3,0},{4,5},{5,6},{6,7},{7,4},{8,9},{9,10},{10,1... | collective-permute-start | bytes 2359304 | tf_op jit(solution)/shard_map/ppermute | solution.py:32
  81.6 35.7 %collective-permute-start.9 = (bf16[2,6,64,512]{3,2,1,0:T(8,128)(2,1)S(1)}, bf16[2,6,64,512]{3,2,1,0:T(8,128)(2,1)S(1)}, u32[]{:S(2)}, u32[]{:S(2)}) collective-permute-start(bf16[2,6,64,512]{3,2,1,0:T(8,128)(2,1)S(1)} %get-tuple-element.55), channel_id=1, source_target_pairs={{0,2},{1,3},{2,0},{3,1},{4,6},{5,7},{6,4},{7,5},{8,10},{9,11},{10,... | collective-permute-start | bytes 2359304 | tf_op jit(solution)/shard_map/ppermute | solution.py:32
  84.8 36.4 %collective-permute-start.10 = (bf16[2,6,64,512]{3,2,1,0:T(8,128)(2,1)S(1)}, bf16[2,6,64,512]{3,2,1,0:T(8,128)(2,1)S(1)}, u32[]{:S(2)}, u32[]{:S(2)}) collective-permute-start(bf16[2,6,64,512]{3,2,1,0:T(8,128)(2,1)S(1)} %get-tuple-element.56), channel_id=1, source_target_pairs={{0,3},{1,0},{2,1},{3,2},{4,7},{5,4},{6,5},{7,6},{8,11},{9,8},{10,9... | collective-permute-start | bytes 2359304 | tf_op jit(solution)/shard_map/ppermute | solution.py:32
  91.2 43.4 %collective-permute-start.4 = (bf16[2,6,64,512]{3,2,1,0:T(8,128)(2,1)S(1)}, bf16[2,6,64,512]{3,2,1,0:T(8,128)(2,1)S(1)}, u32[]{:S(2)}, u32[]{:S(2)}) collective-permute-start(bf16[2,6,64,512]{3,2,1,0:T(8,128)(2,1)S(1)} %get-tuple-element.46), channel_id=1, source_target_pairs={{0,1},{1,2},{2,3},{3,0},{4,5},{5,6},{6,7},{7,4},{8,9},{9,10},{10,1... | collective-permute-start | bytes 2359304 | tf_op jit(solution)/shard_map/ppermute | solution.py:32
  92.2 57.7 %collective-permute-start.5 = (bf16[2,6,64,512]{3,2,1,0:T(8,128)(2,1)S(1)}, bf16[2,6,64,512]{3,2,1,0:T(8,128)(2,1)S(1)}, u32[]{:S(2)}, u32[]{:S(2)}) collective-permute-start(bf16[2,6,64,512]{3,2,1,0:T(8,128)(2,1)S(1)} %get-tuple-element.47), channel_id=1, source_target_pairs={{0,2},{1,3},{2,0},{3,1},{4,6},{5,7},{6,4},{7,5},{8,10},{9,11},{10,... | collective-permute-start | bytes 2359304 | tf_op jit(solution)/shard_map/ppermute | solution.py:32
  100.6 52.6 %collective-permute-start.6 = (bf16[2,6,64,512]{3,2,1,0:T(8,128)(2,1)S(1)}, bf16[2,6,64,512]{3,2,1,0:T(8,128)(2,1)S(1)}, u32[]{:S(2)}, u32[]{:S(2)}) collective-permute-start(bf16[2,6,64,512]{3,2,1,0:T(8,128)(2,1)S(1)} %get-tuple-element.48), channel_id=1, source_target_pairs={{0,3},{1,0},{2,1},{3,2},{4,7},{5,4},{6,5},{7,6},{8,11},{9,8},{10,9... | collective-permute-start | bytes 2359304 | tf_op jit(solution)/shard_map/ppermute | solution.py:32
  117.4 13.9 %collective-permute-start.15 = (bf16[6,64,512]{2,1,0:T(8,128)(2,1)S(1)}, bf16[6,64,512]{2,1,0:T(8,128)(2,1)S(1)}, u32[]{:S(2)}, u32[]{:S(2)}) collective-permute-start(bf16[6,64,512]{2,1,0:T(8,128)(2,1)S(1)} %get-tuple-element.64), channel_id=1, source_target_pairs={{0,4},{1,5},{2,6},{3,7},{4,0},{5,1},{6,2},{7,3},{8,12},{9,13},{10,... | collective-permute-start | bytes 1179656 | tf_op jit(solution)/shard_map/ppermute | solution.py:36
  122.5 40.5 %collective-permute-start.11 = (bf16[6,64,512]{2,1,0:T(8,128)(2,1)S(1)}, bf16[6,64,512]{2,1,0:T(8,128)(2,1)S(1)}, u32[]{:S(2)}, u32[]{:S(2)}) collective-permute-start(bf16[6,64,512]{2,1,0:T(8,128)(2,1)S(1)} %get-tuple-element.58), channel_id=1, source_target_pairs={{0,4},{1,5},{2,6},{3,7},{4,0},{5,1},{6,2},{7,3},{8,12},{9,13},{10,... | collective-permute-start | bytes 1179656 | tf_op jit(solution)/shard_map/ppermute | solution.py:36
  154.4 26.1 %collective-permute-start.7 = (bf16[6,64,512]{2,1,0:T(8,128)(2,1)S(1)}, bf16[6,64,512]{2,1,0:T(8,128)(2,1)S(1)}, u32[]{:S(2)}, u32[]{:S(2)}) collective-permute-start(bf16[6,64,512]{2,1,0:T(8,128)(2,1)S(1)} %get-tuple-element.50), channel_id=1, source_target_pairs={{0,4},{1,5},{2,6},{3,7},{4,0},{5,1},{6,2},{7,3},{8,12},{9,13},{10,... | collective-permute-start | bytes 1179656 | tf_op jit(solution)/shard_map/ppermute | solution.py:36
  159.1 13.9 %all-to-all-start.2 = ((bf16[8,6,32,128]{3,2,1,0:T(8,128)(2,1)}), bf16[8,6,32,128]{3,2,1,0:T(8,128)(2,1)S(1)}, u32[]{:S(2)}, u32[]{:S(2)}) async-start(bf16[8,6,32,128]{3,2,1,0:T(8,128)(2,1)} %pad_maximum_fusion.2), calls=%async_computation.2 | async-start | bytes 786432 | tf_op jit(solution)/shard_map/all_to_all | solution.py:40
  166.3 5.1 %collective-permute-start.18 = (bf16[8,3,32,128]{3,2,1,0:T(8,128)(2,1)S(1)}, bf16[8,3,32,128]{3,2,1,0:T(8,128)(2,1)S(1)}, u32[]{:S(2)}, u32[]{:S(2)}) collective-permute-start(bf16[8,3,32,128]{3,2,1,0:T(8,128)(2,1)S(1)} %get-tuple-element.70), channel_id=1, source_target_pairs={{0,8},{8,16},{16,24},{24,32},{32,40},{40,48},{48,56},{56,64},{64,7... | collective-permute-start | bytes 589832 | tf_op jit(solution)/shard_map/ppermute | solution.py:27
  166.3 5.1 %collective-permute-start.19 = (bf16[8,3,32,128]{3,2,1,0:T(8,128)(2,1)S(1)}, bf16[8,3,32,128]{3,2,1,0:T(8,128)(2,1)S(1)}, u32[]{:S(2)}, u32[]{:S(2)}) collective-permute-start(bf16[8,3,32,128]{3,2,1,0:T(8,128)(2,1)S(1)} %get-tuple-element.71), channel_id=1, source_target_pairs={{0,120},{8,0},{16,8},{24,16},{32,24},{40,32},{48,40},{56,48},{64,5... | collective-permute-start | bytes 589832 | tf_op jit(solution)/shard_map/ppermute | solution.py:27
  173.1 21.4 %all-to-all-start.1 = ((bf16[8,6,32,128]{3,2,1,0:T(8,128)(2,1)}), bf16[8,6,32,128]{3,2,1,0:T(8,128)(2,1)S(1)}, u32[]{:S(2)}, u32[]{:S(2)}) async-start(bf16[8,6,32,128]{3,2,1,0:T(8,128)(2,1)} %pad_maximum_fusion.1), calls=%async_computation.1 | async-start | bytes 786432 | tf_op jit(solution)/shard_map/all_to_all | solution.py:40
  183.8 7.1 %collective-permute-start.16 = (bf16[8,3,32,128]{3,2,1,0:T(8,128)(2,1)S(1)}, bf16[8,3,32,128]{3,2,1,0:T(8,128)(2,1)S(1)}, u32[]{:S(2)}, u32[]{:S(2)}) collective-permute-start(bf16[8,3,32,128]{3,2,1,0:T(8,128)(2,1)S(1)} %get-tuple-element.68), channel_id=1, source_target_pairs={{0,16},{8,24},{16,32},{24,40},{32,48},{40,56},{48,64},{56,72},{64,... | collective-permute-start | bytes 589832 | tf_op jit(solution)/shard_map/ppermute | solution.py:27
  183.8 9.9 %collective-permute-start.17 = (bf16[8,3,32,128]{3,2,1,0:T(8,128)(2,1)S(1)}, bf16[8,3,32,128]{3,2,1,0:T(8,128)(2,1)S(1)}, u32[]{:S(2)}, u32[]{:S(2)}) collective-permute-start(bf16[8,3,32,128]{3,2,1,0:T(8,128)(2,1)S(1)} %get-tuple-element.69), channel_id=1, source_target_pairs={{0,112},{8,120},{16,0},{24,8},{32,16},{40,24},{48,32},{56,40},{64,... | collective-permute-start | bytes 589832 | tf_op jit(solution)/shard_map/ppermute | solution.py:27
  194.5 15.7 %all-to-all-start = ((bf16[8,6,32,128]{3,2,1,0:T(8,128)(2,1)}), bf16[8,6,32,128]{3,2,1,0:T(8,128)(2,1)S(1)}, u32[]{:S(2)}, u32[]{:S(2)}) async-start(bf16[8,6,32,128]{3,2,1,0:T(8,128)(2,1)} %pad_maximum_fusion), calls=%async_computation | async-start | bytes 786432 | tf_op jit(solution)/shard_map/all_to_all | solution.py:40

commit v3 on v2

v3 whole, which is shorter than its diff:
```python
import jax
import jax.numpy as jnp
from jax import lax
from jax.experimental import pallas as pl
from jax.experimental.pallas import tpu as pltpu
from jax.sharding import PartitionSpec as P

BLK = 512
SPAN = 2
MULT = 3
STORED = 8
LISTED = 18
LOCAL = 6
NTRANS = 16
NPW = 8
NY = 4
NZ = 2
ROWS = BLK // NPW
HALF = ROWS // 2
STEPS = (1, -1, 2, -2)
ORDER, FIRST, SECOND, YAT, ZAT, TABLE = 0, LISTED, 2 * LISTED, 3 * LISTED, 3 * LISTED + 1, 3 * LISTED + 2
VMEM_BYTES = 24 * 2**20


def shifted(value, steps):
    pairs = [(source, (source + steps) % NTRANS) for source in range(NTRANS)]
    return lax.ppermute(value, "trans", pairs)


def along_y(value, steps):
    pairs = [(z * NY + y, z * NY + (y + steps) % NY) for z in range(NZ) for y in range(NY)]
    return lax.ppermute(value, "pw", pairs)


def across_z(value):
    return lax.ppermute(value, "pw", [(source, (source + NY) % NPW) for source in range(NPW)])


def exchanged(value):
    return lax.all_to_all(value, "pw", split_axis=0, concat_axis=0, tiled=True)


def start_of(step):
    return 0 if step == 0 else LOCAL + MULT * STEPS.index(step)


def params():
    return pltpu.CompilerParams(vmem_limit_bytes=VMEM_BYTES)


def table_kernel(place_ref, pairs_ref, owner_ref, table_ref):
    device = place_ref[0]
    table_ref[YAT] = place_ref[1] & (NY - 1)
    table_ref[ZAT] = place_ref[1] >> 2
    filled = {step: start_of(step) for step in (0, *STEPS)}
    for q in range(LISTED):
        pair = device * LISTED + q
        first = owner_ref[pairs_ref[0, pair]]
        second = owner_ref[pairs_ref[1, pair]]
        distance = (((second >> 3) - device + SPAN + NTRANS) & (NTRANS - 1)) - SPAN
        place = jnp.int32(0)
        for step in filled:
            here = distance == step
            place = jnp.where(here, filled[step], place)
            filled[step] = jnp.where(here, filled[step] + 1, filled[step])
        source = (device - distance + NTRANS) & (NTRANS - 1)
        table_ref[ORDER + place] = jnp.int32(q)
        table_ref[FIRST + place] = first & (STORED - 1)
        table_ref[SECOND + place] = owner_ref[pairs_ref[1, source * LISTED + q]] & (STORED - 1)


def make_table(place, pairs, owner):
    smem = pl.BlockSpec(memory_space=pltpu.SMEM)
    return pl.pallas_call(
        table_kernel,
        out_shape=jax.ShapeDtypeStruct((TABLE,), jnp.int32),
        in_specs=[smem, smem, smem],
        out_specs=smem,
        compiler_params=params(),
        cost_estimate=pl.CostEstimate(flops=5750000001, bytes_accessed=15000001, transcendentals=0),
        name="make_table",
    )(place, pairs, owner)


def select_kernel(steps, table_ref, blocks_ref, *rest):
    sends, (held, in_sems, out_sems) = rest[: len(steps)], rest[len(steps) :]
    loads, stores = [], []
    for at, step in enumerate(steps):
        for j in range(MULT):
            n = at * MULT + j
            slot = table_ref[FIRST + start_of(step) + j]
            loads.append(pltpu.make_async_copy(blocks_ref.at[slot], held.at[n], in_sems.at[n]))
            stores.append(pltpu.make_async_copy(held.at[n], sends[at].at[j], out_sems.at[n]))
            loads[-1].start()
    for load, store in zip(loads, stores):
        load.wait()
        store.start()
    for store in stores:
        store.wait()


def select(steps, table, blocks):
    width = blocks.shape[2]
    count = MULT * len(steps)
    anywhere = pl.BlockSpec(memory_space=pl.ANY)
    return pl.pallas_call(
        lambda *refs: select_kernel(steps, *refs),
        out_shape=[jax.ShapeDtypeStruct((MULT, BLK, width), jnp.bfloat16)] * len(steps),
        in_specs=[pl.BlockSpec(memory_space=pltpu.SMEM), anywhere],
        out_specs=[anywhere] * len(steps),
        scratch_shapes=[
            pltpu.VMEM((count, BLK, width), jnp.bfloat16),
            pltpu.SemaphoreType.DMA((count,)),
            pltpu.SemaphoreType.DMA((count,)),
        ],
        compiler_params=params(),
        cost_estimate=pl.CostEstimate(flops=5750000001, bytes_accessed=15000001, transcendentals=0),
        name="select",
    )(table, blocks)


def products_kernel(count, table_ref, right_ref, coulomb_ref, *refs):
    lefts, (own_ref, up_add_ref, down_add_ref, up_two_ref, down_two_ref, up_ref, down_ref, weighted_ref) = refs[:-8], refs[-8:]
    each = count // len(lefts)
    y = table_ref[YAT]
    for at, left_ref in enumerate(lefts):

        @pl.when(pl.program_id(0) // each == at)
        def _():
            for dy in range(NY):
                for z in range(NZ):
                    to = (dy * NZ + z) * ROWS
                    source = z * (NY * ROWS) + ((y + dy) & (NY - 1)) * ROWS
                    rows = left_ref[0, pl.ds(pl.multiple_of(source, ROWS), ROWS), :]
                    weighted_ref[to : to + ROWS, :] = (rows.astype(jnp.float32) * coulomb_ref[...]).astype(jnp.bfloat16)

    part = lax.dot_general(
        weighted_ref[...], right_ref[0], (((1,), (1,)), ((), ())), preferred_element_type=jnp.float32
    ).reshape(NY, NZ, 1, ROWS, BLK)
    own_ref[...] = part[0]
    up_add_ref[...] = part[1, 0]
    up_ref[0] = part[1, 1].astype(jnp.bfloat16)
    up_two_ref[...] = part[2, 0].astype(jnp.bfloat16)
    down_two_ref[...] = part[2, 1].astype(jnp.bfloat16)
    down_ref[0] = part[3, 0].astype(jnp.bfloat16)
    down_add_ref[...] = part[3, 1]


def products(table, blocks, coulomb, lefts, start, count):
    width = blocks.shape[2]
    each = count // len(lefts)
    if lefts[0].shape[0] == STORED:
        left_specs = [pl.BlockSpec((1, BLK, width), lambda i, table: (table[FIRST + start + i], 0, 0))]
    else:
        left_specs = [
            pl.BlockSpec((1, BLK, width), lambda i, table, at=at: (jnp.clip(i - at * each, 0, each - 1), 0, 0))
            for at in range(len(lefts))
        ]
    half = (count, ROWS, BLK)
    half_spec = pl.BlockSpec((1, ROWS, BLK), lambda i, table: (i, 0, 0))
    whole = (NZ, count, ROWS, BLK)
    return pl.pallas_call(
        lambda *refs: products_kernel(count, *refs),
        out_shape=[
            jax.ShapeDtypeStruct(whole, jnp.float32),
            jax.ShapeDtypeStruct(half, jnp.float32),
            jax.ShapeDtypeStruct(half, jnp.float32),
            jax.ShapeDtypeStruct(half, jnp.bfloat16),
            jax.ShapeDtypeStruct(half, jnp.bfloat16),
            jax.ShapeDtypeStruct(whole, jnp.bfloat16),
            jax.ShapeDtypeStruct(whole, jnp.bfloat16),
        ],
        grid_spec=pltpu.PrefetchScalarGridSpec(
            num_scalar_prefetch=1,
            grid=(count,),
            in_specs=[
                pl.BlockSpec((1, BLK, width), lambda i, table: (table[SECOND + start + i], 0, 0)),
                pl.BlockSpec((1, width), lambda i, table: (0, 0)),
                *left_specs,
            ],
            out_specs=[
                pl.BlockSpec((NZ, 1, ROWS, BLK), lambda i, table: (0, i, 0, 0)),
                half_spec,
                half_spec,
                half_spec,
                half_spec,
                pl.BlockSpec((1, 1, ROWS, BLK), lambda i, table: (1, i, 0, 0)),
                pl.BlockSpec((1, 1, ROWS, BLK), lambda i, table: (0, i, 0, 0)),
            ],
            scratch_shapes=[pltpu.VMEM((BLK, width), jnp.bfloat16)],
        ),
        compiler_params=params(),
        cost_estimate=pl.CostEstimate(flops=5750000001, bytes_accessed=15000001, transcendentals=0),
        name="products",
    )(table, blocks, coulomb, *lefts)


def passed_kernel(up_add_ref, up_got_ref, down_add_ref, down_got_ref, *refs):
    up_ref, down_ref = refs[-2:]
    up_ref[0] = (up_add_ref[...] + up_got_ref[...].astype(jnp.float32)).astype(jnp.bfloat16)
    down_ref[0] = (down_add_ref[...] + down_got_ref[...].astype(jnp.float32)).astype(jnp.bfloat16)


def passed_on(up_add, up_got, down_add, down_got, up, down):
    count = up_add.shape[0]
    half = pl.BlockSpec((MULT, ROWS, BLK), lambda i: (i, 0, 0))
    whole = jax.ShapeDtypeStruct((NZ, count, ROWS, BLK), jnp.bfloat16)
    return pl.pallas_call(
        passed_kernel,
        out_shape=[whole, whole],
        grid=(count // MULT,),
        in_specs=[half] * 4 + [pl.BlockSpec(memory_space=pl.ANY)] * 2,
        out_specs=[
            pl.BlockSpec((1, MULT, ROWS, BLK), lambda i: (0, i, 0, 0)),
            pl.BlockSpec((1, MULT, ROWS, BLK), lambda i: (1, i, 0, 0)),
        ],
        input_output_aliases={4: 0, 5: 1},
        compiler_params=params(),
        cost_estimate=pl.CostEstimate(flops=5750000001, bytes_accessed=15000001, transcendentals=0),
        name="passed_on",
    )(up_add, up_got, down_add, down_got, up, down)


def plane_kernel(table_ref, own_ref, up_ref, down_ref, keep_ref, give_ref):
    z = table_ref[ZAT]

    def total(side):
        return own_ref[side] + up_ref[side].astype(jnp.float32) + down_ref[side].astype(jnp.float32)

    keep_ref[...] = total(z)
    give_ref[...] = total(1 - z).astype(jnp.bfloat16)


def plane_sums(table, own, up, down):
    count = own.shape[1]
    return pl.pallas_call(
        plane_kernel,
        out_shape=[
            jax.ShapeDtypeStruct((count, ROWS, BLK), jnp.float32),
            jax.ShapeDtypeStruct((count, ROWS, BLK), jnp.bfloat16),
        ],
        grid_spec=pltpu.PrefetchScalarGridSpec(
            num_scalar_prefetch=1,
            grid=(count // MULT,),
            in_specs=[pl.BlockSpec((NZ, MULT, ROWS, BLK), lambda i, table: (0, i, 0, 0))] * 3,
            out_specs=[pl.BlockSpec((MULT, ROWS, BLK), lambda i, table: (i, 0, 0))] * 2,
        ),
        compiler_params=params(),
        cost_estimate=pl.CostEstimate(flops=5750000001, bytes_accessed=15000001, transcendentals=0),
        name="plane_sums",
    )(table, own, up, down)


def cut_columns(total, cut_ref):
    both = jnp.concatenate([total, pltpu.roll(total, BLK - HALF, 1)], axis=0)
    columns = jnp.transpose(both, (1, 0))
    for target in range(NPW):
        cut_ref[target, 0] = columns[target * ROWS : target * ROWS + HALF].astype(cut_ref.dtype)


CUT = (NPW, 1, HALF, 2 * ROWS)


def totals_kernel(placed, table_ref, keep_ref, got_ref, *refs):
    total = keep_ref[0] + got_ref[0].astype(jnp.float32)
    cut_columns(total, refs[-1])
    if placed:
        refs[-2][0] = total
    else:
        for n, out_ref in enumerate(refs[-3:-1]):

            @pl.when(pl.program_id(0) // MULT == n)
            def _():
                out_ref[0] = total.astype(out_ref.dtype)


def totals(table, keep, got, placed, room, cut):
    count = keep.shape[0]
    carried = [] if cut is None else [cut]
    offset = room - count if carried else 0
    block = (1, ROWS, BLK)
    if placed:
        out_shape = [jax.ShapeDtypeStruct((LISTED, ROWS, BLK), jnp.float32)]
        out_specs = [pl.BlockSpec(block, lambda i, table: (table[ORDER + i], 0, 0))]
    else:
        out_shape = [jax.ShapeDtypeStruct((MULT, ROWS, BLK), jnp.bfloat16)] * 2
        out_specs = [
            pl.BlockSpec(block, lambda i, table, n=n: (jnp.clip(i - n * MULT, 0, MULT - 1), 0, 0)) for n in range(2)
        ]
    return pl.pallas_call(
        lambda *refs: totals_kernel(placed, *refs),
        out_shape=out_shape + [jax.ShapeDtypeStruct((NPW, room, HALF, 2 * ROWS), jnp.bfloat16)],
        grid_spec=pltpu.PrefetchScalarGridSpec(
            num_scalar_prefetch=1,
            grid=(count,),
            in_specs=[pl.BlockSpec(block, lambda i, table: (i, 0, 0))] * 2
            + [pl.BlockSpec(memory_space=pl.ANY)] * len(carried),
            out_specs=out_specs + [pl.BlockSpec(CUT, lambda i, table: (0, offset + i, 0, 0))],
        ),
        input_output_aliases={3: len(out_shape)} if carried else {},
        compiler_params=params(),
        cost_estimate=pl.CostEstimate(flops=5750000001, bytes_accessed=15000001, transcendentals=0),
        name="totals",
    )(table, keep, got, *carried)


def finish_kernel(start, count, arrived_start, table_ref, cut_ref, *refs):
    arrived, (kernel_ref, kernel_t_ref, held, sems) = refs[:2], refs[-4:]
    low = lax.broadcasted_iota(jnp.int32, (HALF, 2 * ROWS), 1) < ROWS
    copies = []

    def send(slot, out_ref, at):
        copies.append(pltpu.make_async_copy(held.at[slot], out_ref.at[table_ref[ORDER + at]], sems.at[slot]))
        copies[-1].start()

    for n, arrived_ref in enumerate(arrived):
        for j in range(MULT):
            slot = count + n * MULT + j
            held[slot] = arrived_ref[j].astype(jnp.float32)
            send(slot, kernel_ref, arrived_start + n * MULT + j)
    for at in range(count):
        for pair in range(NPW // 2):
            even = cut_ref[2 * pair, at].astype(jnp.float32)
            odd = cut_ref[2 * pair + 1, at].astype(jnp.float32)
            lanes = pl.ds(2 * ROWS * pair, 2 * ROWS)
            held[at, :HALF, lanes] = jnp.where(low, even, pltpu.roll(odd, ROWS, 1))
            held[at, HALF:, lanes] = jnp.where(low, pltpu.roll(even, ROWS, 1), odd)
        send(at, kernel_t_ref, start + at)
    for copy in copies:
        copy.wait()


def finish(table, cut, arrived, arrived_start, start, kernel, kernel_t):
    count = cut.shape[1]
    carried = [kernel] if kernel_t is None else [kernel, kernel_t]
    vmem = pl.BlockSpec(memory_space=pltpu.VMEM)
    anywhere = pl.BlockSpec(memory_space=pl.ANY)
    slots = count + 2 * MULT
    return pl.pallas_call(
        lambda *refs: finish_kernel(start, count, arrived_start, *refs),
        out_shape=[jax.ShapeDtypeStruct((LISTED, ROWS, BLK), jnp.float32)] * 2,
        in_specs=[pl.BlockSpec(memory_space=pltpu.SMEM), vmem, vmem, vmem] + [anywhere] * len(carried),
        out_specs=[anywhere] * 2,
        scratch_shapes=[pltpu.VMEM((slots, ROWS, BLK), jnp.float32), pltpu.SemaphoreType.DMA((slots,))],
        input_output_aliases={4 + n: n for n in range(len(carried))},
        compiler_params=params(),
        cost_estimate=pl.CostEstimate(flops=5750000001, bytes_accessed=15000001, transcendentals=0),
        name="finish",
    )(table, cut, *arrived, *carried)


def after(values, others):
    count = len(values)
    return lax.optimization_barrier((*values, *others))[:count]


def body(densities, coulomb, pairs, owner):
    blocks = densities.reshape(STORED, BLK, densities.shape[1])
    weight = coulomb.reshape(1, -1)
    place = jnp.stack([lax.axis_index("trans"), lax.axis_index("pw")]).astype(jnp.int32)
    table = make_table(place, pairs.T, owner)

    def begin(lefts, start, table=table):
        own, up_add, down_add, up_two, down_two, up, down = products(table, blocks, weight, lefts, start, 2 * MULT)
        return own, up_add, along_y(up_two, 1), down_add, along_y(down_two, NY - 1), up, down

    def planes(own, up, down):
        return own, along_y(up, 1), along_y(down, NY - 1)

    def across(parts):
        keep, give = plane_sums(table, *parts)
        return keep, across_z(give)

    def back(arrays, steps):
        return [shifted(array, -step) for array, step in zip(arrays, steps)]

    near_steps, far_steps = STEPS[:2], STEPS[2:]
    to_near, to_far = LOCAL, LOCAL + 2 * MULT
    near = select(near_steps, table, blocks)
    (ready,) = after((table,), near)
    near = [shifted(send, step) for step, send in zip(near_steps, near)]
    begun_local = begin([blocks], 0, ready)
    far = select(far_steps, *after((ready,), (begun_local[0],)), blocks)
    passed = passed_on(*begun_local[1:])
    near = after(near, passed)
    local = planes(begun_local[0], *passed)
    far = [shifted(send, step) for step, send in zip(far_steps, after(far, near))]
    begun_near = begin(near, to_near)
    parts_near = planes(begun_near[0], *passed_on(*begun_near[1:]))
    begun_far = begin(after(far, local[1:]), to_far)
    kernel, cut = totals(table, *across(local), True, to_far, None)
    *blocks_near, cut = totals(table, *across(parts_near), False, to_far, cut)
    blocks_near = back(blocks_near, near_steps)
    kernel, kernel_t = finish(table, exchanged(cut), blocks_near, to_near, 0, kernel, None)
    parts_far = planes(begun_far[0], *passed_on(*begun_far[1:]))
    keep, got = across(parts_far)
    *blocks_far, cut = totals(table, *after((keep, got), (kernel_t,)), False, 2 * MULT, None)
    blocks_far = back(blocks_far, far_steps)
    kernel, kernel_t = finish(table, exchanged(cut), blocks_far, to_far, to_far, kernel, kernel_t)
    return jnp.transpose(kernel, (1, 0, 2)), jnp.transpose(kernel_t, (1, 0, 2))


def solution(mesh):
    in_specs = (P("trans", "pw"), P("pw"), P(), P())
    out_specs = (P("pw", "trans", None), P("pw", "trans", None))
    return jax.shard_map(body, mesh=mesh, in_specs=in_specs, out_specs=out_specs, check_vma=False)
```

time: 214 us -> 162 us (0.76)
  waiting for transfers between devices: 108 us -> 61.4 us
  local copies, waits for them, and re-layouts: 3.83 us -> 8.05 us
  Pallas kernels: 45.4 us -> 41.6 us
  starting transfers between devices: 52.6 us -> 50.1 us
  other arithmetic: 2.42 us -> 0.08 us
    ppermute x8, waiting for transfers between devices: 47.6 us -> 13.7 us  [shifted(): return lax.ppermute(value, 'trans', pairs)]
    ppermute x9 -> x12, waiting for transfers between devices: 50.7 us -> 40.3 us  [along_y(): return lax.ppermute(value, 'pw', pairs)]
    all_to_all x3 -> x2, starting transfers between devices: 17.5 us -> 10.3 us  [exchanged(): return lax.all_to_all(value, 'pw', split_axis=0, concat_axis=0, tiled=True)]
    unnamed x10 -> x22, local copies, waits for them, and re-layouts: 3.83 us -> 8.05 us
    ppermute x9 -> x12, starting transfers between devices: 14 us -> 17.6 us  [along_y(): return lax.ppermute(value, 'pw', pairs)]
    pallas_call x8 -> x11, Pallas kernels: 26 us -> 22.5 us  [the longest x3 9.64 us: totals(): pl.pallas_call(lambda *refs: totals_kernel(placed, *refs), out_shape=out_...]
    concatenate x3 -> x0, other arithmetic: 2.34 us -> none  [body(): jnp.concatenate(cuts, axis=1)]
    all_to_all x3 -> x2, waiting for transfers between devices: 4.57 us -> 3.02 us  [exchanged(): return lax.all_to_all(value, 'pw', split_axis=0, concat_axis=0, tiled=True)]
  transfers between devices with their start and end apart: 23 -> 25, of which waited for: 14 -> 12; matrix products, arithmetic and copies ran while one was open for 1% -> 0% of each run, Pallas kernels for 18% -> 20%
where the time goes in v3:
time: 162 us
  waiting for transfers between devices  61.4 us (38%)
  starting transfers between devices  50.1 us (31%)
  Pallas kernels  41.6 us (26%)
  local copies, waits for them, and re-layouts  8.05 us (5%)
    ppermute x12, waiting for transfers between devices, along_y(): return lax.ppermute(value, 'pw', pairs)  40.3 us
    ppermute x12, starting transfers between devices, along_y(): return lax.ppermute(value, 'pw', pairs)  17.6 us
    pallas_call x3, Pallas kernels, products(): pl.pallas_call(lambda *refs: products_kernel(count, *refs), out_shape=[ja...  16 us
    ppermute x8, waiting for transfers between devices, shifted(): return lax.ppermute(value, 'trans', pairs)  13.7 us
    ppermute x3, starting transfers between devices, across_z(): lax.ppermute(value, 'pw', [(source, (source + NY) % NPW) for source in ra...  11.8 us
    ppermute x8, starting transfers between devices, shifted(): return lax.ppermute(value, 'trans', pairs)  10.4 us
    all_to_all x2, starting transfers between devices, exchanged(): return lax.all_to_all(value, 'pw', split_axis=0, concat_axis=0, tiled=True)  10.3 us
    pallas_call x3, Pallas kernels, totals(): pl.pallas_call(lambda *refs: totals_kernel(placed, *refs), out_shape=out_...  9.64 us
  transfers between devices with their start and end apart: 25, of which 12 were waited for; matrix products, arithmetic and copies ran while one was open for 0% of the time, Pallas kernels for 20%

profile of v3, /device:TPU:6, one launch (start us, length us, event | category | flops | bytes accessed | tf_op | source)
XLA Modules:
  0.0 162.0 jit_solution(1227756462772498834)
XLA Ops:
  0.6 0.1 pad_add_fusion.place_ref
  0.7 0.7 copy-done.4
  1.4 0.7 copy-done.5
  2.1 1.5 make_table.1.refs_0_.table_ref
  3.6 1.0 copy-done
  4.5 3.1 %select.2 = (bf16[3,512,640]{2,1,0:T(8,128)(2,1)S(1)}, bf16[3,512,640]{2,1,0:T(8,128)(2,1)S(1)}) custom-call(s32[56]{0:T(128)S(1)} %make_table.1.refs_0_.table_ref, bf16[8,512,640]{2,1,0:T(8,128)(2,1)S(1)} %bitcast.6), custom_call_target="tpu_custom_call" | custom-call | flops 5750000128 | bytes 15000001 | tf_op jit(solution)/shard_map/select/pallas_call | solution.py:106
  7.7 0.1 collective-permute-start
  7.8 1.7 %collective-permute-start.1 = (bf16[3,512,640]{2,1,0:T(8,128)(2,1)S(1)}, bf16[3,512,640]{2,1,0:T(8,128)(2,1)S(1)}, u32[]{:S(2)}, u32[]{:S(2)}) collective-permute-start(bf16[3,512,640]{2,1,0:T(8,128)(2,1)S(1)} %get-tuple-element.62), channel_id=1, source_target_pairs={{0,120},{8,0},{16,8},{24,16},{32,24},{40,32},{48,40},{56,48},{64,5... | collective-permute-start | bytes 5898248 | tf_op jit(solution)/shard_map/ppermute | solution.py:27
  9.5 5.1 %products.3 = (f32[2,6,64,512]{3,2,1,0:T(8,128)S(1)}, f32[6,64,512]{2,1,0:T(8,128)S(1)}, f32[6,64,512]{2,1,0:T(8,128)S(1)}, bf16[6,64,512]{2,1,0:T(8,128)(2,1)S(...) custom-call(s32[56]{0:T(128)S(1)} %make_table.1.refs_0_.table_ref, ...), custom_call_target="tpu_custom_call" | custom-call | flops 5750000128 | bytes 15000001 | tf_op jit(solution)/shard_map/products/pallas_call | solution.py:162
  14.6 1.6 %collective-permute-start.2 = (bf16[6,64,512]{2,1,0:T(8,128)(2,1)S(1)}, bf16[6,64,512]{2,1,0:T(8,128)(2,1)S(1)}, u32[]{:S(2)}, u32[]{:S(2)}) collective-permute-start(bf16[6,64,512]{2,1,0:T(8,128)(2,1)S(1)} %get-tuple-element.69), channel_id=1, source_target_pairs={{0,1},{1,2},{2,3},{3,0},{4,5},{5,6},{6,7},{7,4},{8,9},{9,10},{10,1... | collective-permute-start | bytes 1179656 | tf_op jit(solution)/shard_map/ppermute | solution.py:32
  16.2 1.7 %collective-permute-start.3 = (bf16[6,64,512]{2,1,0:T(8,128)(2,1)S(1)}, bf16[6,64,512]{2,1,0:T(8,128)(2,1)S(1)}, u32[]{:S(2)}, u32[]{:S(2)}) collective-permute-start(bf16[6,64,512]{2,1,0:T(8,128)(2,1)S(1)} %get-tuple-element.71), channel_id=1, source_target_pairs={{0,3},{1,0},{2,1},{3,2},{4,7},{5,4},{6,5},{7,6},{8,11},{9,8},{10,9... | collective-permute-start | bytes 1179656 | tf_op jit(solution)/shard_map/ppermute | solution.py:32
  17.9 3.1 %select.3 = (bf16[3,512,640]{2,1,0:T(8,128)(2,1)S(1)}, bf16[3,512,640]{2,1,0:T(8,128)(2,1)S(1)}) custom-call(s32[56]{0:T(128)S(1)} %make_table.1.refs_0_.table_ref, bf16[8,512,640]{2,1,0:T(8,128)(2,1)S(1)} %bitcast.9), custom_call_target="tpu_custom_call" | custom-call | flops 5750000128 | bytes 15000001 | tf_op jit(solution)/shard_map/select/pallas_call | solution.py:106
  21.0 6.1 %collective-permute-done.2.up_got_ref = bf16[6,64,512]{2,1,0:T(8,128)(2,1)S(1)} collective-permute-done((bf16[6,64,512]{2,1,0:T(8,128)(2,1)S(1)}, bf16[6,64,512]{2,1,0:T(8,128)(2,1)S(1)}, u32[]{:S(2)}, u32[]{:S(2)}) %collective-permute-start.2) | collective-permute-done | bytes 393248 | tf_op jit(solution)/shard_map/ppermute | solution.py:32
  27.2 0.0 collective-permute-done.3.down_got_ref
  27.2 0.2 passed_on.3
  27.4 4.5 %collective-permute-done.refs_3_ = bf16[3,512,640]{2,1,0:T(8,128)(2,1)S(1)} collective-permute-done((bf16[3,512,640]{2,1,0:T(8,128)(2,1)S(1)}, bf16[3,512,640]{2,1,0:T(8,128)(2,1)S(1)}, u32[]{:S(2)}, u32[]{:S(2)}) %collective-permute-start) | collective-permute-done | bytes 1966112 | tf_op jit(solution)/shard_map/ppermute | solution.py:27
  31.8 3.9 %collective-permute-start.4 = (bf16[3,512,640]{2,1,0:T(8,128)(2,1)S(1)}, bf16[3,512,640]{2,1,0:T(8,128)(2,1)S(1)}, u32[]{:S(2)}, u32[]{:S(2)}) collective-permute-start(bf16[3,512,640]{2,1,0:T(8,128)(2,1)S(1)} %get-tuple-element.78), channel_id=1, source_target_pairs={{0,16},{8,24},{16,32},{24,40},{32,48},{40,56},{48,64},{56,72},{64,... | collective-permute-start | bytes 5898248 | tf_op jit(solution)/shard_map/ppermute | solution.py:27
  35.8 5.1 %products.5 = (f32[2,6,64,512]{3,2,1,0:T(8,128)S(1)}, f32[6,64,512]{2,1,0:T(8,128)S(1)}, f32[6,64,512]{2,1,0:T(8,128)S(1)}, bf16[6,64,512]{2,1,0:T(8,128)(2,1)S(...) custom-call(s32[56]{0:T(128)S(1)} %make_table.1.refs_0_.table_ref, ...), custom_call_target="tpu_custom_call" | custom-call | flops 5750000128 | bytes 15000001 | tf_op jit(solution)/shard_map/products/pallas_call | solution.py:162
  40.9 1.6 %collective-permute-start.13 = (bf16[6,64,512]{2,1,0:T(8,128)(2,1)S(1)}, bf16[6,64,512]{2,1,0:T(8,128)(2,1)S(1)}, u32[]{:S(2)}, u32[]{:S(2)}) collective-permute-start(bf16[6,64,512]{2,1,0:T(8,128)(2,1)S(1)} %get-tuple-element.95), channel_id=1, source_target_pairs={{0,1},{1,2},{2,3},{3,0},{4,5},{5,6},{6,7},{7,4},{8,9},{9,10},{10,1... | collective-permute-start | bytes 1179656 | tf_op jit(solution)/shard_map/ppermute | solution.py:32
  42.6 1.7 %collective-permute-start.14 = (bf16[6,64,512]{2,1,0:T(8,128)(2,1)S(1)}, bf16[6,64,512]{2,1,0:T(8,128)(2,1)S(1)}, u32[]{:S(2)}, u32[]{:S(2)}) collective-permute-start(bf16[6,64,512]{2,1,0:T(8,128)(2,1)S(1)} %get-tuple-element.97), channel_id=1, source_target_pairs={{0,3},{1,0},{2,1},{3,2},{4,7},{5,4},{6,5},{7,6},{8,11},{9,8},{10,9... | collective-permute-start | bytes 1179656 | tf_op jit(solution)/shard_map/ppermute | solution.py:32
  44.2 0.4 collective-permute-start.6
  44.6 9.0 %collective-permute-done.13.up_got_ref = bf16[6,64,512]{2,1,0:T(8,128)(2,1)S(1)} collective-permute-done((bf16[6,64,512]{2,1,0:T(8,128)(2,1)S(1)}, bf16[6,64,512]{2,1,0:T(8,128)(2,1)S(1)}, u32[]{:S(2)}, u32[]{:S(2)}) %collective-permute-start.13) | collective-permute-done | bytes 393248 | tf_op jit(solution)/shard_map/ppermute | solution.py:32
  53.6 1.9 %collective-permute-start.7 = (bf16[2,6,64,512]{3,2,1,0:T(8,128)(2,1)S(1)}, bf16[2,6,64,512]{3,2,1,0:T(8,128)(2,1)S(1)}, u32[]{:S(2)}, u32[]{:S(2)}) collective-permute-start(bf16[2,6,64,512]{3,2,1,0:T(8,128)(2,1)S(1)} %get-tuple-element.75), channel_id=1, source_target_pairs={{0,3},{1,0},{2,1},{3,2},{4,7},{5,4},{6,5},{7,6},{8,11},{9,8},{10,9... | collective-permute-start | bytes 2359304 | tf_op jit(solution)/shard_map/ppermute | solution.py:32
  55.4 0.2 passed_on.5
  55.6 0.4 collective-permute-start.15
  56.0 14.4 %collective-permute-done.6.up_ref = bf16[2,6,64,512]{3,2,1,0:T(8,128)(2,1)S(1)} collective-permute-done((bf16[2,6,64,512]{3,2,1,0:T(8,128)(2,1)S(1)}, bf16[2,6,64,512]{3,2,1,0:T(8,128)(2,1)S(1)}, u32[]{:S(2)}, u32[]{:S(2)}) %collective-permute-start.6) | collective-permute-done | bytes 786464 | tf_op jit(solution)/shard_map/ppermute | solution.py:32
  70.4 1.9 %collective-permute-start.16 = (bf16[2,6,64,512]{3,2,1,0:T(8,128)(2,1)S(1)}, bf16[2,6,64,512]{3,2,1,0:T(8,128)(2,1)S(1)}, u32[]{:S(2)}, u32[]{:S(2)}) collective-permute-start(bf16[2,6,64,512]{3,2,1,0:T(8,128)(2,1)S(1)} %get-tuple-element.101), channel_id=1, source_target_pairs={{0,3},{1,0},{2,1},{3,2},{4,7},{5,4},{6,5},{7,6},{8,11},{9,8},{10,9... | collective-permute-start | bytes 2359304 | tf_op jit(solution)/shard_map/ppermute | solution.py:32
  72.3 1.4 collective-permute-done.7.down_ref
  73.7 1.0 plane_sums.5
  74.7 3.7 %collective-permute-start.18 = (bf16[6,64,512]{2,1,0:T(8,128)(2,1)S(1)}, bf16[6,64,512]{2,1,0:T(8,128)(2,1)S(1)}, u32[]{:S(2)}, u32[]{:S(2)}) collective-permute-start(bf16[6,64,512]{2,1,0:T(8,128)(2,1)S(1)} %get-tuple-element.105), channel_id=1, source_target_pairs={{0,4},{1,5},{2,6},{3,7},{4,0},{5,1},{6,2},{7,3},{8,12},{9,13},{10,... | collective-permute-start | bytes 1179656 | tf_op jit(solution)/shard_map/ppermute | solution.py:36
  78.4 0.0 collective-permute-done.4.refs_3_
  78.4 4.4 %collective-permute-done.5.refs_4_ = bf16[3,512,640]{2,1,0:T(8,128)(2,1)S(1)} collective-permute-done((bf16[3,512,640]{2,1,0:T(8,128)(2,1)S(1)}, bf16[3,512,640]{2,1,0:T(8,128)(2,1)S(1)}, u32[]{:S(2)}, u32[]{:S(2)}) %collective-permute-start.5) | collective-permute-done | bytes 1966112 | tf_op jit(solution)/shard_map/ppermute | solution.py:27
  82.8 5.8 %products.4 = (f32[2,6,64,512]{3,2,1,0:T(8,128)S(1)}, f32[6,64,512]{2,1,0:T(8,128)S(1)}, f32[6,64,512]{2,1,0:T(8,128)S(1)}, bf16[6,64,512]{2,1,0:T(8,128)(2,1)S(...) custom-call(s32[56]{0:T(128)S(1)} %make_table.1.refs_0_.table_ref, ...), custom_call_target="tpu_custom_call" | custom-call | flops 5750000128 | bytes 15000001 | tf_op jit(solution)/shard_map/products/pallas_call | solution.py:162
  88.6 1.1 copy-done.6
  89.7 1.6 collective-permute-start.8
  91.3 1.7 %collective-permute-start.9 = (bf16[6,64,512]{2,1,0:T(8,128)(2,1)S(1)}, bf16[6,64,512]{2,1,0:T(8,128)(2,1)S(1)}, u32[]{:S(2)}, u32[]{:S(2)}) collective-permute-start(bf16[6,64,512]{2,1,0:T(8,128)(2,1)S(1)} %get-tuple-element.86), channel_id=1, source_target_pairs={{0,3},{1,0},{2,1},{3,2},{4,7},{5,4},{6,5},{7,6},{8,11},{9,8},{10,9... | collective-permute-start | bytes 1179656 | tf_op jit(solution)/shard_map/ppermute | solution.py:32
  93.0 1.0 plane_sums.4
  94.0 3.7 %collective-permute-start.17 = (bf16[6,64,512]{2,1,0:T(8,128)(2,1)S(1)}, bf16[6,64,512]{2,1,0:T(8,128)(2,1)S(1)}, u32[]{:S(2)}, u32[]{:S(2)}) collective-permute-start(bf16[6,64,512]{2,1,0:T(8,128)(2,1)S(1)} %get-tuple-element.103), channel_id=1, source_target_pairs={{0,4},{1,5},{2,6},{3,7},{4,0},{5,1},{6,2},{7,3},{8,12},{9,13},{10,... | collective-permute-start | bytes 1179656 | tf_op jit(solution)/shard_map/ppermute | solution.py:36
  97.7 3.5 %collective-permute-done.8.up_got_ref = bf16[6,64,512]{2,1,0:T(8,128)(2,1)S(1)} collective-permute-done((bf16[6,64,512]{2,1,0:T(8,128)(2,1)S(1)}, bf16[6,64,512]{2,1,0:T(8,128)(2,1)S(1)}, u32[]{:S(2)}, u32[]{:S(2)}) %collective-permute-start.8) | collective-permute-done | bytes 393248 | tf_op jit(solution)/shard_map/ppermute | solution.py:32
  101.2 0.1 collective-permute-done.9.down_got_ref
  101.3 0.8 passed_on.4
  102.1 1.6 collective-permute-start.10
  103.7 1.7 %collective-permute-start.11 = (bf16[2,6,64,512]{3,2,1,0:T(8,128)(2,1)}, bf16[2,6,64,512]{3,2,1,0:T(8,128)(2,1)S(1)}, u32[]{:S(2)}, u32[]{:S(2)}) collective-permute-start(bf16[2,6,64,512]{3,2,1,0:T(8,128)(2,1)} %get-tuple-element.90), channel_id=1, source_target_pairs={{0,3},{1,0},{2,1},{3,2},{4,7},{5,4},{6,5},{7,6},{8,11},{9,8},{10,9... | collective-permute-start | bytes 2359304 | tf_op jit(solution)/shard_map/ppermute | solution.py:32
  105.3 3.2 %totals.3 = (f32[18,64,512]{2,1,0:T(8,128)}, bf16[8,12,32,128]{3,2,1,0:T(8,128)(2,1)}) custom-call(s32[56]{0:T(128)S(1)} %make_table.1.refs_0_.table_ref, f32[6,64,512]{2,1,0:T(8,128)S(1)} %get-tuple-element.104.refs_1_, bf16[6,64,512]{2,1,0:T(8,128)(2,1)S(1)} %collective-permute-done.18.refs_2_), custom_call_target="tpu_custom_call" | custom-call | flops 5750000128 | bytes 15000001 | tf_op jit(solution)/shard_map/totals/pallas_call | solution.py:290
  108.6 3.2 %totals.4 = (bf16[3,64,512]{2,1,0:T(8,128)(2,1)S(1)}, bf16[3,64,512]{2,1,0:T(8,128)(2,1)S(1)}, bf16[8,12,32,128]{3,2,1,0:T(8,128)(2,1)}) custom-call(s32[56]{0:T(128)S(1)} %make_table.1.refs_0_.table_ref, f32[6,64,512]{2,1,0:T(8,128)S(1)} %get-tuple-element.102.refs_1_, ...), custom_call_target="tpu_custom_call", output_to_operand_aliasing={{2}: (3, {})} | custom-call | flops 5750000128 | bytes 15000001 | tf_op jit(solution)/shard_map/totals/pallas_call | solution.py:290
  111.8 0.7 copy-done.3
  112.5 6.0 %all-to-all-start = ((bf16[8,12,32,128]{3,2,1,0:T(8,128)(2,1)}), bf16[8,12,32,128]{3,2,1,0:T(8,128)(2,1)S(1)}, u32[]{:S(2)}, u32[]{:S(2)}) async-start(bf16[8,12,32,128]{3,2,1,0:T(8,128)(2,1)} %get-tuple-element.107), calls=%async_computation | async-start | bytes 1572864 | tf_op jit(solution)/shard_map/all_to_all | solution.py:40
  118.5 0.5 collective-permute-start.20
  119.0 5.8 %collective-permute-done.10.up_ref = bf16[2,6,64,512]{3,2,1,0:T(8,128)(2,1)S(1)} collective-permute-done((bf16[2,6,64,512]{3,2,1,0:T(8,128)(2,1)S(1)}, bf16[2,6,64,512]{3,2,1,0:T(8,128)(2,1)S(1)}, u32[]{:S(2)}, u32[]{:S(2)}) %collective-permute-start.10) | collective-permute-done | bytes 786464 | tf_op jit(solution)/shard_map/ppermute | solution.py:32
  124.8 1.4 copy-done.7
  126.2 1.0 plane_sums.3
  127.3 0.9 copy-done.8
  128.2 4.5 %collective-permute-start.12 = (bf16[6,64,512]{2,1,0:T(8,128)(2,1)S(1)}, bf16[6,64,512]{2,1,0:T(8,128)(2,1)S(1)}, u32[]{:S(2)}, u32[]{:S(2)}) collective-permute-start(bf16[6,64,512]{2,1,0:T(8,128)(2,1)S(1)} %get-tuple-element.92), channel_id=1, source_target_pairs={{0,4},{1,5},{2,6},{3,7},{4,0},{5,1},{6,2},{7,3},{8,12},{9,13},{10,... | collective-permute-start | bytes 1179656 | tf_op jit(solution)/shard_map/ppermute | solution.py:36
  132.7 0.7 copy-done.1
  133.3 0.9 copy-done.2
  134.3 2.1 %finish.2 = (f32[18,64,512]{2,1,0:T(8,128)}, f32[18,64,512]{2,1,0:T(8,128)}) custom-call(s32[56]{0:T(128)S(1)} %make_table.1.refs_0_.table_ref, bf16[8,12,32,128]{3,2,1,0:T(8,128)(2,1)S(1)} %all-to-all-done.refs_1_, bf16[3,64,512]{2,1,0:T(8,128)(2,1)S(1)} %collective-permute-done.19.refs_2_, ...), custom_call_target="tpu_custom_call", output_to_operand_aliasing={{0}: (4, {})} | custom-call | flops 5750000128 | bytes 15000001 | tf_op jit(solution)/shard_map/finish/pallas_call | solution.py:339
  136.4 4.4 %collective-permute-done.12.refs_2_ = bf16[6,64,512]{2,1,0:T(8,128)(2,1)S(1)} collective-permute-done((bf16[6,64,512]{2,1,0:T(8,128)(2,1)S(1)}, bf16[6,64,512]{2,1,0:T(8,128)(2,1)S(1)}, u32[]{:S(2)}, u32[]{:S(2)}) %collective-permute-start.12) | collective-permute-done | bytes 393248 | tf_op jit(solution)/shard_map/ppermute | solution.py:36
  140.8 3.2 %totals.5 = (bf16[3,64,512]{2,1,0:T(8,128)(2,1)S(1)}, bf16[3,64,512]{2,1,0:T(8,128)(2,1)S(1)}, bf16[8,6,32,128]{3,2,1,0:T(8,128)(2,1)}) custom-call(s32[56]{0:T(128)S(1)} %make_table.1.refs_0_.table_ref, f32[6,64,512]{2,1,0:T(8,128)S(1)} %copy-done.9, bf16[6,64,512]{2,1,0:T(8,128)(2,1)S(1)} %collective-permute-done.12.refs_2_), custom_call_target="tpu_custom_call" | custom-call | flops 5750000128 | bytes 15000001 | tf_op jit(solution)/shard_map/totals/pallas_call | solution.py:290
  144.0 4.3 %all-to-all-start.1 = ((bf16[8,6,32,128]{3,2,1,0:T(8,128)(2,1)}), bf16[8,6,32,128]{3,2,1,0:T(8,128)(2,1)S(1)}, u32[]{:S(2)}, u32[]{:S(2)}) async-start(bf16[8,6,32,128]{3,2,1,0:T(8,128)(2,1)} %get-tuple-element.114), calls=%async_computation.1 | async-start | bytes 786432 | tf_op jit(solution)/shard_map/all_to_all | solution.py:40
  148.2 0.8 collective-permute-start.21
  149.1 3.3 %collective-permute-start.22 = (bf16[3,64,512]{2,1,0:T(8,128)(2,1)S(1)}, bf16[3,64,512]{2,1,0:T(8,128)(2,1)S(1)}, u32[]{:S(2)}, u32[]{:S(2)}) collective-permute-start(bf16[3,64,512]{2,1,0:T(8,128)(2,1)S(1)} %get-tuple-element.116), channel_id=1, source_target_pairs={{0,16},{8,24},{16,32},{24,40},{32,48},{40,56},{48,64},{56,72},{64,... | collective-permute-start | bytes 589832 | tf_op jit(solution)/shard_map/ppermute | solution.py:27
  152.4 4.8 %collective-permute-done.21.refs_2_ = bf16[3,64,512]{2,1,0:T(8,128)(2,1)S(1)} collective-permute-done((bf16[3,64,512]{2,1,0:T(8,128)(2,1)S(1)}, bf16[3,64,512]{2,1,0:T(8,128)(2,1)S(1)}, u32[]{:S(2)}, u32[]{:S(2)}) %collective-permute-start.21) | collective-permute-done | bytes 196640 | tf_op jit(solution)/shard_map/ppermute | solution.py:27
  157.2 3.0 %all-to-all-done.1.refs_1_ = bf16[8,6,32,128]{3,2,1,0:T(8,128)(2,1)S(1)} async-done(((bf16[8,6,32,128]{3,2,1,0:T(8,128)(2,1)}), bf16[8,6,32,128]{3,2,1,0:T(8,128)(2,1)S(1)}, u32[]{:S(2)}, u32[]{:S(2)}) %all-to-all-start.1) | async-done | bytes 393248 | tf_op jit(solution)/shard_map/all_to_all | solution.py:40
  160.2 1.8 %finish.3 = (f32[18,64,512]{2,1,0:T(8,128)}, f32[18,64,512]{2,1,0:T(8,128)}) custom-call(s32[56]{0:T(128)S(1)} %make_table.1.refs_0_.table_ref, bf16[8,6,32,128]{3,2,1,0:T(8,128)(2,1)S(1)} %all-to-all-done.1.refs_1_, bf16[3,64,512]{2,1,0:T(8,128)(2,1)S(1)} %collective-permute-done.21.refs_2_, ...), custom_call_target="tpu_custom_call", output_to_operand_aliasing={{0}: (4, {}), {1}: (5, {})} | custom-call | flops 5750000128 | bytes 15000001 | tf_op jit(solution)/shard_map/finish/pallas_call | solution.py:339
  (27 shorter events, 0.1 us)
Async XLA Ops:
  0.7 0.7 copy-start.4
  1.4 0.7 copy-start.5
  2.0 2.5 %copy-start = (bf16[4096,640]{1,0:T(8,128)(2,1)S(1)}, bf16[4096,640]{1,0:T(8,128)(2,1)}, u32[]{:S(2)}) copy-start(bf16[4096,640]{1,0:T(8,128)(2,1)} %param.4) | copy-start | bytes 15728644
  4.5 5.0 %copy-start.10 = (f32[640]{0:T(1024)S(1)}, f32[640]{0:T(1024)}, u32[]{:S(2)}) copy-start(f32[640]{0:T(1024)} %param.5) | copy-start | bytes 7684
  7.7 24.1 %collective-permute-start = (bf16[3,512,640]{2,1,0:T(8,128)(2,1)S(1)}, bf16[3,512,640]{2,1,0:T(8,128)(2,1)S(1)}, u32[]{:S(2)}, u32[]{:S(2)}) collective-permute-start(bf16[3,512,640]{2,1,0:T(8,128)(2,1)S(1)} %get-tuple-element.61), channel_id=1, source_target_pairs={{0,8},{8,16},{16,24},{24,32},{32,40},{40,48},{48,56},{56,64},{64,7... | collective-permute-start | bytes 5898248 | tf_op jit(solution)/shard_map/ppermute | solution.py:27
  7.8 24.0 %collective-permute-start.1 = (bf16[3,512,640]{2,1,0:T(8,128)(2,1)S(1)}, bf16[3,512,640]{2,1,0:T(8,128)(2,1)S(1)}, u32[]{:S(2)}, u32[]{:S(2)}) collective-permute-start(bf16[3,512,640]{2,1,0:T(8,128)(2,1)S(1)} %get-tuple-element.62), channel_id=1, source_target_pairs={{0,120},{8,0},{16,8},{24,16},{32,24},{40,32},{48,40},{56,48},{64,5... | collective-permute-start | bytes 5898248 | tf_op jit(solution)/shard_map/ppermute | solution.py:27
  14.6 12.6 %collective-permute-start.2 = (bf16[6,64,512]{2,1,0:T(8,128)(2,1)S(1)}, bf16[6,64,512]{2,1,0:T(8,128)(2,1)S(1)}, u32[]{:S(2)}, u32[]{:S(2)}) collective-permute-start(bf16[6,64,512]{2,1,0:T(8,128)(2,1)S(1)} %get-tuple-element.69), channel_id=1, source_target_pairs={{0,1},{1,2},{2,3},{3,0},{4,5},{5,6},{6,7},{7,4},{8,9},{9,10},{10,1... | collective-permute-start | bytes 1179656 | tf_op jit(solution)/shard_map/ppermute | solution.py:32
  16.2 11.0 %collective-permute-start.3 = (bf16[6,64,512]{2,1,0:T(8,128)(2,1)S(1)}, bf16[6,64,512]{2,1,0:T(8,128)(2,1)S(1)}, u32[]{:S(2)}, u32[]{:S(2)}) collective-permute-start(bf16[6,64,512]{2,1,0:T(8,128)(2,1)S(1)} %get-tuple-element.71), channel_id=1, source_target_pairs={{0,3},{1,0},{2,1},{3,2},{4,7},{5,4},{6,5},{7,6},{8,11},{9,8},{10,9... | collective-permute-start | bytes 1179656 | tf_op jit(solution)/shard_map/ppermute | solution.py:32
  31.8 46.6 %collective-permute-start.4 = (bf16[3,512,640]{2,1,0:T(8,128)(2,1)S(1)}, bf16[3,512,640]{2,1,0:T(8,128)(2,1)S(1)}, u32[]{:S(2)}, u32[]{:S(2)}) collective-permute-start(bf16[3,512,640]{2,1,0:T(8,128)(2,1)S(1)} %get-tuple-element.78), channel_id=1, source_target_pairs={{0,16},{8,24},{16,32},{24,40},{32,48},{40,56},{48,64},{56,72},{64,... | collective-permute-start | bytes 5898248 | tf_op jit(solution)/shard_map/ppermute | solution.py:27
  35.8 47.0 %collective-permute-start.5 = (bf16[3,512,640]{2,1,0:T(8,128)(2,1)S(1)}, bf16[3,512,640]{2,1,0:T(8,128)(2,1)S(1)}, u32[]{:S(2)}, u32[]{:S(2)}) collective-permute-start(bf16[3,512,640]{2,1,0:T(8,128)(2,1)S(1)} %get-tuple-element.79), channel_id=1, source_target_pairs={{0,112},{8,120},{16,0},{24,8},{32,16},{40,24},{48,32},{56,40},{64,... | collective-permute-start | bytes 5898248 | tf_op jit(solution)/shard_map/ppermute | solution.py:27
  40.9 12.6 %collective-permute-start.13 = (bf16[6,64,512]{2,1,0:T(8,128)(2,1)S(1)}, bf16[6,64,512]{2,1,0:T(8,128)(2,1)S(1)}, u32[]{:S(2)}, u32[]{:S(2)}) collective-permute-start(bf16[6,64,512]{2,1,0:T(8,128)(2,1)S(1)} %get-tuple-element.95), channel_id=1, source_target_pairs={{0,1},{1,2},{2,3},{3,0},{4,5},{5,6},{6,7},{7,4},{8,9},{9,10},{10,1... | collective-permute-start | bytes 1179656 | tf_op jit(solution)/shard_map/ppermute | solution.py:32
  42.6 12.9 %collective-permute-start.14 = (bf16[6,64,512]{2,1,0:T(8,128)(2,1)S(1)}, bf16[6,64,512]{2,1,0:T(8,128)(2,1)S(1)}, u32[]{:S(2)}, u32[]{:S(2)}) collective-permute-start(bf16[6,64,512]{2,1,0:T(8,128)(2,1)S(1)} %get-tuple-element.97), channel_id=1, source_target_pairs={{0,3},{1,0},{2,1},{3,2},{4,7},{5,4},{6,5},{7,6},{8,11},{9,8},{10,9... | collective-permute-start | bytes 1179656 | tf_op jit(solution)/shard_map/ppermute | solution.py:32
  44.2 26.2 %collective-permute-start.6 = (bf16[2,6,64,512]{3,2,1,0:T(8,128)(2,1)S(1)}, bf16[2,6,64,512]{3,2,1,0:T(8,128)(2,1)S(1)}, u32[]{:S(2)}, u32[]{:S(2)}) collective-permute-start(bf16[2,6,64,512]{3,2,1,0:T(8,128)(2,1)S(1)} %get-tuple-element.74), channel_id=1, source_target_pairs={{0,1},{1,2},{2,3},{3,0},{4,5},{5,6},{6,7},{7,4},{8,9},{9,10},{10,1... | collective-permute-start | bytes 2359304 | tf_op jit(solution)/shard_map/ppermute | solution.py:32
  53.6 20.1 %collective-permute-start.7 = (bf16[2,6,64,512]{3,2,1,0:T(8,128)(2,1)S(1)}, bf16[2,6,64,512]{3,2,1,0:T(8,128)(2,1)S(1)}, u32[]{:S(2)}, u32[]{:S(2)}) collective-permute-start(bf16[2,6,64,512]{3,2,1,0:T(8,128)(2,1)S(1)} %get-tuple-element.75), channel_id=1, source_target_pairs={{0,3},{1,0},{2,1},{3,2},{4,7},{5,4},{6,5},{7,6},{8,11},{9,8},{10,9... | collective-permute-start | bytes 2359304 | tf_op jit(solution)/shard_map/ppermute | solution.py:32
  55.6 37.4 %collective-permute-start.15 = (bf16[2,6,64,512]{3,2,1,0:T(8,128)(2,1)S(1)}, bf16[2,6,64,512]{3,2,1,0:T(8,128)(2,1)S(1)}, u32[]{:S(2)}, u32[]{:S(2)}) collective-permute-start(bf16[2,6,64,512]{3,2,1,0:T(8,128)(2,1)S(1)} %get-tuple-element.100), channel_id=1, source_target_pairs={{0,1},{1,2},{2,3},{3,0},{4,5},{5,6},{6,7},{7,4},{8,9},{9,10},{10,1... | collective-permute-start | bytes 2359304 | tf_op jit(solution)/shard_map/ppermute | solution.py:32
  70.4 22.6 %collective-permute-start.16 = (bf16[2,6,64,512]{3,2,1,0:T(8,128)(2,1)S(1)}, bf16[2,6,64,512]{3,2,1,0:T(8,128)(2,1)S(1)}, u32[]{:S(2)}, u32[]{:S(2)}) collective-permute-start(bf16[2,6,64,512]{3,2,1,0:T(8,128)(2,1)S(1)} %get-tuple-element.101), channel_id=1, source_target_pairs={{0,3},{1,0},{2,1},{3,2},{4,7},{5,4},{6,5},{7,6},{8,11},{9,8},{10,9... | collective-permute-start | bytes 2359304 | tf_op jit(solution)/shard_map/ppermute | solution.py:32
  74.7 30.6 %collective-permute-start.18 = (bf16[6,64,512]{2,1,0:T(8,128)(2,1)S(1)}, bf16[6,64,512]{2,1,0:T(8,128)(2,1)S(1)}, u32[]{:S(2)}, u32[]{:S(2)}) collective-permute-start(bf16[6,64,512]{2,1,0:T(8,128)(2,1)S(1)} %get-tuple-element.105), channel_id=1, source_target_pairs={{0,4},{1,5},{2,6},{3,7},{4,0},{5,1},{6,2},{7,3},{8,12},{9,13},{10,... | collective-permute-start | bytes 1179656 | tf_op jit(solution)/shard_map/ppermute | solution.py:36
  88.6 1.1 copy-start.6
  89.7 11.5 %collective-permute-start.8 = (bf16[6,64,512]{2,1,0:T(8,128)(2,1)S(1)}, bf16[6,64,512]{2,1,0:T(8,128)(2,1)S(1)}, u32[]{:S(2)}, u32[]{:S(2)}) collective-permute-start(bf16[6,64,512]{2,1,0:T(8,128)(2,1)S(1)} %get-tuple-element.84), channel_id=1, source_target_pairs={{0,1},{1,2},{2,3},{3,0},{4,5},{5,6},{6,7},{7,4},{8,9},{9,10},{10,1... | collective-permute-start | bytes 1179656 | tf_op jit(solution)/shard_map/ppermute | solution.py:32
  91.3 10.0 %collective-permute-start.9 = (bf16[6,64,512]{2,1,0:T(8,128)(2,1)S(1)}, bf16[6,64,512]{2,1,0:T(8,128)(2,1)S(1)}, u32[]{:S(2)}, u32[]{:S(2)}) collective-permute-start(bf16[6,64,512]{2,1,0:T(8,128)(2,1)S(1)} %get-tuple-element.86), channel_id=1, source_target_pairs={{0,3},{1,0},{2,1},{3,2},{4,7},{5,4},{6,5},{7,6},{8,11},{9,8},{10,9... | collective-permute-start | bytes 1179656 | tf_op jit(solution)/shard_map/ppermute | solution.py:32
  94.0 14.5 %collective-permute-start.17 = (bf16[6,64,512]{2,1,0:T(8,128)(2,1)S(1)}, bf16[6,64,512]{2,1,0:T(8,128)(2,1)S(1)}, u32[]{:S(2)}, u32[]{:S(2)}) collective-permute-start(bf16[6,64,512]{2,1,0:T(8,128)(2,1)S(1)} %get-tuple-element.103), channel_id=1, source_target_pairs={{0,4},{1,5},{2,6},{3,7},{4,0},{5,1},{6,2},{7,3},{8,12},{9,13},{10,... | collective-permute-start | bytes 1179656 | tf_op jit(solution)/shard_map/ppermute | solution.py:36
  102.1 22.7 %collective-permute-start.10 = (bf16[2,6,64,512]{3,2,1,0:T(8,128)(2,1)S(1)}, bf16[2,6,64,512]{3,2,1,0:T(8,128)(2,1)S(1)}, u32[]{:S(2)}, u32[]{:S(2)}) collective-permute-start(bf16[2,6,64,512]{3,2,1,0:T(8,128)(2,1)S(1)} %get-tuple-element.89), channel_id=1, source_target_pairs={{0,1},{1,2},{2,3},{3,0},{4,5},{5,6},{6,7},{7,4},{8,9},{9,10},{10,1... | collective-permute-start | bytes 2359304 | tf_op jit(solution)/shard_map/ppermute | solution.py:32
  103.7 21.2 %collective-permute-start.11 = (bf16[2,6,64,512]{3,2,1,0:T(8,128)(2,1)}, bf16[2,6,64,512]{3,2,1,0:T(8,128)(2,1)S(1)}, u32[]{:S(2)}, u32[]{:S(2)}) collective-permute-start(bf16[2,6,64,512]{3,2,1,0:T(8,128)(2,1)} %get-tuple-element.90), channel_id=1, source_target_pairs={{0,3},{1,0},{2,1},{3,2},{4,7},{5,4},{6,5},{7,6},{8,11},{9,8},{10,9... | collective-permute-start | bytes 2359304 | tf_op jit(solution)/shard_map/ppermute | solution.py:32
  111.8 0.7 copy-start.3
  112.5 20.9 %all-to-all-start = ((bf16[8,12,32,128]{3,2,1,0:T(8,128)(2,1)}), bf16[8,12,32,128]{3,2,1,0:T(8,128)(2,1)S(1)}, u32[]{:S(2)}, u32[]{:S(2)}) async-start(bf16[8,12,32,128]{3,2,1,0:T(8,128)(2,1)} %get-tuple-element.107), calls=%async_computation | async-start | bytes 1572864 | tf_op jit(solution)/shard_map/all_to_all | solution.py:40
  118.5 14.2 %collective-permute-start.19 = (bf16[3,64,512]{2,1,0:T(8,128)(2,1)}, bf16[3,64,512]{2,1,0:T(8,128)(2,1)S(1)}, u32[]{:S(2)}, u32[]{:S(2)}) collective-permute-start(bf16[3,64,512]{2,1,0:T(8,128)(2,1)} %copy-done.3), channel_id=1, source_target_pairs={{0,120},{8,0},{16,8},{24,16},{32,24},{40,32},{48,40},{56,48},{64,5... | collective-permute-start | bytes 589832 | tf_op jit(solution)/shard_map/ppermute | solution.py:27
  118.5 14.2 %collective-permute-start.20 = (bf16[3,64,512]{2,1,0:T(8,128)(2,1)S(1)}, bf16[3,64,512]{2,1,0:T(8,128)(2,1)S(1)}, u32[]{:S(2)}, u32[]{:S(2)}) collective-permute-start(bf16[3,64,512]{2,1,0:T(8,128)(2,1)S(1)} %get-tuple-element.109), channel_id=1, source_target_pairs={{0,8},{8,16},{16,24},{24,32},{32,40},{40,48},{48,56},{56,64},{64,7... | collective-permute-start | bytes 589832 | tf_op jit(solution)/shard_map/ppermute | solution.py:27
  124.8 1.4 copy-start.7
  127.3 0.9 copy-start.8
  128.2 12.6 %collective-permute-start.12 = (bf16[6,64,512]{2,1,0:T(8,128)(2,1)S(1)}, bf16[6,64,512]{2,1,0:T(8,128)(2,1)S(1)}, u32[]{:S(2)}, u32[]{:S(2)}) collective-permute-start(bf16[6,64,512]{2,1,0:T(8,128)(2,1)S(1)} %get-tuple-element.92), channel_id=1, source_target_pairs={{0,4},{1,5},{2,6},{3,7},{4,0},{5,1},{6,2},{7,3},{8,12},{9,13},{10,... | collective-permute-start | bytes 1179656 | tf_op jit(solution)/shard_map/ppermute | solution.py:36
  132.7 0.7 copy-start.1
  133.3 0.9 copy-start.2
  134.3 6.5 %copy-start.9 = (f32[6,64,512]{2,1,0:T(8,128)S(1)}, f32[6,64,512]{2,1,0:T(8,128)}, u32[]{:S(2)}) copy-start(f32[6,64,512]{2,1,0:T(8,128)} %copy-done.8) | copy-start | bytes 2359300
  144.0 16.3 %all-to-all-start.1 = ((bf16[8,6,32,128]{3,2,1,0:T(8,128)(2,1)}), bf16[8,6,32,128]{3,2,1,0:T(8,128)(2,1)S(1)}, u32[]{:S(2)}, u32[]{:S(2)}) async-start(bf16[8,6,32,128]{3,2,1,0:T(8,128)(2,1)} %get-tuple-element.114), calls=%async_computation.1 | async-start | bytes 786432 | tf_op jit(solution)/shard_map/all_to_all | solution.py:40
  148.2 9.0 %collective-permute-start.21 = (bf16[3,64,512]{2,1,0:T(8,128)(2,1)S(1)}, bf16[3,64,512]{2,1,0:T(8,128)(2,1)S(1)}, u32[]{:S(2)}, u32[]{:S(2)}) collective-permute-start(bf16[3,64,512]{2,1,0:T(8,128)(2,1)S(1)} %get-tuple-element.115), channel_id=1, source_target_pairs={{0,112},{8,120},{16,0},{24,8},{32,16},{40,24},{48,32},{56,40},{64,... | collective-permute-start | bytes 589832 | tf_op jit(solution)/shard_map/ppermute | solution.py:27
  149.1 8.1 %collective-permute-start.22 = (bf16[3,64,512]{2,1,0:T(8,128)(2,1)S(1)}, bf16[3,64,512]{2,1,0:T(8,128)(2,1)S(1)}, u32[]{:S(2)}, u32[]{:S(2)}) collective-permute-start(bf16[3,64,512]{2,1,0:T(8,128)(2,1)S(1)} %get-tuple-element.116), channel_id=1, source_target_pairs={{0,16},{8,24},{16,32},{24,40},{32,48},{40,56},{48,64},{56,72},{64,... | collective-permute-start | bytes 589832 | tf_op jit(solution)/shard_map/ppermute | solution.py:27

commit v4 on v3

v4 whole, which is shorter than its diff:
```python
import jax
import jax.numpy as jnp
from jax import lax
from jax.experimental import pallas as pl
from jax.experimental.pallas import tpu as pltpu
from jax.sharding import PartitionSpec as P

BLK = 512
SPAN = 2
MULT = 3
STORED = 8
LISTED = 18
LOCAL = 6
NTRANS = 16
NPW = 8
NY = 4
NZ = 2
ROWS = BLK // NPW
RUNS = ((0, 6), (1, 3), (-1, 3), (2, 2), (-2, 2), (2, 1), (-2, 1))
NEAR_AT, FAR_AT, LAST_AT = 6, 12, 16
RESULTS = ((0, 1, 2, 3, 4, 5), (6, 7, 8), (9, 10, 11), (12, 13, 16), (14, 15, 17))
ORDER, FIRST, SECOND, YAT, ZAT, TABLE = 0, LISTED, 2 * LISTED, 3 * LISTED, 3 * LISTED + 1, 3 * LISTED + 2
VMEM_BYTES = 24 * 2**20


def shifted(value, steps):
    pairs = [(source, (source + steps) % NTRANS) for source in range(NTRANS)]
    return lax.ppermute(value, "trans", pairs)


def along_y(value, steps):
    pairs = [(z * NY + y, z * NY + (y + steps) % NY) for z in range(NZ) for y in range(NY)]
    return lax.ppermute(value, "pw", pairs)


def across_z(value):
    return lax.ppermute(value, "pw", [(source, (source + NY) % NPW) for source in range(NPW)])


def exchanged(value):
    return lax.all_to_all(value, "pw", split_axis=0, concat_axis=0, tiled=True)


def params():
    return pltpu.CompilerParams(vmem_limit_bytes=VMEM_BYTES)


def table_kernel(place_ref, pairs_ref, owner_ref, table_ref):
    device = place_ref[0]
    table_ref[YAT] = place_ref[1] & (NY - 1)
    table_ref[ZAT] = place_ref[1] >> 2
    places, at = {}, 0
    for step, count in RUNS:
        places.setdefault(step, []).extend(range(at, at + count))
        at += count
    filled = {step: jnp.int32(0) for step in places}
    for q in range(LISTED):
        pair = device * LISTED + q
        first = owner_ref[pairs_ref[0, pair]]
        second = owner_ref[pairs_ref[1, pair]]
        distance = (((second >> 3) - device + SPAN + NTRANS) & (NTRANS - 1)) - SPAN
        place = jnp.int32(0)
        for step, slots in places.items():
            here = distance == step
            for number, slot in enumerate(slots):
                place = jnp.where(here & (filled[step] == number), slot, place)
            filled[step] = jnp.where(here, filled[step] + 1, filled[step])
        source = (device - distance + NTRANS) & (NTRANS - 1)
        table_ref[ORDER + place] = jnp.int32(q)
        table_ref[FIRST + place] = first & (STORED - 1)
        table_ref[SECOND + place] = owner_ref[pairs_ref[1, source * LISTED + q]] & (STORED - 1)


def make_table(place, pairs, owner):
    smem = pl.BlockSpec(memory_space=pltpu.SMEM)
    return pl.pallas_call(
        table_kernel,
        out_shape=jax.ShapeDtypeStruct((TABLE,), jnp.int32),
        in_specs=[smem, smem, smem],
        out_specs=smem,
        compiler_params=params(),
        cost_estimate=pl.CostEstimate(flops=115000001, bytes_accessed=300001, transcendentals=0),
        name="make_table",
    )(place, pairs, owner)


def select_kernel(start, each, table_ref, blocks_ref, *rest):
    sends, (held, in_sems, out_sems) = rest[:2], rest[2:]
    loads, stores = [], []
    for at, send in enumerate(sends):
        for j in range(each):
            n = at * each + j
            slot = table_ref[FIRST + start + n]
            loads.append(pltpu.make_async_copy(blocks_ref.at[slot], held.at[n], in_sems.at[n]))
            stores.append(pltpu.make_async_copy(held.at[n], send.at[j], out_sems.at[n]))
            loads[-1].start()
    for load, store in zip(loads, stores):
        load.wait()
        store.start()
    for store in stores:
        store.wait()


def select(start, each, table, blocks):
    width = blocks.shape[2]
    count = 2 * each
    anywhere = pl.BlockSpec(memory_space=pl.ANY)
    return pl.pallas_call(
        lambda *refs: select_kernel(start, each, *refs),
        out_shape=[jax.ShapeDtypeStruct((each, BLK, width), jnp.bfloat16)] * 2,
        in_specs=[pl.BlockSpec(memory_space=pltpu.SMEM), pl.BlockSpec(memory_space=pltpu.HBM)],
        out_specs=[anywhere] * 2,
        scratch_shapes=[
            pltpu.VMEM((count, BLK, width), jnp.bfloat16),
            pltpu.SemaphoreType.DMA((count,)),
            pltpu.SemaphoreType.DMA((count,)),
        ],
        compiler_params=params(),
        cost_estimate=pl.CostEstimate(flops=115000001, bytes_accessed=300001, transcendentals=0),
        name="select",
    )(table, blocks)


def products_kernel(count, table_ref, right_ref, coulomb_ref, *refs):
    lefts, (own_ref, up_add_ref, down_add_ref, up_ref, down_ref, weighted_ref) = refs[:-6], refs[-6:]
    each = count // len(lefts)
    y = table_ref[YAT]
    for at, left_ref in enumerate(lefts):

        @pl.when(pl.program_id(0) // each == at)
        def _():
            for dy in range(NY):
                for z in range(NZ):
                    to = (dy * NZ + z) * ROWS
                    source = z * (NY * ROWS) + ((y + dy) & (NY - 1)) * ROWS
                    rows = left_ref[0, pl.ds(pl.multiple_of(source, ROWS), ROWS), :]
                    weighted_ref[to : to + ROWS, :] = (rows.astype(jnp.float32) * coulomb_ref[...]).astype(jnp.bfloat16)

    part = lax.dot_general(
        weighted_ref[...], right_ref[0], (((1,), (1,)), ((), ())), preferred_element_type=jnp.float32
    ).reshape(NY, NZ, 1, ROWS, BLK)
    own_ref[...] = part[0]
    up_add_ref[...] = part[1, 0]
    up_ref[0] = part[2, 0].astype(jnp.bfloat16)
    up_ref[1] = part[1, 1].astype(jnp.bfloat16)
    down_ref[0] = part[3, 0].astype(jnp.bfloat16)
    down_ref[1] = part[2, 1].astype(jnp.bfloat16)
    down_add_ref[...] = part[3, 1]


def products(table, blocks, coulomb, lefts, start, count):
    width = blocks.shape[2]
    each = count // len(lefts)
    if lefts[0].shape[0] == STORED:
        left_specs = [pl.BlockSpec((1, BLK, width), lambda i, table: (table[FIRST + start + i], 0, 0))]
    else:
        left_specs = [
            pl.BlockSpec((1, BLK, width), lambda i, table, at=at: (jnp.clip(i - at * each, 0, each - 1), 0, 0))
            for at in range(len(lefts))
        ]
    half = (count, ROWS, BLK)
    half_spec = pl.BlockSpec((1, ROWS, BLK), lambda i, table: (i, 0, 0))
    whole = (NZ, count, ROWS, BLK)
    whole_spec = pl.BlockSpec((NZ, 1, ROWS, BLK), lambda i, table: (0, i, 0, 0))
    return pl.pallas_call(
        lambda *refs: products_kernel(count, *refs),
        out_shape=[
            jax.ShapeDtypeStruct(whole, jnp.float32),
            jax.ShapeDtypeStruct(half, jnp.float32),
            jax.ShapeDtypeStruct(half, jnp.float32),
            jax.ShapeDtypeStruct(whole, jnp.bfloat16),
            jax.ShapeDtypeStruct(whole, jnp.bfloat16),
        ],
        grid_spec=pltpu.PrefetchScalarGridSpec(
            num_scalar_prefetch=1,
            grid=(count,),
            in_specs=[
                pl.BlockSpec((1, BLK, width), lambda i, table: (table[SECOND + start + i], 0, 0)),
                pl.BlockSpec((1, width), lambda i, table: (0, 0)),
                *left_specs,
            ],
            out_specs=[whole_spec, half_spec, half_spec, whole_spec, whole_spec],
            scratch_shapes=[pltpu.VMEM((BLK, width), jnp.bfloat16)],
        ),
        compiler_params=params(),
        cost_estimate=pl.CostEstimate(flops=115000001, bytes_accessed=300001, transcendentals=0),
        name="products",
    )(table, blocks, coulomb, *lefts)


def passed_kernel(up_add_ref, down_add_ref, up_got_ref, down_got_ref, up_ref, down_ref):
    up_ref[...] = (up_add_ref[...] + up_got_ref[0].astype(jnp.float32)).astype(jnp.bfloat16)
    down_ref[...] = (down_add_ref[...] + down_got_ref[0].astype(jnp.float32)).astype(jnp.bfloat16)


def passed_on(up_add, down_add, up_got, down_got):
    count = up_add.shape[0]
    block = (count // 2, ROWS, BLK)
    half = pl.BlockSpec(block, lambda i: (i, 0, 0))
    return pl.pallas_call(
        passed_kernel,
        out_shape=[jax.ShapeDtypeStruct(up_add.shape, jnp.bfloat16)] * 2,
        grid=(2,),
        in_specs=[
            half,
            half,
            pl.BlockSpec((1, *block), lambda i: (0, i, 0, 0)),
            pl.BlockSpec((1, *block), lambda i: (1, i, 0, 0)),
        ],
        out_specs=[half, half],
        compiler_params=params(),
        cost_estimate=pl.CostEstimate(flops=115000001, bytes_accessed=300001, transcendentals=0),
        name="passed_on",
    )(up_add, down_add, up_got, down_got)


def plane_kernel(begins, table_ref, *refs):
    parts, (keep_ref, give_ref) = refs[:-2], refs[-2:]
    z, i = table_ref[ZAT], pl.program_id(0)
    for at in range(len(begins) - 1):
        own_ref, up_ref, down_ref, up_sum_ref, down_sum_ref = parts[5 * at : 5 * at + 5]

        @pl.when((i >= begins[at]) & (i < begins[at + 1]))
        def _():
            low = own_ref[0] + down_ref[0].astype(jnp.float32) + up_sum_ref[...].astype(jnp.float32)
            high = own_ref[1] + up_ref[0].astype(jnp.float32) + down_sum_ref[...].astype(jnp.float32)
            keep_ref[...] = jnp.where(z == 0, low, high)
            give_ref[...] = jnp.where(z == 0, high, low).astype(jnp.bfloat16)


def plane_sums(table, groups, each):
    begins = [0]
    for group in groups:
        begins.append(begins[-1] + group[0].shape[1] // each)
    in_specs = []
    for lo, hi in zip(begins, begins[1:]):

        def at(i, lo=lo, hi=hi):
            return jnp.clip(i - lo, 0, hi - lo - 1)

        in_specs += [
            pl.BlockSpec((NZ, each, ROWS, BLK), lambda i, table, at=at: (0, at(i), 0, 0)),
            pl.BlockSpec((1, each, ROWS, BLK), lambda i, table, at=at: (1, at(i), 0, 0)),
            pl.BlockSpec((1, each, ROWS, BLK), lambda i, table, at=at: (0, at(i), 0, 0)),
            pl.BlockSpec((each, ROWS, BLK), lambda i, table, at=at: (at(i), 0, 0)),
            pl.BlockSpec((each, ROWS, BLK), lambda i, table, at=at: (at(i), 0, 0)),
        ]
    return pl.pallas_call(
        lambda *refs: plane_kernel(begins, *refs),
        out_shape=[
            jax.ShapeDtypeStruct((begins[-1] * each, ROWS, BLK), jnp.float32),
            jax.ShapeDtypeStruct((begins[-1] * each, ROWS, BLK), jnp.bfloat16),
        ],
        grid_spec=pltpu.PrefetchScalarGridSpec(
            num_scalar_prefetch=1,
            grid=(begins[-1],),
            in_specs=in_specs,
            out_specs=[pl.BlockSpec((each, ROWS, BLK), lambda i, table: (i, 0, 0))] * 2,
        ),
        compiler_params=params(),
        cost_estimate=pl.CostEstimate(flops=115000001, bytes_accessed=300001, transcendentals=0),
        name="plane_sums",
    )(table, *[part for group in groups for part in group])


def totals_kernel(at, outs, keep_ref, got_ref, *refs):
    cut_ref = refs[-1]
    total = keep_ref[...] + got_ref[...].astype(jnp.float32)
    columns = jnp.transpose(total.reshape(2 * ROWS, BLK), (1, 0)).astype(cut_ref.dtype)
    for target in range(NPW):
        cut_ref[target, 0] = columns[target * ROWS : (target + 1) * ROWS]
    for places, out_ref in zip(outs, refs[-1 - len(outs) : -1]):
        for slot, place in enumerate(places):

            @pl.when(pl.program_id(0) == (place - at) // 2)
            def _():
                out_ref[slot] = total[(place - at) % 2].astype(out_ref.dtype)


def totals(keep, got, at, cut):
    count = keep.shape[0]
    carried = [] if cut is None else [cut]
    outs = [places for places in RESULTS if at <= places[0] < at + count]
    out_shape = [
        jax.ShapeDtypeStruct((len(places), ROWS, BLK), jnp.bfloat16 if places[0] else jnp.float32) for places in outs
    ]
    couples = pl.BlockSpec((2, ROWS, BLK), lambda i: (i, 0, 0))
    return pl.pallas_call(
        lambda *refs: totals_kernel(at, outs, *refs),
        out_shape=out_shape + [jax.ShapeDtypeStruct((NPW, LISTED // 2, ROWS, 2 * ROWS), jnp.bfloat16)],
        grid=(count // 2,),
        in_specs=[couples] * 2 + [pl.BlockSpec(memory_space=pl.ANY)] * len(carried),
        out_specs=[pl.BlockSpec(shape.shape, lambda i: (0, 0, 0)) for shape in out_shape]
        + [pl.BlockSpec((NPW, 1, ROWS, 2 * ROWS), lambda i: (0, at // 2 + i, 0, 0))],
        input_output_aliases={2: len(outs)} if carried else {},
        compiler_params=params(),
        cost_estimate=pl.CostEstimate(flops=115000001, bytes_accessed=300001, transcendentals=0),
        name="totals",
    )(keep, got, *carried)


def finish_kernel(table_ref, cut_ref, *refs):
    results, (kernel_ref, kernel_t_ref, held, sems) = refs[: len(RESULTS)], refs[len(RESULTS) :]
    low = lax.broadcasted_iota(jnp.int32, (ROWS, 2 * ROWS), 1) < ROWS
    copies = []

    def send(source, out_ref, at):
        copies.append(pltpu.make_async_copy(source, out_ref.at[table_ref[ORDER + at]], sems.at[len(copies)]))
        copies[-1].start()

    for j, at in enumerate(RESULTS[0]):
        send(results[0].at[j], kernel_ref, at)
    for couple in range(LISTED // 2):
        for pair in range(NPW // 2):
            even = cut_ref[2 * pair, couple].astype(jnp.float32)
            odd = cut_ref[2 * pair + 1, couple].astype(jnp.float32)
            lanes = pl.ds(2 * ROWS * pair, 2 * ROWS)
            held[2 * couple, :, lanes] = jnp.where(low, even, pltpu.roll(odd, ROWS, 1))
            held[2 * couple + 1, :, lanes] = jnp.where(low, pltpu.roll(even, ROWS, 1), odd)
        for at in (2 * couple, 2 * couple + 1):
            send(held.at[at], kernel_t_ref, at)
    for places, arrived_ref in zip(RESULTS[1:], results[1:]):
        for j, at in enumerate(places):
            slot = LISTED - LOCAL + at
            held[slot] = arrived_ref[j].astype(jnp.float32)
            send(held.at[slot], kernel_ref, at)
    for copy in copies:
        copy.wait()


def finish(table, cut, results):
    vmem = pl.BlockSpec(memory_space=pltpu.VMEM)
    anywhere = pl.BlockSpec(memory_space=pl.ANY)
    return pl.pallas_call(
        finish_kernel,
        out_shape=[jax.ShapeDtypeStruct((LISTED, ROWS, BLK), jnp.float32)] * 2,
        in_specs=[pl.BlockSpec(memory_space=pltpu.SMEM)] + [vmem] * (1 + len(results)),
        out_specs=[anywhere] * 2,
        scratch_shapes=[
            pltpu.VMEM((2 * LISTED - LOCAL, ROWS, BLK), jnp.float32),
            pltpu.SemaphoreType.DMA((2 * LISTED,)),
        ],
        compiler_params=params(),
        cost_estimate=pl.CostEstimate(flops=115000001, bytes_accessed=300001, transcendentals=0),
        name="finish",
    )(table, cut, *results)


def after(values, others):
    count = len(values)
    return lax.optimization_barrier((*values, *others))[:count]


def body(densities, coulomb, pairs, owner):
    blocks = densities.reshape(STORED, BLK, densities.shape[1])
    weight = coulomb.reshape(1, -1)
    place = jnp.stack([lax.axis_index("trans"), lax.axis_index("pw")]).astype(jnp.int32)
    table = make_table(place, pairs.T, owner)

    def begin(lefts, start, count, table=table):
        own, up_add, down_add, up, down = products(table, blocks, weight, lefts, start, count)
        return own, up_add, down_add, along_y(up, 1), along_y(down, NY - 1)

    def carry_on(own, up_add, down_add, up, down):
        up_sum, down_sum = passed_on(up_add, down_add, up, down)
        return own, up, down, along_y(up_sum, 1), along_y(down_sum, NY - 1)

    near = select(NEAR_AT, 3, table, blocks)
    (ready,) = after((table,), near)
    near = [shifted(send, step) for step, send in zip((1, -1), near)]
    local = begin([blocks], 0, LOCAL, ready)
    (ready,) = after((ready,), local[:1])
    far, last = select(FAR_AT, 2, ready, blocks), select(LAST_AT, 1, ready, blocks)
    own, up_add, down_add, up, down = local
    sums = passed_on(up_add, down_add, up, down)
    local = own, up, down, along_y(sums[0], 1), along_y(sums[1], NY - 1)
    near = after(near, (*last, *sums))
    far = [shifted(send, step) for step, send in zip((2, -2), after(far, near))]
    own, up_add, down_add, up, down = begin(near, NEAR_AT, 2 * MULT)
    sums = passed_on(up_add, down_add, up, down)
    parts_near = own, up, down, along_y(sums[0], 1), along_y(sums[1], NY - 1)
    last = [shifted(send, step) for step, send in zip((2, -2), after(last, far))]
    parts_far = carry_on(*begin(after(far, (*sums, *local[3:])), FAR_AT, LAST_AT - FAR_AT))
    parts_last = carry_on(*begin(after(last, parts_near[3:]), LAST_AT, LISTED - LAST_AT))
    keep, give = plane_sums(table, (after(local, parts_last[:1]), parts_near), MULT)
    stay, near_a, near_b, cut = totals(keep, across_z(give), 0, None)
    keep, give = plane_sums(table, (parts_far, parts_last), 2)
    far_a, far_b, cut = totals(keep, across_z(give), FAR_AT, cut)
    back = [shifted(array, -step) for array, step in zip((near_a, near_b, far_a, far_b), (1, -1, 2, -2))]
    kernel, kernel_t = finish(table, exchanged(cut), (stay, *back))
    return jnp.transpose(kernel, (1, 0, 2)), jnp.transpose(kernel_t, (1, 0, 2))


def solution(mesh):
    in_specs = (P("trans", "pw"), P("pw"), P(), P())
    out_specs = (P("pw", "trans", None), P("pw", "trans", None))
    return jax.shard_map(body, mesh=mesh, in_specs=in_specs, out_specs=out_specs, check_vma=False)
```

time: 162 us -> 153 us (0.944); the launches traced: 162 us -> 150 us
  Pallas kernels: 41.6 us -> 35.3 us
  local copies, waits for them, and re-layouts: 8.05 us -> 3.84 us
  waiting for transfers between devices: 61.4 us -> 59.4 us
    pallas_call x13 -> x12, Pallas kernels: 24.1 us -> 17.2 us  [the longest x3 6.82 us: select(): pl.pallas_call(lambda *refs: select_kernel(start, each, *refs), out_shape...]
    ppermute x12 -> x16, starting transfers between devices: 17.6 us -> 24.3 us  [along_y(): return lax.ppermute(value, 'pw', pairs)]
    unnamed x22 -> x12, local copies, waits for them, and re-layouts: 8.05 us -> 3.84 us
    ppermute x3 -> x2, starting transfers between devices: 11.8 us -> 7.61 us  [across_z(): lax.ppermute(value, 'pw', [(source, (source + NY) % NPW) for source in ra...]
    all_to_all x2 -> x1, starting transfers between devices: 10.3 us -> 7.72 us  [exchanged(): return lax.all_to_all(value, 'pw', split_axis=0, concat_axis=0, tiled=True)]
    ppermute x3 -> x2, waiting for transfers between devices: 4.37 us -> 3.23 us  [across_z(): lax.ppermute(value, 'pw', [(source, (source + NY) % NPW) for source in ra...]
    ppermute x8 -> x10, waiting for transfers between devices: 13.7 us -> 12.6 us  [shifted(): return lax.ppermute(value, 'trans', pairs)]
    ppermute x12 -> x16, waiting for transfers between devices: 40.3 us -> 41.3 us  [along_y(): return lax.ppermute(value, 'pw', pairs)]
  transfers between devices with their start and end apart: 25 -> 29, of which waited for: 12 -> 13; matrix products, arithmetic and copies ran while one was open for 0% -> 0% of each run, Pallas kernels for 20% -> 17%
where the time goes in v4:
time: 153 us; the launch traced here: 150 us
  waiting for transfers between devices  59.4 us (39%)
  starting transfers between devices  50.6 us (33%)
  Pallas kernels  35.3 us (23%)
  local copies, waits for them, and re-layouts  3.84 us (3%)
    ppermute x16, waiting for transfers between devices, along_y(): return lax.ppermute(value, 'pw', pairs)  41.3 us
    ppermute x16, starting transfers between devices, along_y(): return lax.ppermute(value, 'pw', pairs)  24.3 us
    pallas_call x4, Pallas kernels, products(): pl.pallas_call(lambda *refs: products_kernel(count, *refs), out_shape=[ja...  16.4 us
    ppermute x10, waiting for transfers between devices, shifted(): return lax.ppermute(value, 'trans', pairs)  12.6 us
    ppermute x10, starting transfers between devices, shifted(): return lax.ppermute(value, 'trans', pairs)  10.9 us
    all_to_all x1, starting transfers between devices, exchanged(): return lax.all_to_all(value, 'pw', split_axis=0, concat_axis=0, tiled=True)  7.72 us
    ppermute x2, starting transfers between devices, across_z(): lax.ppermute(value, 'pw', [(source, (source + NY) % NPW) for source in ra...  7.61 us
    pallas_call x3, Pallas kernels, select(): pl.pallas_call(lambda *refs: select_kernel(start, each, *refs), out_shape...  6.82 us
  transfers between devices with their start and end apart: 29, of which 13 were waited for; matrix products, arithmetic and copies ran while one was open for 0% of the time, Pallas kernels for 17%

profile of v4, /device:TPU:6, one launch (start us, length us, event | category | flops | bytes accessed | tf_op | source)
XLA Modules:
  0.0 150.2 jit_solution(11849752424291182007)
XLA Ops:
  0.6 0.1 pad_add_fusion.place_ref
  0.7 0.7 copy-done.1
  1.4 0.7 copy-done.2
  2.0 1.7 %make_table.1.refs_0_.table_ref = s32[56]{0:T(128)S(1)} custom-call(s32[2]{0:T(128)S(1)} %pad_add_fusion.place_ref, s32[2,288]{1,0:T(2,128)S(1)} %bitcast.16, s32[128]{0:T(128)S(1)} %copy-done.2), custom_call_target="tpu_custom_call" | custom-call | flops 115000000 | bytes 300001 | tf_op jit(solution)/shard_map/make_table/pallas_call | solution.py:76
  3.8 0.0 copy-start
  3.8 2.5 %copy-done = bf16[4096,640]{1,0:T(8,128)(2,1)S(1)} copy-done((bf16[4096,640]{1,0:T(8,128)(2,1)S(1)}, bf16[4096,640]{1,0:T(8,128)(2,1)}, u32[]{:S(2)}) %copy-start) | copy-done | bytes 5242904
  6.3 3.1 %select.3 = (bf16[3,512,640]{2,1,0:T(8,128)(2,1)S(1)}, bf16[3,512,640]{2,1,0:T(8,128)(2,1)S(1)}) custom-call(s32[56]{0:T(128)S(1)} %make_table.1.refs_0_.table_ref, bf16[8,512,640]{2,1,0:T(8,128)(2,1)S(1)} %bitcast.6), custom_call_target="tpu_custom_call" | custom-call | flops 115000000 | bytes 300001 | tf_op jit(solution)/shard_map/select/pallas_call | solution.py:108
  9.4 0.1 collective-permute-start
  9.5 1.7 %collective-permute-start.1 = (bf16[3,512,640]{2,1,0:T(8,128)(2,1)S(1)}, bf16[3,512,640]{2,1,0:T(8,128)(2,1)S(1)}, u32[]{:S(2)}, u32[]{:S(2)}) collective-permute-start(bf16[3,512,640]{2,1,0:T(8,128)(2,1)S(1)} %get-tuple-element.67), channel_id=1, source_target_pairs={{0,120},{8,0},{16,8},{24,16},{32,24},{40,32},{48,40},{56,48},{64,5... | collective-permute-start | bytes 5898248 | tf_op jit(solution)/shard_map/ppermute | solution.py:28
  11.2 5.2 %products.4 = (f32[2,6,64,512]{3,2,1,0:T(8,128)S(1)}, f32[6,64,512]{2,1,0:T(8,128)S(1)}, f32[6,64,512]{2,1,0:T(8,128)S(1)}, bf16[2,6,64,512]{3,2,1,0:T(8,128)(2,1)S(1)}, bf16[2,6,64,512]{3,2,1,0:T(8,128)(2,1)S(1)}) custom-call(s32[56]{0:T(128)S(1)} %make_table.1.refs_0_.table_ref, bf16[8,512,640]{2,1,0:T(8,128)(2,1)S(1)} %bitcast.7, ...), custom_call_target="tpu_custom_call" | custom-call | flops 115000000 | bytes 300001 | tf_op jit(solution)/shard_map/products/pallas_call | solution.py:165
  16.5 1.6 %collective-permute-start.2 = (bf16[2,6,64,512]{3,2,1,0:T(8,128)(2,1)S(1)}, bf16[2,6,64,512]{3,2,1,0:T(8,128)(2,1)S(1)}, u32[]{:S(2)}, u32[]{:S(2)}) collective-permute-start(bf16[2,6,64,512]{3,2,1,0:T(8,128)(2,1)S(1)} %get-tuple-element.77), channel_id=1, source_target_pairs={{0,1},{1,2},{2,3},{3,0},{4,5},{5,6},{6,7},{7,4},{8,9},{9,10},{10,1... | collective-permute-start | bytes 2359304 | tf_op jit(solution)/shard_map/ppermute | solution.py:33
  18.1 1.7 %collective-permute-start.3 = (bf16[2,6,64,512]{3,2,1,0:T(8,128)(2,1)S(1)}, bf16[2,6,64,512]{3,2,1,0:T(8,128)(2,1)S(1)}, u32[]{:S(2)}, u32[]{:S(2)}) collective-permute-start(bf16[2,6,64,512]{3,2,1,0:T(8,128)(2,1)S(1)} %get-tuple-element.78), channel_id=1, source_target_pairs={{0,3},{1,0},{2,1},{3,2},{4,7},{5,4},{6,5},{7,6},{8,11},{9,8},{10,9... | collective-permute-start | bytes 2359304 | tf_op jit(solution)/shard_map/ppermute | solution.py:33
  19.8 1.4 select.5
  21.2 0.0 slice-start.1
  21.2 2.3 %select.4 = (bf16[2,512,640]{2,1,0:T(8,128)(2,1)S(1)}, bf16[2,512,640]{2,1,0:T(8,128)(2,1)S(1)}) custom-call(s32[56]{0:T(128)S(1)} %make_table.1.refs_0_.table_ref, bf16[8,512,640]{2,1,0:T(8,128)(2,1)S(1)} %bitcast.10), custom_call_target="tpu_custom_call" | custom-call | flops 115000000 | bytes 300001 | tf_op jit(solution)/shard_map/select/pallas_call | solution.py:108
  23.5 14.0 %collective-permute-done.2.up_got_ref.refs_2_ = bf16[2,6,64,512]{3,2,1,0:T(8,128)(2,1)S(1)} collective-permute-done((bf16[2,6,64,512]{3,2,1,0:T(8,128)(2,1)S(1)}, bf16[2,6,64,512]{3,2,1,0:T(8,128)(2,1)S(1)}, u32[]{:S(2)}, u32[]{:S(2)}) %collective-permute-start.2) | collective-permute-done | bytes 786464 | tf_op jit(solution)/shard_map/ppermute | solution.py:33
  37.5 0.0 collective-permute-done.3.down_got_ref.refs_3_
  37.5 0.2 passed_on.4
  37.7 1.6 %collective-permute-start.4 = (bf16[2,512,640]{2,1,0:T(8,128)(2,1)S(1)}, bf16[2,512,640]{2,1,0:T(8,128)(2,1)S(1)}, u32[]{:S(2)}, u32[]{:S(2)}) collective-permute-start(bf16[2,512,640]{2,1,0:T(8,128)(2,1)S(1)} %get-tuple-element.83), channel_id=1, source_target_pairs={{0,16},{8,24},{16,32},{24,40},{32,48},{40,56},{48,64},{56,72},{64,... | collective-permute-start | bytes 3932168 | tf_op jit(solution)/shard_map/ppermute | solution.py:28
  39.3 0.5 collective-permute-start.5
  39.8 5.3 %products.5 = (f32[2,6,64,512]{3,2,1,0:T(8,128)S(1)}, f32[6,64,512]{2,1,0:T(8,128)S(1)}, f32[6,64,512]{2,1,0:T(8,128)S(1)}, bf16[2,6,64,512]{3,2,1,0:T(8,128)(2,1)S(1)}, bf16[2,6,64,512]{3,2,1,0:T(8,128)(2,1)S(1)}) custom-call(s32[56]{0:T(128)S(1)} %make_table.1.refs_0_.table_ref, bf16[8,512,640]{2,1,0:T(8,128)(2,1)S(1)} %bitcast.13, ...), custom_call_target="tpu_custom_call" | custom-call | flops 115000000 | bytes 300001 | tf_op jit(solution)/shard_map/products/pallas_call | solution.py:165
  45.1 1.6 %collective-permute-start.6 = (bf16[2,6,64,512]{3,2,1,0:T(8,128)(2,1)S(1)}, bf16[2,6,64,512]{3,2,1,0:T(8,128)(2,1)S(1)}, u32[]{:S(2)}, u32[]{:S(2)}) collective-permute-start(bf16[2,6,64,512]{3,2,1,0:T(8,128)(2,1)S(1)} %get-tuple-element.87), channel_id=1, source_target_pairs={{0,1},{1,2},{2,3},{3,0},{4,5},{5,6},{6,7},{7,4},{8,9},{9,10},{10,1... | collective-permute-start | bytes 2359304 | tf_op jit(solution)/shard_map/ppermute | solution.py:33
  46.8 1.7 %collective-permute-start.7 = (bf16[2,6,64,512]{3,2,1,0:T(8,128)(2,1)S(1)}, bf16[2,6,64,512]{3,2,1,0:T(8,128)(2,1)S(1)}, u32[]{:S(2)}, u32[]{:S(2)}) collective-permute-start(bf16[2,6,64,512]{3,2,1,0:T(8,128)(2,1)S(1)} %get-tuple-element.88), channel_id=1, source_target_pairs={{0,3},{1,0},{2,1},{3,2},{4,7},{5,4},{6,5},{7,6},{8,11},{9,8},{10,9... | collective-permute-start | bytes 2359304 | tf_op jit(solution)/shard_map/ppermute | solution.py:33
  48.4 0.4 collective-permute-start.8
  48.8 18.1 %collective-permute-done.6.up_got_ref.refs_7_ = bf16[2,6,64,512]{3,2,1,0:T(8,128)(2,1)S(1)} collective-permute-done((bf16[2,6,64,512]{3,2,1,0:T(8,128)(2,1)S(1)}, bf16[2,6,64,512]{3,2,1,0:T(8,128)(2,1)S(1)}, u32[]{:S(2)}, u32[]{:S(2)}) %collective-permute-start.6) | collective-permute-done | bytes 786464 | tf_op jit(solution)/shard_map/ppermute | solution.py:33
  66.9 1.8 %collective-permute-start.9 = (bf16[6,64,512]{2,1,0:T(8,128)(2,1)S(1)}, bf16[6,64,512]{2,1,0:T(8,128)(2,1)S(1)}, u32[]{:S(2)}, u32[]{:S(2)}) collective-permute-start(bf16[6,64,512]{2,1,0:T(8,128)(2,1)S(1)} %get-tuple-element.80), channel_id=1, source_target_pairs={{0,3},{1,0},{2,1},{3,2},{4,7},{5,4},{6,5},{7,6},{8,11},{9,8},{10,9... | collective-permute-start | bytes 1179656 | tf_op jit(solution)/shard_map/ppermute | solution.py:33
  68.7 0.2 passed_on.5
  68.9 0.3 collective-permute-start.16
  69.2 1.2 collective-permute-done.5.refs_4_
  70.4 2.4 %collective-permute-start.14 = (bf16[1,512,640]{2,1,0:T(8,128)(2,1)S(1)}, bf16[1,512,640]{2,1,0:T(8,128)(2,1)S(1)}, u32[]{:S(2)}, u32[]{:S(2)}) collective-permute-start(bf16[1,512,640]{2,1,0:T(8,128)(2,1)S(1)} %get-tuple-element.100), channel_id=1, source_target_pairs={{0,16},{8,24},{16,32},{24,40},{32,48},{40,56},{48,64},{56,72},{64,... | collective-permute-start | bytes 1966088 | tf_op jit(solution)/shard_map/ppermute | solution.py:28
  72.8 2.5 %collective-permute-done.8.refs_4_ = bf16[6,64,512]{2,1,0:T(8,128)(2,1)S(1)} collective-permute-done((bf16[6,64,512]{2,1,0:T(8,128)(2,1)S(1)}, bf16[6,64,512]{2,1,0:T(8,128)(2,1)S(1)}, u32[]{:S(2)}, u32[]{:S(2)}) %collective-permute-start.8) | collective-permute-done | bytes 393248 | tf_op jit(solution)/shard_map/ppermute | solution.py:33
  75.3 1.8 %collective-permute-start.17 = (bf16[6,64,512]{2,1,0:T(8,128)(2,1)S(1)}, bf16[6,64,512]{2,1,0:T(8,128)(2,1)S(1)}, u32[]{:S(2)}, u32[]{:S(2)}) collective-permute-start(bf16[6,64,512]{2,1,0:T(8,128)(2,1)S(1)} %get-tuple-element.90), channel_id=1, source_target_pairs={{0,3},{1,0},{2,1},{3,2},{4,7},{5,4},{6,5},{7,6},{8,11},{9,8},{10,9... | collective-permute-start | bytes 1179656 | tf_op jit(solution)/shard_map/ppermute | solution.py:33
  77.1 3.7 %products.6 = (f32[2,4,64,512]{3,2,1,0:T(8,128)S(1)}, f32[4,64,512]{2,1,0:T(8,128)S(1)}, f32[4,64,512]{2,1,0:T(8,128)S(1)}, bf16[2,4,64,512]{3,2,1,0:T(8,128)(2,1)S(1)}, bf16[2,4,64,512]{3,2,1,0:T(8,128)(2,1)S(1)}) custom-call(s32[56]{0:T(128)S(1)} %make_table.1.refs_0_.table_ref, bf16[8,512,640]{2,1,0:T(8,128)(2,1)S(1)} %bitcast.14, ...), custom_call_target="tpu_custom_call" | custom-call | flops 115000000 | bytes 300001 | tf_op jit(solution)/shard_map/products/pallas_call | solution.py:165
  80.8 0.3 collective-permute-start.10
  81.1 1.9 %collective-permute-done.16.refs_9_ = bf16[6,64,512]{2,1,0:T(8,128)(2,1)S(1)} collective-permute-done((bf16[6,64,512]{2,1,0:T(8,128)(2,1)S(1)}, bf16[6,64,512]{2,1,0:T(8,128)(2,1)S(1)}, u32[]{:S(2)}, u32[]{:S(2)}) %collective-permute-start.16) | collective-permute-done | bytes 393248 | tf_op jit(solution)/shard_map/ppermute | solution.py:33
  83.0 2.6 %collective-permute-start.11 = (bf16[2,4,64,512]{3,2,1,0:T(8,128)(2,1)S(1)}, bf16[2,4,64,512]{3,2,1,0:T(8,128)(2,1)S(1)}, u32[]{:S(2)}, u32[]{:S(2)}) collective-permute-start(bf16[2,4,64,512]{3,2,1,0:T(8,128)(2,1)S(1)} %get-tuple-element.95), channel_id=1, source_target_pairs={{0,3},{1,0},{2,1},{3,2},{4,7},{5,4},{6,5},{7,6},{8,11},{9,8},{10,9... | collective-permute-start | bytes 1572872 | tf_op jit(solution)/shard_map/ppermute | solution.py:33
  85.5 1.3 collective-permute-done.15.refs_4_
  86.8 2.1 %products.7 = (f32[2,2,64,512]{3,2,1,0:T(8,128)S(1)}, f32[2,64,512]{2,1,0:T(8,128)S(1)}, f32[2,64,512]{2,1,0:T(8,128)S(1)}, bf16[2,2,64,512]{3,2,1,0:T(8,128)(2,1)S(1)}, bf16[2,2,64,512]{3,2,1,0:T(8,128)(2,1)S(1)}) custom-call(s32[56]{0:T(128)S(1)} %make_table.1.refs_0_.table_ref, bf16[8,512,640]{2,1,0:T(8,128)(2,1)S(1)} %bitcast.15, ...), custom_call_target="tpu_custom_call" | custom-call | flops 115000000 | bytes 300001 | tf_op jit(solution)/shard_map/products/pallas_call | solution.py:165
  89.0 1.6 %collective-permute-start.18 = (bf16[2,2,64,512]{3,2,1,0:T(8,128)(2,1)S(1)}, bf16[2,2,64,512]{3,2,1,0:T(8,128)(2,1)S(1)}, u32[]{:S(2)}, u32[]{:S(2)}) collective-permute-start(bf16[2,2,64,512]{3,2,1,0:T(8,128)(2,1)S(1)} %get-tuple-element.105), channel_id=1, source_target_pairs={{0,1},{1,2},{2,3},{3,0},{4,5},{5,6},{6,7},{7,4},{8,9},{9,10},{10,1... | collective-permute-start | bytes 786440 | tf_op jit(solution)/shard_map/ppermute | solution.py:33
  90.6 1.7 %collective-permute-start.19 = (bf16[2,2,64,512]{3,2,1,0:T(8,128)(2,1)S(1)}, bf16[2,2,64,512]{3,2,1,0:T(8,128)(2,1)S(1)}, u32[]{:S(2)}, u32[]{:S(2)}) collective-permute-start(bf16[2,2,64,512]{3,2,1,0:T(8,128)(2,1)S(1)} %get-tuple-element.106), channel_id=1, source_target_pairs={{0,3},{1,0},{2,1},{3,2},{4,7},{5,4},{6,5},{7,6},{8,11},{9,8},{10,9... | collective-permute-start | bytes 786440 | tf_op jit(solution)/shard_map/ppermute | solution.py:33
  92.3 1.7 %plane_sums.3 = (f32[12,64,512]{2,1,0:T(8,128)S(1)}, bf16[12,64,512]{2,1,0:T(8,128)(2,1)S(1)}) custom-call(s32[56]{0:T(128)S(1)} %make_table.1.refs_0_.table_ref, f32[2,6,64,512]{3,2,1,0:T(8,128)S(1)} %get-tuple-element.113.refs_1_, bf16[2,6,64,512]{3,2,1,0:T(8,128)(2,1)S(1)} %collective-permute-done.2.up_got_ref.refs_2_, ...), custom_call_target="tpu_custom_call" | custom-call | flops 115000000 | bytes 300001 | tf_op jit(solution)/shard_map/plane_sums/pallas_call | solution.py:248
  93.9 3.7 %collective-permute-start.23 = (bf16[12,64,512]{2,1,0:T(8,128)(2,1)S(1)}, bf16[12,64,512]{2,1,0:T(8,128)(2,1)S(1)}, u32[]{:S(2)}, u32[]{:S(2)}) collective-permute-start(bf16[12,64,512]{2,1,0:T(8,128)(2,1)S(1)} %get-tuple-element.120), channel_id=1, source_target_pairs={{0,4},{1,5},{2,6},{3,7},{4,0},{5,1},{6,2},{7,3},{8,12},{9,13},{10,... | collective-permute-start | bytes 2359304 | tf_op jit(solution)/shard_map/ppermute | solution.py:37
  97.6 0.2 collective-permute-done.11.down_got_ref.refs_3_
  97.8 0.1 passed_on.6
  98.0 0.4 collective-permute-start.12
  98.4 3.4 %collective-permute-start.13 = (bf16[4,64,512]{2,1,0:T(8,128)(2,1)S(1)}, bf16[4,64,512]{2,1,0:T(8,128)(2,1)S(1)}, u32[]{:S(2)}, u32[]{:S(2)}) collective-permute-start(bf16[4,64,512]{2,1,0:T(8,128)(2,1)S(1)} %get-tuple-element.99), channel_id=1, source_target_pairs={{0,3},{1,0},{2,1},{3,2},{4,7},{5,4},{6,5},{7,6},{8,11},{9,8},{10,9... | collective-permute-start | bytes 786440 | tf_op jit(solution)/shard_map/ppermute | solution.py:33
  101.7 1.7 %collective-permute-done.19.down_got_ref.refs_8_ = bf16[2,2,64,512]{3,2,1,0:T(8,128)(2,1)S(1)} collective-permute-done((bf16[2,2,64,512]{3,2,1,0:T(8,128)(2,1)S(1)}, bf16[2,2,64,512]{3,2,1,0:T(8,128)(2,1)S(1)}, u32[]{:S(2)}, u32[]{:S(2)}) %collective-permute-start.19) | collective-permute-done | bytes 262176 | tf_op jit(solution)/shard_map/ppermute | solution.py:33
  103.5 0.1 passed_on.7
  103.5 0.1 collective-permute-start.20
  103.6 3.5 %collective-permute-start.21 = (bf16[2,64,512]{2,1,0:T(8,128)(2,1)S(1)}, bf16[2,64,512]{2,1,0:T(8,128)(2,1)S(1)}, u32[]{:S(2)}, u32[]{:S(2)}) collective-permute-start(bf16[2,64,512]{2,1,0:T(8,128)(2,1)S(1)} %get-tuple-element.110), channel_id=1, source_target_pairs={{0,3},{1,0},{2,1},{3,2},{4,7},{5,4},{6,5},{7,6},{8,11},{9,8},{10,9... | collective-permute-start | bytes 393224 | tf_op jit(solution)/shard_map/ppermute | solution.py:33
  107.1 2.9 %collective-permute-done.20.refs_9_ = bf16[2,64,512]{2,1,0:T(8,128)(2,1)S(1)} collective-permute-done((bf16[2,64,512]{2,1,0:T(8,128)(2,1)S(1)}, bf16[2,64,512]{2,1,0:T(8,128)(2,1)S(1)}, u32[]{:S(2)}, u32[]{:S(2)}) %collective-permute-start.20) | collective-permute-done | bytes 131104 | tf_op jit(solution)/shard_map/ppermute | solution.py:33
  110.0 1.0 plane_sums.2
  111.0 3.9 %collective-permute-start.22 = (bf16[6,64,512]{2,1,0:T(8,128)(2,1)S(1)}, bf16[6,64,512]{2,1,0:T(8,128)(2,1)S(1)}, u32[]{:S(2)}, u32[]{:S(2)}) collective-permute-start(bf16[6,64,512]{2,1,0:T(8,128)(2,1)S(1)} %get-tuple-element.112), channel_id=1, source_target_pairs={{0,4},{1,5},{2,6},{3,7},{4,0},{5,1},{6,2},{7,3},{8,12},{9,13},{10,... | collective-permute-start | bytes 1179656 | tf_op jit(solution)/shard_map/ppermute | solution.py:37
  115.0 2.5 %totals.2 = (f32[6,64,512]{2,1,0:T(8,128)S(1)}, bf16[3,64,512]{2,1,0:T(8,128)(2,1)S(1)}, bf16[3,64,512]{2,1,0:T(8,128)(2,1)S(1)}, bf16[8,9,64,128]{3,2,1,0:T(8,128)(2,1)}) custom-call(f32[12,64,512]{2,1,0:T(8,128)S(1)} %get-tuple-element.119.refs_0_, bf16[12,64,512]{2,1,0:T(8,128)(2,1)S(1)} %collective-permute-done.23.refs_1_), custom_call_target="tpu_custom_call" | custom-call | flops 115000000 | bytes 300001 | tf_op jit(solution)/shard_map/totals/pallas_call | solution.py:288
  117.5 3.2 %collective-permute-done.22.refs_1_ = bf16[6,64,512]{2,1,0:T(8,128)(2,1)S(1)} collective-permute-done((bf16[6,64,512]{2,1,0:T(8,128)(2,1)S(1)}, bf16[6,64,512]{2,1,0:T(8,128)(2,1)S(1)}, u32[]{:S(2)}, u32[]{:S(2)}) %collective-permute-start.22) | collective-permute-done | bytes 393248 | tf_op jit(solution)/shard_map/ppermute | solution.py:37
  120.7 1.6 %totals.3 = (bf16[3,64,512]{2,1,0:T(8,128)(2,1)S(1)}, bf16[3,64,512]{2,1,0:T(8,128)(2,1)S(1)}, bf16[8,9,64,128]{3,2,1,0:T(8,128)(2,1)}) custom-call(f32[6,64,512]{2,1,0:T(8,128)S(1)} %get-tuple-element.111.refs_0_, bf16[6,64,512]{2,1,0:T(8,128)(2,1)S(1)} %collective-permute-done.22.refs_1_, ...), custom_call_target="tpu_custom_call", output_to_operand_aliasing={{2}: (2, {})} | custom-call | flops 115000000 | bytes 300001 | tf_op jit(solution)/shard_map/totals/pallas_call | solution.py:288
  122.3 7.7 %all-to-all-start = ((bf16[8,9,64,128]{3,2,1,0:T(8,128)(2,1)}), bf16[8,9,64,128]{3,2,1,0:T(8,128)(2,1)S(1)}, u32[]{:S(2)}, u32[]{:S(2)}) async-start(bf16[8,9,64,128]{3,2,1,0:T(8,128)(2,1)} %get-tuple-element.122), calls=%async_computation | async-start | bytes 2359296 | tf_op jit(solution)/shard_map/all_to_all | solution.py:41
  130.0 0.5 collective-permute-start.25
  130.5 0.5 collective-permute-start.26
  131.0 3.6 %collective-permute-start.27 = (bf16[3,64,512]{2,1,0:T(8,128)(2,1)S(1)}, bf16[3,64,512]{2,1,0:T(8,128)(2,1)S(1)}, u32[]{:S(2)}, u32[]{:S(2)}) collective-permute-start(bf16[3,64,512]{2,1,0:T(8,128)(2,1)S(1)} %get-tuple-element.127), channel_id=1, source_target_pairs={{0,16},{8,24},{16,32},{24,40},{32,48},{40,56},{48,64},{56,72},{64,... | collective-permute-start | bytes 589832 | tf_op jit(solution)/shard_map/ppermute | solution.py:28
  134.7 1.1 collective-permute-done.25.refs_2_
  135.7 9.0 %collective-permute-done.26.refs_3_ = bf16[3,64,512]{2,1,0:T(8,128)(2,1)S(1)} collective-permute-done((bf16[3,64,512]{2,1,0:T(8,128)(2,1)S(1)}, bf16[3,64,512]{2,1,0:T(8,128)(2,1)S(1)}, u32[]{:S(2)}, u32[]{:S(2)}) %collective-permute-start.26) | collective-permute-done | bytes 196640 | tf_op jit(solution)/shard_map/ppermute | solution.py:28
  144.8 2.3 %all-to-all-done.cut_ref = bf16[8,9,64,128]{3,2,1,0:T(8,128)(2,1)S(1)} async-done(((bf16[8,9,64,128]{3,2,1,0:T(8,128)(2,1)}), bf16[8,9,64,128]{3,2,1,0:T(8,128)(2,1)S(1)}, u32[]{:S(2)}, u32[]{:S(2)}) %all-to-all-start) | async-done | bytes 1179680 | tf_op jit(solution)/shard_map/all_to_all | solution.py:41
  147.1 3.0 %finish.1 = (f32[18,64,512]{2,1,0:T(8,128)}, f32[18,64,512]{2,1,0:T(8,128)}) custom-call(s32[56]{0:T(128)S(1)} %make_table.1.refs_0_.table_ref, bf16[8,9,64,128]{3,2,1,0:T(8,128)(2,1)S(1)} %all-to-all-done.cut_ref, f32[6,64,512]{2,1,0:T(8,128)S(1)} %get-tuple-element.123.refs_0_, bf16[3,64,512]{2,1,0:T(8,128)(2,1)S(1)} %collective-permute-done.24.refs_1_, ...), custom_call_target="tpu_custom_call" | custom-call | flops 115000000 | bytes 300001 | tf_op jit(solution)/shard_map/finish/pallas_call | solution.py:334
  (26 shorter events, 0.1 us)
Async XLA Ops:
  0.7 0.7 copy-start.1
  1.4 0.7 copy-start.2
  3.8 2.5 %copy-start = (bf16[4096,640]{1,0:T(8,128)(2,1)S(1)}, bf16[4096,640]{1,0:T(8,128)(2,1)}, u32[]{:S(2)}) copy-start(bf16[4096,640]{1,0:T(8,128)(2,1)} %param.4) | copy-start | bytes 15728644
  6.3 5.0 %copy-start.3 = (f32[640]{0:T(1024)S(1)}, f32[640]{0:T(1024)}, u32[]{:S(2)}) copy-start(f32[640]{0:T(1024)} %param.5) | copy-start | bytes 7684
  9.4 28.3 %collective-permute-start = (bf16[3,512,640]{2,1,0:T(8,128)(2,1)S(1)}, bf16[3,512,640]{2,1,0:T(8,128)(2,1)S(1)}, u32[]{:S(2)}, u32[]{:S(2)}) collective-permute-start(bf16[3,512,640]{2,1,0:T(8,128)(2,1)S(1)} %get-tuple-element.66), channel_id=1, source_target_pairs={{0,8},{8,16},{16,24},{24,32},{32,40},{40,48},{48,56},{56,64},{64,7... | collective-permute-start | bytes 5898248 | tf_op jit(solution)/shard_map/ppermute | solution.py:28
  9.5 28.2 %collective-permute-start.1 = (bf16[3,512,640]{2,1,0:T(8,128)(2,1)S(1)}, bf16[3,512,640]{2,1,0:T(8,128)(2,1)S(1)}, u32[]{:S(2)}, u32[]{:S(2)}) collective-permute-start(bf16[3,512,640]{2,1,0:T(8,128)(2,1)S(1)} %get-tuple-element.67), channel_id=1, source_target_pairs={{0,120},{8,0},{16,8},{24,16},{32,24},{40,32},{48,40},{56,48},{64,5... | collective-permute-start | bytes 5898248 | tf_op jit(solution)/shard_map/ppermute | solution.py:28
  16.5 21.0 %collective-permute-start.2 = (bf16[2,6,64,512]{3,2,1,0:T(8,128)(2,1)S(1)}, bf16[2,6,64,512]{3,2,1,0:T(8,128)(2,1)S(1)}, u32[]{:S(2)}, u32[]{:S(2)}) collective-permute-start(bf16[2,6,64,512]{3,2,1,0:T(8,128)(2,1)S(1)} %get-tuple-element.77), channel_id=1, source_target_pairs={{0,1},{1,2},{2,3},{3,0},{4,5},{5,6},{6,7},{7,4},{8,9},{9,10},{10,1... | collective-permute-start | bytes 2359304 | tf_op jit(solution)/shard_map/ppermute | solution.py:33
  18.1 19.4 %collective-permute-start.3 = (bf16[2,6,64,512]{3,2,1,0:T(8,128)(2,1)S(1)}, bf16[2,6,64,512]{3,2,1,0:T(8,128)(2,1)S(1)}, u32[]{:S(2)}, u32[]{:S(2)}) collective-permute-start(bf16[2,6,64,512]{3,2,1,0:T(8,128)(2,1)S(1)} %get-tuple-element.78), channel_id=1, source_target_pairs={{0,3},{1,0},{2,1},{3,2},{4,7},{5,4},{6,5},{7,6},{8,11},{9,8},{10,9... | collective-permute-start | bytes 2359304 | tf_op jit(solution)/shard_map/ppermute | solution.py:33
  19.8 20.0 %slice-start = ((s8[5242880]{0:T(1024)(128)(4,1)}), s8[4194304]{0:T(1024)(128)(4,1)S(1)}, s32[]{:S(2)}) async-start(s8[5242880]{0:T(1024)(128)(4,1)} %bitcast.11), calls=%async_computation.1 | async-start | bytes 8388608
  21.2 18.6 %slice-start.1 = ((s8[5242880]{0:T(1024)(128)(4,1)}), s8[1048576]{0:T(1024)(128)(4,1)S(1)}, s32[]{:S(2)}) async-start(s8[5242880]{0:T(1024)(128)(4,1)} %bitcast.11), calls=%async_computation.2 | async-start | bytes 2097152
  37.7 31.5 %collective-permute-start.4 = (bf16[2,512,640]{2,1,0:T(8,128)(2,1)S(1)}, bf16[2,512,640]{2,1,0:T(8,128)(2,1)S(1)}, u32[]{:S(2)}, u32[]{:S(2)}) collective-permute-start(bf16[2,512,640]{2,1,0:T(8,128)(2,1)S(1)} %get-tuple-element.83), channel_id=1, source_target_pairs={{0,16},{8,24},{16,32},{24,40},{32,48},{40,56},{48,64},{56,72},{64,... | collective-permute-start | bytes 3932168 | tf_op jit(solution)/shard_map/ppermute | solution.py:28
  39.3 31.1 %collective-permute-start.5 = (bf16[2,512,640]{2,1,0:T(8,128)(2,1)S(1)}, bf16[2,512,640]{2,1,0:T(8,128)(2,1)S(1)}, u32[]{:S(2)}, u32[]{:S(2)}) collective-permute-start(bf16[2,512,640]{2,1,0:T(8,128)(2,1)S(1)} %get-tuple-element.84), channel_id=1, source_target_pairs={{0,112},{8,120},{16,0},{24,8},{32,16},{40,24},{48,32},{56,40},{64,... | collective-permute-start | bytes 3932168 | tf_op jit(solution)/shard_map/ppermute | solution.py:28
  45.1 21.8 %collective-permute-start.6 = (bf16[2,6,64,512]{3,2,1,0:T(8,128)(2,1)S(1)}, bf16[2,6,64,512]{3,2,1,0:T(8,128)(2,1)S(1)}, u32[]{:S(2)}, u32[]{:S(2)}) collective-permute-start(bf16[2,6,64,512]{3,2,1,0:T(8,128)(2,1)S(1)} %get-tuple-element.87), channel_id=1, source_target_pairs={{0,1},{1,2},{2,3},{3,0},{4,5},{5,6},{6,7},{7,4},{8,9},{9,10},{10,1... | collective-permute-start | bytes 2359304 | tf_op jit(solution)/shard_map/ppermute | solution.py:33
  46.8 21.9 %collective-permute-start.7 = (bf16[2,6,64,512]{3,2,1,0:T(8,128)(2,1)S(1)}, bf16[2,6,64,512]{3,2,1,0:T(8,128)(2,1)S(1)}, u32[]{:S(2)}, u32[]{:S(2)}) collective-permute-start(bf16[2,6,64,512]{3,2,1,0:T(8,128)(2,1)S(1)} %get-tuple-element.88), channel_id=1, source_target_pairs={{0,3},{1,0},{2,1},{3,2},{4,7},{5,4},{6,5},{7,6},{8,11},{9,8},{10,9... | collective-permute-start | bytes 2359304 | tf_op jit(solution)/shard_map/ppermute | solution.py:33
  48.4 26.9 %collective-permute-start.8 = (bf16[6,64,512]{2,1,0:T(8,128)(2,1)S(1)}, bf16[6,64,512]{2,1,0:T(8,128)(2,1)S(1)}, u32[]{:S(2)}, u32[]{:S(2)}) collective-permute-start(bf16[6,64,512]{2,1,0:T(8,128)(2,1)S(1)} %get-tuple-element.79), channel_id=1, source_target_pairs={{0,1},{1,2},{2,3},{3,0},{4,5},{5,6},{6,7},{7,4},{8,9},{9,10},{10,1... | collective-permute-start | bytes 1179656 | tf_op jit(solution)/shard_map/ppermute | solution.py:33
  66.9 10.2 %collective-permute-start.9 = (bf16[6,64,512]{2,1,0:T(8,128)(2,1)S(1)}, bf16[6,64,512]{2,1,0:T(8,128)(2,1)S(1)}, u32[]{:S(2)}, u32[]{:S(2)}) collective-permute-start(bf16[6,64,512]{2,1,0:T(8,128)(2,1)S(1)} %get-tuple-element.80), channel_id=1, source_target_pairs={{0,3},{1,0},{2,1},{3,2},{4,7},{5,4},{6,5},{7,6},{8,11},{9,8},{10,9... | collective-permute-start | bytes 1179656 | tf_op jit(solution)/shard_map/ppermute | solution.py:33
  68.9 14.1 %collective-permute-start.16 = (bf16[6,64,512]{2,1,0:T(8,128)(2,1)S(1)}, bf16[6,64,512]{2,1,0:T(8,128)(2,1)S(1)}, u32[]{:S(2)}, u32[]{:S(2)}) collective-permute-start(bf16[6,64,512]{2,1,0:T(8,128)(2,1)S(1)} %get-tuple-element.89), channel_id=1, source_target_pairs={{0,1},{1,2},{2,3},{3,0},{4,5},{5,6},{6,7},{7,4},{8,9},{9,10},{10,1... | collective-permute-start | bytes 1179656 | tf_op jit(solution)/shard_map/ppermute | solution.py:33
  70.4 15.1 %collective-permute-start.14 = (bf16[1,512,640]{2,1,0:T(8,128)(2,1)S(1)}, bf16[1,512,640]{2,1,0:T(8,128)(2,1)S(1)}, u32[]{:S(2)}, u32[]{:S(2)}) collective-permute-start(bf16[1,512,640]{2,1,0:T(8,128)(2,1)S(1)} %get-tuple-element.100), channel_id=1, source_target_pairs={{0,16},{8,24},{16,32},{24,40},{32,48},{40,56},{48,64},{56,72},{64,... | collective-permute-start | bytes 1966088 | tf_op jit(solution)/shard_map/ppermute | solution.py:28
  72.8 14.0 %collective-permute-start.15 = (bf16[1,512,640]{2,1,0:T(8,128)(2,1)S(1)}, bf16[1,512,640]{2,1,0:T(8,128)(2,1)S(1)}, u32[]{:S(2)}, u32[]{:S(2)}) collective-permute-start(bf16[1,512,640]{2,1,0:T(8,128)(2,1)S(1)} %get-tuple-element.101), channel_id=1, source_target_pairs={{0,112},{8,120},{16,0},{24,8},{32,16},{40,24},{48,32},{56,40},{64,... | collective-permute-start | bytes 1966088 | tf_op jit(solution)/shard_map/ppermute | solution.py:28
  75.3 10.2 %collective-permute-start.17 = (bf16[6,64,512]{2,1,0:T(8,128)(2,1)S(1)}, bf16[6,64,512]{2,1,0:T(8,128)(2,1)S(1)}, u32[]{:S(2)}, u32[]{:S(2)}) collective-permute-start(bf16[6,64,512]{2,1,0:T(8,128)(2,1)S(1)} %get-tuple-element.90), channel_id=1, source_target_pairs={{0,3},{1,0},{2,1},{3,2},{4,7},{5,4},{6,5},{7,6},{8,11},{9,8},{10,9... | collective-permute-start | bytes 1179656 | tf_op jit(solution)/shard_map/ppermute | solution.py:33
  80.8 16.8 %collective-permute-start.10 = (bf16[2,4,64,512]{3,2,1,0:T(8,128)(2,1)S(1)}, bf16[2,4,64,512]{3,2,1,0:T(8,128)(2,1)S(1)}, u32[]{:S(2)}, u32[]{:S(2)}) collective-permute-start(bf16[2,4,64,512]{3,2,1,0:T(8,128)(2,1)S(1)} %get-tuple-element.94), channel_id=1, source_target_pairs={{0,1},{1,2},{2,3},{3,0},{4,5},{5,6},{6,7},{7,4},{8,9},{9,10},{10,1... | collective-permute-start | bytes 1572872 | tf_op jit(solution)/shard_map/ppermute | solution.py:33
  83.0 14.9 %collective-permute-start.11 = (bf16[2,4,64,512]{3,2,1,0:T(8,128)(2,1)S(1)}, bf16[2,4,64,512]{3,2,1,0:T(8,128)(2,1)S(1)}, u32[]{:S(2)}, u32[]{:S(2)}) collective-permute-start(bf16[2,4,64,512]{3,2,1,0:T(8,128)(2,1)S(1)} %get-tuple-element.95), channel_id=1, source_target_pairs={{0,3},{1,0},{2,1},{3,2},{4,7},{5,4},{6,5},{7,6},{8,11},{9,8},{10,9... | collective-permute-start | bytes 1572872 | tf_op jit(solution)/shard_map/ppermute | solution.py:33
  89.0 12.8 %collective-permute-start.18 = (bf16[2,2,64,512]{3,2,1,0:T(8,128)(2,1)S(1)}, bf16[2,2,64,512]{3,2,1,0:T(8,128)(2,1)S(1)}, u32[]{:S(2)}, u32[]{:S(2)}) collective-permute-start(bf16[2,2,64,512]{3,2,1,0:T(8,128)(2,1)S(1)} %get-tuple-element.105), channel_id=1, source_target_pairs={{0,1},{1,2},{2,3},{3,0},{4,5},{5,6},{6,7},{7,4},{8,9},{9,10},{10,1... | collective-permute-start | bytes 786440 | tf_op jit(solution)/shard_map/ppermute | solution.py:33
  90.6 12.8 %collective-permute-start.19 = (bf16[2,2,64,512]{3,2,1,0:T(8,128)(2,1)S(1)}, bf16[2,2,64,512]{3,2,1,0:T(8,128)(2,1)S(1)}, u32[]{:S(2)}, u32[]{:S(2)}) collective-permute-start(bf16[2,2,64,512]{3,2,1,0:T(8,128)(2,1)S(1)} %get-tuple-element.106), channel_id=1, source_target_pairs={{0,3},{1,0},{2,1},{3,2},{4,7},{5,4},{6,5},{7,6},{8,11},{9,8},{10,9... | collective-permute-start | bytes 786440 | tf_op jit(solution)/shard_map/ppermute | solution.py:33
  93.9 21.1 %collective-permute-start.23 = (bf16[12,64,512]{2,1,0:T(8,128)(2,1)S(1)}, bf16[12,64,512]{2,1,0:T(8,128)(2,1)S(1)}, u32[]{:S(2)}, u32[]{:S(2)}) collective-permute-start(bf16[12,64,512]{2,1,0:T(8,128)(2,1)S(1)} %get-tuple-element.120), channel_id=1, source_target_pairs={{0,4},{1,5},{2,6},{3,7},{4,0},{5,1},{6,2},{7,3},{8,12},{9,13},{10,... | collective-permute-start | bytes 2359304 | tf_op jit(solution)/shard_map/ppermute | solution.py:37
  98.0 9.1 %collective-permute-start.12 = (bf16[4,64,512]{2,1,0:T(8,128)(2,1)S(1)}, bf16[4,64,512]{2,1,0:T(8,128)(2,1)S(1)}, u32[]{:S(2)}, u32[]{:S(2)}) collective-permute-start(bf16[4,64,512]{2,1,0:T(8,128)(2,1)S(1)} %get-tuple-element.98), channel_id=1, source_target_pairs={{0,1},{1,2},{2,3},{3,0},{4,5},{5,6},{6,7},{7,4},{8,9},{9,10},{10,1... | collective-permute-start | bytes 786440 | tf_op jit(solution)/shard_map/ppermute | solution.py:33
  98.4 8.7 %collective-permute-start.13 = (bf16[4,64,512]{2,1,0:T(8,128)(2,1)S(1)}, bf16[4,64,512]{2,1,0:T(8,128)(2,1)S(1)}, u32[]{:S(2)}, u32[]{:S(2)}) collective-permute-start(bf16[4,64,512]{2,1,0:T(8,128)(2,1)S(1)} %get-tuple-element.99), channel_id=1, source_target_pairs={{0,3},{1,0},{2,1},{3,2},{4,7},{5,4},{6,5},{7,6},{8,11},{9,8},{10,9... | collective-permute-start | bytes 786440 | tf_op jit(solution)/shard_map/ppermute | solution.py:33
  103.5 6.4 %collective-permute-start.20 = (bf16[2,64,512]{2,1,0:T(8,128)(2,1)S(1)}, bf16[2,64,512]{2,1,0:T(8,128)(2,1)S(1)}, u32[]{:S(2)}, u32[]{:S(2)}) collective-permute-start(bf16[2,64,512]{2,1,0:T(8,128)(2,1)S(1)} %get-tuple-element.109), channel_id=1, source_target_pairs={{0,1},{1,2},{2,3},{3,0},{4,5},{5,6},{6,7},{7,4},{8,9},{9,10},{10,1... | collective-permute-start | bytes 393224 | tf_op jit(solution)/shard_map/ppermute | solution.py:33
  103.6 6.4 %collective-permute-start.21 = (bf16[2,64,512]{2,1,0:T(8,128)(2,1)S(1)}, bf16[2,64,512]{2,1,0:T(8,128)(2,1)S(1)}, u32[]{:S(2)}, u32[]{:S(2)}) collective-permute-start(bf16[2,64,512]{2,1,0:T(8,128)(2,1)S(1)} %get-tuple-element.110), channel_id=1, source_target_pairs={{0,3},{1,0},{2,1},{3,2},{4,7},{5,4},{6,5},{7,6},{8,11},{9,8},{10,9... | collective-permute-start | bytes 393224 | tf_op jit(solution)/shard_map/ppermute | solution.py:33
  111.0 9.7 %collective-permute-start.22 = (bf16[6,64,512]{2,1,0:T(8,128)(2,1)S(1)}, bf16[6,64,512]{2,1,0:T(8,128)(2,1)S(1)}, u32[]{:S(2)}, u32[]{:S(2)}) collective-permute-start(bf16[6,64,512]{2,1,0:T(8,128)(2,1)S(1)} %get-tuple-element.112), channel_id=1, source_target_pairs={{0,4},{1,5},{2,6},{3,7},{4,0},{5,1},{6,2},{7,3},{8,12},{9,13},{10,... | collective-permute-start | bytes 1179656 | tf_op jit(solution)/shard_map/ppermute | solution.py:37
  122.3 24.8 %all-to-all-start = ((bf16[8,9,64,128]{3,2,1,0:T(8,128)(2,1)}), bf16[8,9,64,128]{3,2,1,0:T(8,128)(2,1)S(1)}, u32[]{:S(2)}, u32[]{:S(2)}) async-start(bf16[8,9,64,128]{3,2,1,0:T(8,128)(2,1)} %get-tuple-element.122), calls=%async_computation | async-start | bytes 2359296 | tf_op jit(solution)/shard_map/all_to_all | solution.py:41
  130.0 4.7 %collective-permute-start.24 = (bf16[3,64,512]{2,1,0:T(8,128)(2,1)S(1)}, bf16[3,64,512]{2,1,0:T(8,128)(2,1)S(1)}, u32[]{:S(2)}, u32[]{:S(2)}) collective-permute-start(bf16[3,64,512]{2,1,0:T(8,128)(2,1)S(1)} %get-tuple-element.124), channel_id=1, source_target_pairs={{0,120},{8,0},{16,8},{24,16},{32,24},{40,32},{48,40},{56,48},{64,5... | collective-permute-start | bytes 589832 | tf_op jit(solution)/shard_map/ppermute | solution.py:28
  130.0 5.7 %collective-permute-start.25 = (bf16[3,64,512]{2,1,0:T(8,128)(2,1)S(1)}, bf16[3,64,512]{2,1,0:T(8,128)(2,1)S(1)}, u32[]{:S(2)}, u32[]{:S(2)}) collective-permute-start(bf16[3,64,512]{2,1,0:T(8,128)(2,1)S(1)} %get-tuple-element.125), channel_id=1, source_target_pairs={{0,8},{8,16},{16,24},{24,32},{32,40},{40,48},{48,56},{56,64},{64,7... | collective-permute-start | bytes 589832 | tf_op jit(solution)/shard_map/ppermute | solution.py:28
  130.5 14.2 %collective-permute-start.26 = (bf16[3,64,512]{2,1,0:T(8,128)(2,1)S(1)}, bf16[3,64,512]{2,1,0:T(8,128)(2,1)S(1)}, u32[]{:S(2)}, u32[]{:S(2)}) collective-permute-start(bf16[3,64,512]{2,1,0:T(8,128)(2,1)S(1)} %get-tuple-element.126), channel_id=1, source_target_pairs={{0,112},{8,120},{16,0},{24,8},{32,16},{40,24},{48,32},{56,40},{64,... | collective-permute-start | bytes 589832 | tf_op jit(solution)/shard_map/ppermute | solution.py:28
  131.0 13.7 %collective-permute-start.27 = (bf16[3,64,512]{2,1,0:T(8,128)(2,1)S(1)}, bf16[3,64,512]{2,1,0:T(8,128)(2,1)S(1)}, u32[]{:S(2)}, u32[]{:S(2)}) collective-permute-start(bf16[3,64,512]{2,1,0:T(8,128)(2,1)S(1)} %get-tuple-element.127), channel_id=1, source_target_pairs={{0,16},{8,24},{16,32},{24,40},{32,48},{40,56},{48,64},{56,72},{64,... | collective-permute-start | bytes 589832 | tf_op jit(solution)/shard_map/ppermute | solution.py:28

commit v5 on v4

--- a/solution.py
+++ b/solution.py
@@ -79,42 +79,31 @@
         in_specs=[smem, smem, smem],
         out_specs=smem,
         compiler_params=params(),
-        cost_estimate=pl.CostEstimate(flops=115000001, bytes_accessed=300001, transcendentals=0),
+        cost_estimate=pl.CostEstimate(flops=2300000001, bytes_accessed=6000001, transcendentals=0),
         name="make_table",
     )(place, pairs, owner)
 
 
 def select_kernel(start, each, table_ref, blocks_ref, *rest):
-    sends, (held, in_sems, out_sems) = rest[:2], rest[2:]
-    loads, stores = [], []
+    sends, sems = rest[:2], rest[2]
+    copies = []
     for at, send in enumerate(sends):
         for j in range(each):
             n = at * each + j
-            slot = table_ref[FIRST + start + n]
-            loads.append(pltpu.make_async_copy(blocks_ref.at[slot], held.at[n], in_sems.at[n]))
-            stores.append(pltpu.make_async_copy(held.at[n], send.at[j], out_sems.at[n]))
-            loads[-1].start()
-    for load, store in zip(loads, stores):
-        load.wait()
-        store.start()
-    for store in stores:
-        store.wait()
+            copies.append(pltpu.make_async_copy(blocks_ref.at[table_ref[FIRST + start + n]], send.at[j], sems.at[n]))
+            copies[-1].start()
+    for copy in copies:
+        copy.wait()
 
 
 def select(start, each, table, blocks):
     width = blocks.shape[2]
-    count = 2 * each
-    anywhere = pl.BlockSpec(memory_space=pl.ANY)
     return pl.pallas_call(
         lambda *refs: select_kernel(start, each, *refs),
         out_shape=[jax.ShapeDtypeStruct((each, BLK, width), jnp.bfloat16)] * 2,
-        in_specs=[pl.BlockSpec(memory_space=pltpu.SMEM), pl.BlockSpec(memory_space=pltpu.HBM)],
-        out_specs=[anywhere] * 2,
-        scratch_shapes=[
-            pltpu.VMEM((count, BLK, width), jnp.bfloat16),
-            pltpu.SemaphoreType.DMA((count,)),
-            pltpu.SemaphoreType.DMA((count,)),
-        ],
+        in_specs=[pl.BlockSpec(memory_space=pltpu.SMEM), pl.BlockSpec(memory_space=pl.ANY)],
+        out_specs=[pl.BlockSpec(memory_space=pltpu.VMEM)] * 2,
+        scratch_shapes=[pltpu.SemaphoreType.DMA((2 * each,))],
         compiler_params=params(),
         cost_estimate=pl.CostEstimate(flops=115000001, bytes_accessed=300001, transcendentals=0),
         name="select",

time: 153 us -> 150 us (0.980)
  Pallas kernels: 35.3 us -> 32.8 us
  local copies, waits for them, and re-layouts: 3.84 us -> 2.1 us
    pallas_call x3, Pallas kernels: 6.82 us -> 4.25 us  [select(): pl.pallas_call(lambda *refs: select_kernel(start, each, *refs), out_shape...]
    unnamed x12 -> x8, local copies, waits for them, and re-layouts: 3.84 us -> 2.1 us
where the time goes in v5:
time: 150 us; the launch traced here: 147 us
  waiting for transfers between devices  60.4 us (40%)
  starting transfers between devices  50.9 us (34%)
  Pallas kernels  32.8 us (22%)
  local copies, waits for them, and re-layouts  2.1 us (1%)
    ppermute x16, waiting for transfers between devices, along_y(): return lax.ppermute(value, 'pw', pairs)  42.5 us
    ppermute x16, starting transfers between devices, along_y(): return lax.ppermute(value, 'pw', pairs)  24.9 us
    pallas_call x4, Pallas kernels, products(): pl.pallas_call(lambda *refs: products_kernel(count, *refs), out_shape=[ja...  16.4 us
    ppermute x10, waiting for transfers between devices, shifted(): return lax.ppermute(value, 'trans', pairs)  12.4 us
    ppermute x10, starting transfers between devices, shifted(): return lax.ppermute(value, 'trans', pairs)  11 us
    all_to_all x1, starting transfers between devices, exchanged(): return lax.all_to_all(value, 'pw', split_axis=0, concat_axis=0, tiled=True)  7.72 us
    ppermute x2, starting transfers between devices, across_z(): lax.ppermute(value, 'pw', [(source, (source + NY) % NPW) for source in ra...  7.33 us
    pallas_call x3, Pallas kernels, select(): pl.pallas_call(lambda *refs: select_kernel(start, each, *refs), out_shape...  4.25 us
  transfers between devices with their start and end apart: 29, of which 13 were waited for; matrix products, arithmetic and copies ran while one was open for 0% of the time, Pallas kernels for 17%

profile of v5, /device:TPU:6, one launch (start us, length us, event | category | flops | bytes accessed | tf_op | source)
XLA Modules:
  0.0 147.3 jit_solution(4651556215960494728)
XLA Ops:
  0.6 0.1 pad_add_fusion.place_ref
  0.7 0.7 copy-done.1
  1.4 0.7 copy-done.2
  2.1 1.7 %make_table.1.refs_0_.table_ref = s32[56]{0:T(128)S(1)} custom-call(s32[2]{0:T(128)S(1)} %pad_add_fusion.place_ref, s32[2,288]{1,0:T(2,128)S(1)} %bitcast.14, s32[128]{0:T(128)S(1)} %copy-done.2), custom_call_target="tpu_custom_call" | custom-call | flops 2300000000 | bytes 6000001 | tf_op jit(solution)/shard_map/make_table/pallas_call | solution.py:76
  3.8 0.8 copy-done
  4.5 1.9 %select.3 = (bf16[3,512,640]{2,1,0:T(8,128)(2,1)S(1)}, bf16[3,512,640]{2,1,0:T(8,128)(2,1)S(1)}) custom-call(s32[56]{0:T(128)S(1)} %make_table.1.refs_0_.table_ref, bf16[8,512,640]{2,1,0:T(8,128)(2,1)S(1)} %bitcast.6), custom_call_target="tpu_custom_call" | custom-call | flops 115000000 | bytes 300001 | tf_op jit(solution)/shard_map/select/pallas_call | solution.py:101
  6.4 0.1 collective-permute-start
  6.5 1.7 %collective-permute-start.1 = (bf16[3,512,640]{2,1,0:T(8,128)(2,1)S(1)}, bf16[3,512,640]{2,1,0:T(8,128)(2,1)S(1)}, u32[]{:S(2)}, u32[]{:S(2)}) collective-permute-start(bf16[3,512,640]{2,1,0:T(8,128)(2,1)S(1)} %get-tuple-element.67), channel_id=1, source_target_pairs={{0,120},{8,0},{16,8},{24,16},{32,24},{40,32},{48,40},{56,48},{64,5... | collective-permute-start | bytes 5898248 | tf_op jit(solution)/shard_map/ppermute | solution.py:28
  8.2 5.2 %products.4 = (f32[2,6,64,512]{3,2,1,0:T(8,128)S(1)}, f32[6,64,512]{2,1,0:T(8,128)S(1)}, f32[6,64,512]{2,1,0:T(8,128)S(1)}, bf16[2,6,64,512]{3,2,1,0:T(8,128)(2,1)S(1)}, bf16[2,6,64,512]{3,2,1,0:T(8,128)(2,1)S(1)}) custom-call(s32[56]{0:T(128)S(1)} %make_table.1.refs_0_.table_ref, bf16[8,512,640]{2,1,0:T(8,128)(2,1)S(1)} %bitcast.7, ...), custom_call_target="tpu_custom_call" | custom-call | flops 115000000 | bytes 300001 | tf_op jit(solution)/shard_map/products/pallas_call | solution.py:154
  13.5 1.6 %collective-permute-start.2 = (bf16[2,6,64,512]{3,2,1,0:T(8,128)(2,1)S(1)}, bf16[2,6,64,512]{3,2,1,0:T(8,128)(2,1)S(1)}, u32[]{:S(2)}, u32[]{:S(2)}) collective-permute-start(bf16[2,6,64,512]{3,2,1,0:T(8,128)(2,1)S(1)} %get-tuple-element.77), channel_id=1, source_target_pairs={{0,1},{1,2},{2,3},{3,0},{4,5},{5,6},{6,7},{7,4},{8,9},{9,10},{10,1... | collective-permute-start | bytes 2359304 | tf_op jit(solution)/shard_map/ppermute | solution.py:33
  15.1 1.7 %collective-permute-start.3 = (bf16[2,6,64,512]{3,2,1,0:T(8,128)(2,1)S(1)}, bf16[2,6,64,512]{3,2,1,0:T(8,128)(2,1)S(1)}, u32[]{:S(2)}, u32[]{:S(2)}) collective-permute-start(bf16[2,6,64,512]{3,2,1,0:T(8,128)(2,1)S(1)} %get-tuple-element.78), channel_id=1, source_target_pairs={{0,3},{1,0},{2,1},{3,2},{4,7},{5,4},{6,5},{7,6},{8,11},{9,8},{10,9... | collective-permute-start | bytes 2359304 | tf_op jit(solution)/shard_map/ppermute | solution.py:33
  16.8 1.0 select.5
  17.8 1.4 select.4
  19.2 15.3 %collective-permute-done.2.up_got_ref.refs_2_ = bf16[2,6,64,512]{3,2,1,0:T(8,128)(2,1)S(1)} collective-permute-done((bf16[2,6,64,512]{3,2,1,0:T(8,128)(2,1)S(1)}, bf16[2,6,64,512]{3,2,1,0:T(8,128)(2,1)S(1)}, u32[]{:S(2)}, u32[]{:S(2)}) %collective-permute-start.2) | collective-permute-done | bytes 786464 | tf_op jit(solution)/shard_map/ppermute | solution.py:33
  34.5 0.0 collective-permute-done.3.down_got_ref.refs_3_
  34.5 0.2 passed_on.4
  34.7 0.0 collective-permute-done.refs_3_
  34.8 1.6 %collective-permute-start.4 = (bf16[2,512,640]{2,1,0:T(8,128)(2,1)S(1)}, bf16[2,512,640]{2,1,0:T(8,128)(2,1)S(1)}, u32[]{:S(2)}, u32[]{:S(2)}) collective-permute-start(bf16[2,512,640]{2,1,0:T(8,128)(2,1)S(1)} %get-tuple-element.83), channel_id=1, source_target_pairs={{0,16},{8,24},{16,32},{24,40},{32,48},{40,56},{48,64},{56,72},{64,... | collective-permute-start | bytes 3932168 | tf_op jit(solution)/shard_map/ppermute | solution.py:28
  36.3 0.5 collective-permute-start.5
  36.9 5.3 %products.5 = (f32[2,6,64,512]{3,2,1,0:T(8,128)S(1)}, f32[6,64,512]{2,1,0:T(8,128)S(1)}, f32[6,64,512]{2,1,0:T(8,128)S(1)}, bf16[2,6,64,512]{3,2,1,0:T(8,128)(2,1)S(1)}, bf16[2,6,64,512]{3,2,1,0:T(8,128)(2,1)S(1)}) custom-call(s32[56]{0:T(128)S(1)} %make_table.1.refs_0_.table_ref, bf16[8,512,640]{2,1,0:T(8,128)(2,1)S(1)} %bitcast.11, ...), custom_call_target="tpu_custom_call" | custom-call | flops 115000000 | bytes 300001 | tf_op jit(solution)/shard_map/products/pallas_call | solution.py:154
  42.2 1.6 %collective-permute-start.6 = (bf16[2,6,64,512]{3,2,1,0:T(8,128)(2,1)S(1)}, bf16[2,6,64,512]{3,2,1,0:T(8,128)(2,1)S(1)}, u32[]{:S(2)}, u32[]{:S(2)}) collective-permute-start(bf16[2,6,64,512]{3,2,1,0:T(8,128)(2,1)S(1)} %get-tuple-element.87), channel_id=1, source_target_pairs={{0,1},{1,2},{2,3},{3,0},{4,5},{5,6},{6,7},{7,4},{8,9},{9,10},{10,1... | collective-permute-start | bytes 2359304 | tf_op jit(solution)/shard_map/ppermute | solution.py:33
  43.8 1.7 %collective-permute-start.7 = (bf16[2,6,64,512]{3,2,1,0:T(8,128)(2,1)S(1)}, bf16[2,6,64,512]{3,2,1,0:T(8,128)(2,1)S(1)}, u32[]{:S(2)}, u32[]{:S(2)}) collective-permute-start(bf16[2,6,64,512]{3,2,1,0:T(8,128)(2,1)S(1)} %get-tuple-element.88), channel_id=1, source_target_pairs={{0,3},{1,0},{2,1},{3,2},{4,7},{5,4},{6,5},{7,6},{8,11},{9,8},{10,9... | collective-permute-start | bytes 2359304 | tf_op jit(solution)/shard_map/ppermute | solution.py:33
  45.5 0.4 collective-permute-start.8
  45.9 18.1 %collective-permute-done.6.up_got_ref.refs_7_ = bf16[2,6,64,512]{3,2,1,0:T(8,128)(2,1)S(1)} collective-permute-done((bf16[2,6,64,512]{3,2,1,0:T(8,128)(2,1)S(1)}, bf16[2,6,64,512]{3,2,1,0:T(8,128)(2,1)S(1)}, u32[]{:S(2)}, u32[]{:S(2)}) %collective-permute-start.6) | collective-permute-done | bytes 786464 | tf_op jit(solution)/shard_map/ppermute | solution.py:33
  63.9 1.8 %collective-permute-start.9 = (bf16[6,64,512]{2,1,0:T(8,128)(2,1)S(1)}, bf16[6,64,512]{2,1,0:T(8,128)(2,1)S(1)}, u32[]{:S(2)}, u32[]{:S(2)}) collective-permute-start(bf16[6,64,512]{2,1,0:T(8,128)(2,1)S(1)} %get-tuple-element.80), channel_id=1, source_target_pairs={{0,3},{1,0},{2,1},{3,2},{4,7},{5,4},{6,5},{7,6},{8,11},{9,8},{10,9... | collective-permute-start | bytes 1179656 | tf_op jit(solution)/shard_map/ppermute | solution.py:33
  65.7 0.2 passed_on.5
  65.9 0.3 collective-permute-start.16
  66.2 0.0 collective-permute-done.4.refs_3_
  66.2 1.1 collective-permute-done.5.refs_4_
  67.4 2.5 %collective-permute-start.14 = (bf16[1,512,640]{2,1,0:T(8,128)(2,1)S(1)}, bf16[1,512,640]{2,1,0:T(8,128)(2,1)S(1)}, u32[]{:S(2)}, u32[]{:S(2)}) collective-permute-start(bf16[1,512,640]{2,1,0:T(8,128)(2,1)S(1)} %get-tuple-element.100), channel_id=1, source_target_pairs={{0,16},{8,24},{16,32},{24,40},{32,48},{40,56},{48,64},{56,72},{64,... | collective-permute-start | bytes 1966088 | tf_op jit(solution)/shard_map/ppermute | solution.py:28
  69.9 2.5 %collective-permute-done.8.refs_4_ = bf16[6,64,512]{2,1,0:T(8,128)(2,1)S(1)} collective-permute-done((bf16[6,64,512]{2,1,0:T(8,128)(2,1)S(1)}, bf16[6,64,512]{2,1,0:T(8,128)(2,1)S(1)}, u32[]{:S(2)}, u32[]{:S(2)}) %collective-permute-start.8) | collective-permute-done | bytes 393248 | tf_op jit(solution)/shard_map/ppermute | solution.py:33
  72.4 1.8 %collective-permute-start.17 = (bf16[6,64,512]{2,1,0:T(8,128)(2,1)S(1)}, bf16[6,64,512]{2,1,0:T(8,128)(2,1)S(1)}, u32[]{:S(2)}, u32[]{:S(2)}) collective-permute-start(bf16[6,64,512]{2,1,0:T(8,128)(2,1)S(1)} %get-tuple-element.90), channel_id=1, source_target_pairs={{0,3},{1,0},{2,1},{3,2},{4,7},{5,4},{6,5},{7,6},{8,11},{9,8},{10,9... | collective-permute-start | bytes 1179656 | tf_op jit(solution)/shard_map/ppermute | solution.py:33
  74.2 3.7 %products.6 = (f32[2,4,64,512]{3,2,1,0:T(8,128)S(1)}, f32[4,64,512]{2,1,0:T(8,128)S(1)}, f32[4,64,512]{2,1,0:T(8,128)S(1)}, bf16[2,4,64,512]{3,2,1,0:T(8,128)(2,1)S(1)}, bf16[2,4,64,512]{3,2,1,0:T(8,128)(2,1)S(1)}) custom-call(s32[56]{0:T(128)S(1)} %make_table.1.refs_0_.table_ref, bf16[8,512,640]{2,1,0:T(8,128)(2,1)S(1)} %bitcast.12, ...), custom_call_target="tpu_custom_call" | custom-call | flops 115000000 | bytes 300001 | tf_op jit(solution)/shard_map/products/pallas_call | solution.py:154
  77.9 0.3 collective-permute-start.10
  78.2 1.8 %collective-permute-done.16.refs_9_ = bf16[6,64,512]{2,1,0:T(8,128)(2,1)S(1)} collective-permute-done((bf16[6,64,512]{2,1,0:T(8,128)(2,1)S(1)}, bf16[6,64,512]{2,1,0:T(8,128)(2,1)S(1)}, u32[]{:S(2)}, u32[]{:S(2)}) %collective-permute-start.16) | collective-permute-done | bytes 393248 | tf_op jit(solution)/shard_map/ppermute | solution.py:33
  80.0 2.6 %collective-permute-start.11 = (bf16[2,4,64,512]{3,2,1,0:T(8,128)(2,1)S(1)}, bf16[2,4,64,512]{3,2,1,0:T(8,128)(2,1)S(1)}, u32[]{:S(2)}, u32[]{:S(2)}) collective-permute-start(bf16[2,4,64,512]{3,2,1,0:T(8,128)(2,1)S(1)} %get-tuple-element.95), channel_id=1, source_target_pairs={{0,3},{1,0},{2,1},{3,2},{4,7},{5,4},{6,5},{7,6},{8,11},{9,8},{10,9... | collective-permute-start | bytes 1572872 | tf_op jit(solution)/shard_map/ppermute | solution.py:33
  82.6 1.2 collective-permute-done.15.refs_4_
  83.8 2.1 %products.7 = (f32[2,2,64,512]{3,2,1,0:T(8,128)S(1)}, f32[2,64,512]{2,1,0:T(8,128)S(1)}, f32[2,64,512]{2,1,0:T(8,128)S(1)}, bf16[2,2,64,512]{3,2,1,0:T(8,128)(2,1)S(1)}, bf16[2,2,64,512]{3,2,1,0:T(8,128)(2,1)S(1)}) custom-call(s32[56]{0:T(128)S(1)} %make_table.1.refs_0_.table_ref, bf16[8,512,640]{2,1,0:T(8,128)(2,1)S(1)} %bitcast.13, ...), custom_call_target="tpu_custom_call" | custom-call | flops 115000000 | bytes 300001 | tf_op jit(solution)/shard_map/products/pallas_call | solution.py:154
  85.9 1.6 %collective-permute-start.18 = (bf16[2,2,64,512]{3,2,1,0:T(8,128)(2,1)S(1)}, bf16[2,2,64,512]{3,2,1,0:T(8,128)(2,1)S(1)}, u32[]{:S(2)}, u32[]{:S(2)}) collective-permute-start(bf16[2,2,64,512]{3,2,1,0:T(8,128)(2,1)S(1)} %get-tuple-element.105), channel_id=1, source_target_pairs={{0,1},{1,2},{2,3},{3,0},{4,5},{5,6},{6,7},{7,4},{8,9},{9,10},{10,1... | collective-permute-start | bytes 786440 | tf_op jit(solution)/shard_map/ppermute | solution.py:33
  87.5 1.7 %collective-permute-start.19 = (bf16[2,2,64,512]{3,2,1,0:T(8,128)(2,1)S(1)}, bf16[2,2,64,512]{3,2,1,0:T(8,128)(2,1)S(1)}, u32[]{:S(2)}, u32[]{:S(2)}) collective-permute-start(bf16[2,2,64,512]{3,2,1,0:T(8,128)(2,1)S(1)} %get-tuple-element.106), channel_id=1, source_target_pairs={{0,3},{1,0},{2,1},{3,2},{4,7},{5,4},{6,5},{7,6},{8,11},{9,8},{10,9... | collective-permute-start | bytes 786440 | tf_op jit(solution)/shard_map/ppermute | solution.py:33
  89.2 1.7 %plane_sums.3 = (f32[12,64,512]{2,1,0:T(8,128)S(1)}, bf16[12,64,512]{2,1,0:T(8,128)(2,1)S(1)}) custom-call(s32[56]{0:T(128)S(1)} %make_table.1.refs_0_.table_ref, f32[2,6,64,512]{3,2,1,0:T(8,128)S(1)} %get-tuple-element.113.refs_1_, bf16[2,6,64,512]{3,2,1,0:T(8,128)(2,1)S(1)} %collective-permute-done.2.up_got_ref.refs_2_, ...), custom_call_target="tpu_custom_call" | custom-call | flops 115000000 | bytes 300001 | tf_op jit(solution)/shard_map/plane_sums/pallas_call | solution.py:237
  90.8 3.7 %collective-permute-start.23 = (bf16[12,64,512]{2,1,0:T(8,128)(2,1)S(1)}, bf16[12,64,512]{2,1,0:T(8,128)(2,1)S(1)}, u32[]{:S(2)}, u32[]{:S(2)}) collective-permute-start(bf16[12,64,512]{2,1,0:T(8,128)(2,1)S(1)} %get-tuple-element.120), channel_id=1, source_target_pairs={{0,4},{1,5},{2,6},{3,7},{4,0},{5,1},{6,2},{7,3},{8,12},{9,13},{10,... | collective-permute-start | bytes 2359304 | tf_op jit(solution)/shard_map/ppermute | solution.py:37
  94.5 0.5 collective-permute-done.11.down_got_ref.refs_3_
  95.0 0.1 passed_on.6
  95.1 0.1 collective-permute-start.12
  95.2 3.9 %collective-permute-start.13 = (bf16[4,64,512]{2,1,0:T(8,128)(2,1)S(1)}, bf16[4,64,512]{2,1,0:T(8,128)(2,1)S(1)}, u32[]{:S(2)}, u32[]{:S(2)}) collective-permute-start(bf16[4,64,512]{2,1,0:T(8,128)(2,1)S(1)} %get-tuple-element.99), channel_id=1, source_target_pairs={{0,3},{1,0},{2,1},{3,2},{4,7},{5,4},{6,5},{7,6},{8,11},{9,8},{10,9... | collective-permute-start | bytes 786440 | tf_op jit(solution)/shard_map/ppermute | solution.py:33
  99.1 1.4 collective-permute-done.19.down_got_ref.refs_8_
  100.5 0.1 passed_on.7
  100.6 0.1 collective-permute-start.20
  100.7 3.8 %collective-permute-start.21 = (bf16[2,64,512]{2,1,0:T(8,128)(2,1)S(1)}, bf16[2,64,512]{2,1,0:T(8,128)(2,1)S(1)}, u32[]{:S(2)}, u32[]{:S(2)}) collective-permute-start(bf16[2,64,512]{2,1,0:T(8,128)(2,1)S(1)} %get-tuple-element.110), channel_id=1, source_target_pairs={{0,3},{1,0},{2,1},{3,2},{4,7},{5,4},{6,5},{7,6},{8,11},{9,8},{10,9... | collective-permute-start | bytes 393224 | tf_op jit(solution)/shard_map/ppermute | solution.py:33
  104.5 2.9 %collective-permute-done.20.refs_9_ = bf16[2,64,512]{2,1,0:T(8,128)(2,1)S(1)} collective-permute-done((bf16[2,64,512]{2,1,0:T(8,128)(2,1)S(1)}, bf16[2,64,512]{2,1,0:T(8,128)(2,1)S(1)}, u32[]{:S(2)}, u32[]{:S(2)}) %collective-permute-start.20) | collective-permute-done | bytes 131104 | tf_op jit(solution)/shard_map/ppermute | solution.py:33
  107.3 1.0 plane_sums.2
  108.4 3.7 %collective-permute-start.22 = (bf16[6,64,512]{2,1,0:T(8,128)(2,1)S(1)}, bf16[6,64,512]{2,1,0:T(8,128)(2,1)S(1)}, u32[]{:S(2)}, u32[]{:S(2)}) collective-permute-start(bf16[6,64,512]{2,1,0:T(8,128)(2,1)S(1)} %get-tuple-element.112), channel_id=1, source_target_pairs={{0,4},{1,5},{2,6},{3,7},{4,0},{5,1},{6,2},{7,3},{8,12},{9,13},{10,... | collective-permute-start | bytes 1179656 | tf_op jit(solution)/shard_map/ppermute | solution.py:37
  112.1 2.5 %totals.2 = (f32[6,64,512]{2,1,0:T(8,128)S(1)}, bf16[3,64,512]{2,1,0:T(8,128)(2,1)S(1)}, bf16[3,64,512]{2,1,0:T(8,128)(2,1)S(1)}, bf16[8,9,64,128]{3,2,1,0:T(8,128)(2,1)}) custom-call(f32[12,64,512]{2,1,0:T(8,128)S(1)} %get-tuple-element.119.refs_0_, bf16[12,64,512]{2,1,0:T(8,128)(2,1)S(1)} %collective-permute-done.23.refs_1_), custom_call_target="tpu_custom_call" | custom-call | flops 115000000 | bytes 300001 | tf_op jit(solution)/shard_map/totals/pallas_call | solution.py:277
  114.6 3.2 %collective-permute-done.22.refs_1_ = bf16[6,64,512]{2,1,0:T(8,128)(2,1)S(1)} collective-permute-done((bf16[6,64,512]{2,1,0:T(8,128)(2,1)S(1)}, bf16[6,64,512]{2,1,0:T(8,128)(2,1)S(1)}, u32[]{:S(2)}, u32[]{:S(2)}) %collective-permute-start.22) | collective-permute-done | bytes 393248 | tf_op jit(solution)/shard_map/ppermute | solution.py:37
  117.8 1.6 %totals.3 = (bf16[3,64,512]{2,1,0:T(8,128)(2,1)S(1)}, bf16[3,64,512]{2,1,0:T(8,128)(2,1)S(1)}, bf16[8,9,64,128]{3,2,1,0:T(8,128)(2,1)}) custom-call(f32[6,64,512]{2,1,0:T(8,128)S(1)} %get-tuple-element.111.refs_0_, bf16[6,64,512]{2,1,0:T(8,128)(2,1)S(1)} %collective-permute-done.22.refs_1_, ...), custom_call_target="tpu_custom_call", output_to_operand_aliasing={{2}: (2, {})} | custom-call | flops 115000000 | bytes 300001 | tf_op jit(solution)/shard_map/totals/pallas_call | solution.py:277
  119.4 7.7 %all-to-all-start = ((bf16[8,9,64,128]{3,2,1,0:T(8,128)(2,1)}), bf16[8,9,64,128]{3,2,1,0:T(8,128)(2,1)S(1)}, u32[]{:S(2)}, u32[]{:S(2)}) async-start(bf16[8,9,64,128]{3,2,1,0:T(8,128)(2,1)} %get-tuple-element.122), calls=%async_computation | async-start | bytes 2359296 | tf_op jit(solution)/shard_map/all_to_all | solution.py:41
  127.1 0.5 collective-permute-start.25
  127.6 0.5 collective-permute-start.26
  128.1 3.6 %collective-permute-start.27 = (bf16[3,64,512]{2,1,0:T(8,128)(2,1)S(1)}, bf16[3,64,512]{2,1,0:T(8,128)(2,1)S(1)}, u32[]{:S(2)}, u32[]{:S(2)}) collective-permute-start(bf16[3,64,512]{2,1,0:T(8,128)(2,1)S(1)} %get-tuple-element.127), channel_id=1, source_target_pairs={{0,16},{8,24},{16,32},{24,40},{32,48},{40,56},{48,64},{56,72},{64,... | collective-permute-start | bytes 589832 | tf_op jit(solution)/shard_map/ppermute | solution.py:28
  131.7 1.1 collective-permute-done.25.refs_2_
  132.8 9.0 %collective-permute-done.26.refs_3_ = bf16[3,64,512]{2,1,0:T(8,128)(2,1)S(1)} collective-permute-done((bf16[3,64,512]{2,1,0:T(8,128)(2,1)S(1)}, bf16[3,64,512]{2,1,0:T(8,128)(2,1)S(1)}, u32[]{:S(2)}, u32[]{:S(2)}) %collective-permute-start.26) | collective-permute-done | bytes 196640 | tf_op jit(solution)/shard_map/ppermute | solution.py:28
  141.8 2.3 %all-to-all-done.cut_ref = bf16[8,9,64,128]{3,2,1,0:T(8,128)(2,1)S(1)} async-done(((bf16[8,9,64,128]{3,2,1,0:T(8,128)(2,1)}), bf16[8,9,64,128]{3,2,1,0:T(8,128)(2,1)S(1)}, u32[]{:S(2)}, u32[]{:S(2)}) %all-to-all-start) | async-done | bytes 1179680 | tf_op jit(solution)/shard_map/all_to_all | solution.py:41
  144.1 3.0 %finish.1 = (f32[18,64,512]{2,1,0:T(8,128)}, f32[18,64,512]{2,1,0:T(8,128)}) custom-call(s32[56]{0:T(128)S(1)} %make_table.1.refs_0_.table_ref, bf16[8,9,64,128]{3,2,1,0:T(8,128)(2,1)S(1)} %all-to-all-done.cut_ref, f32[6,64,512]{2,1,0:T(8,128)S(1)} %get-tuple-element.123.refs_0_, bf16[3,64,512]{2,1,0:T(8,128)(2,1)S(1)} %collective-permute-done.24.refs_1_, ...), custom_call_target="tpu_custom_call" | custom-call | flops 115000000 | bytes 300001 | tf_op jit(solution)/shard_map/finish/pallas_call | solution.py:323
  (21 shorter events, 0.1 us)
Async XLA Ops:
  0.7 0.7 copy-start.1
  1.4 0.7 copy-start.2
  2.0 2.5 %copy-start = (bf16[4096,640]{1,0:T(8,128)(2,1)S(1)}, bf16[4096,640]{1,0:T(8,128)(2,1)}, u32[]{:S(2)}) copy-start(bf16[4096,640]{1,0:T(8,128)(2,1)} %param.4) | copy-start | bytes 15728644
  4.5 3.7 %copy-start.3 = (f32[640]{0:T(1024)S(1)}, f32[640]{0:T(1024)}, u32[]{:S(2)}) copy-start(f32[640]{0:T(1024)} %param.5) | copy-start | bytes 7684
  6.4 28.3 %collective-permute-start = (bf16[3,512,640]{2,1,0:T(8,128)(2,1)S(1)}, bf16[3,512,640]{2,1,0:T(8,128)(2,1)S(1)}, u32[]{:S(2)}, u32[]{:S(2)}) collective-permute-start(bf16[3,512,640]{2,1,0:T(8,128)(2,1)S(1)} %get-tuple-element.66), channel_id=1, source_target_pairs={{0,8},{8,16},{16,24},{24,32},{32,40},{40,48},{48,56},{56,64},{64,7... | collective-permute-start | bytes 5898248 | tf_op jit(solution)/shard_map/ppermute | solution.py:28
  6.5 28.3 %collective-permute-start.1 = (bf16[3,512,640]{2,1,0:T(8,128)(2,1)S(1)}, bf16[3,512,640]{2,1,0:T(8,128)(2,1)S(1)}, u32[]{:S(2)}, u32[]{:S(2)}) collective-permute-start(bf16[3,512,640]{2,1,0:T(8,128)(2,1)S(1)} %get-tuple-element.67), channel_id=1, source_target_pairs={{0,120},{8,0},{16,8},{24,16},{32,24},{40,32},{48,40},{56,48},{64,5... | collective-permute-start | bytes 5898248 | tf_op jit(solution)/shard_map/ppermute | solution.py:28
  13.5 21.0 %collective-permute-start.2 = (bf16[2,6,64,512]{3,2,1,0:T(8,128)(2,1)S(1)}, bf16[2,6,64,512]{3,2,1,0:T(8,128)(2,1)S(1)}, u32[]{:S(2)}, u32[]{:S(2)}) collective-permute-start(bf16[2,6,64,512]{3,2,1,0:T(8,128)(2,1)S(1)} %get-tuple-element.77), channel_id=1, source_target_pairs={{0,1},{1,2},{2,3},{3,0},{4,5},{5,6},{6,7},{7,4},{8,9},{9,10},{10,1... | collective-permute-start | bytes 2359304 | tf_op jit(solution)/shard_map/ppermute | solution.py:33
  15.1 19.4 %collective-permute-start.3 = (bf16[2,6,64,512]{3,2,1,0:T(8,128)(2,1)S(1)}, bf16[2,6,64,512]{3,2,1,0:T(8,128)(2,1)S(1)}, u32[]{:S(2)}, u32[]{:S(2)}) collective-permute-start(bf16[2,6,64,512]{3,2,1,0:T(8,128)(2,1)S(1)} %get-tuple-element.78), channel_id=1, source_target_pairs={{0,3},{1,0},{2,1},{3,2},{4,7},{5,4},{6,5},{7,6},{8,11},{9,8},{10,9... | collective-permute-start | bytes 2359304 | tf_op jit(solution)/shard_map/ppermute | solution.py:33
  34.8 31.5 %collective-permute-start.4 = (bf16[2,512,640]{2,1,0:T(8,128)(2,1)S(1)}, bf16[2,512,640]{2,1,0:T(8,128)(2,1)S(1)}, u32[]{:S(2)}, u32[]{:S(2)}) collective-permute-start(bf16[2,512,640]{2,1,0:T(8,128)(2,1)S(1)} %get-tuple-element.83), channel_id=1, source_target_pairs={{0,16},{8,24},{16,32},{24,40},{32,48},{40,56},{48,64},{56,72},{64,... | collective-permute-start | bytes 3932168 | tf_op jit(solution)/shard_map/ppermute | solution.py:28
  36.3 31.1 %collective-permute-start.5 = (bf16[2,512,640]{2,1,0:T(8,128)(2,1)S(1)}, bf16[2,512,640]{2,1,0:T(8,128)(2,1)S(1)}, u32[]{:S(2)}, u32[]{:S(2)}) collective-permute-start(bf16[2,512,640]{2,1,0:T(8,128)(2,1)S(1)} %get-tuple-element.84), channel_id=1, source_target_pairs={{0,112},{8,120},{16,0},{24,8},{32,16},{40,24},{48,32},{56,40},{64,... | collective-permute-start | bytes 3932168 | tf_op jit(solution)/shard_map/ppermute | solution.py:28
  42.2 21.8 %collective-permute-start.6 = (bf16[2,6,64,512]{3,2,1,0:T(8,128)(2,1)S(1)}, bf16[2,6,64,512]{3,2,1,0:T(8,128)(2,1)S(1)}, u32[]{:S(2)}, u32[]{:S(2)}) collective-permute-start(bf16[2,6,64,512]{3,2,1,0:T(8,128)(2,1)S(1)} %get-tuple-element.87), channel_id=1, source_target_pairs={{0,1},{1,2},{2,3},{3,0},{4,5},{5,6},{6,7},{7,4},{8,9},{9,10},{10,1... | collective-permute-start | bytes 2359304 | tf_op jit(solution)/shard_map/ppermute | solution.py:33
  43.8 21.9 %collective-permute-start.7 = (bf16[2,6,64,512]{3,2,1,0:T(8,128)(2,1)S(1)}, bf16[2,6,64,512]{3,2,1,0:T(8,128)(2,1)S(1)}, u32[]{:S(2)}, u32[]{:S(2)}) collective-permute-start(bf16[2,6,64,512]{3,2,1,0:T(8,128)(2,1)S(1)} %get-tuple-element.88), channel_id=1, source_target_pairs={{0,3},{1,0},{2,1},{3,2},{4,7},{5,4},{6,5},{7,6},{8,11},{9,8},{10,9... | collective-permute-start | bytes 2359304 | tf_op jit(solution)/shard_map/ppermute | solution.py:33
  45.5 26.9 %collective-permute-start.8 = (bf16[6,64,512]{2,1,0:T(8,128)(2,1)S(1)}, bf16[6,64,512]{2,1,0:T(8,128)(2,1)S(1)}, u32[]{:S(2)}, u32[]{:S(2)}) collective-permute-start(bf16[6,64,512]{2,1,0:T(8,128)(2,1)S(1)} %get-tuple-element.79), channel_id=1, source_target_pairs={{0,1},{1,2},{2,3},{3,0},{4,5},{5,6},{6,7},{7,4},{8,9},{9,10},{10,1... | collective-permute-start | bytes 1179656 | tf_op jit(solution)/shard_map/ppermute | solution.py:33
  63.9 10.2 %collective-permute-start.9 = (bf16[6,64,512]{2,1,0:T(8,128)(2,1)S(1)}, bf16[6,64,512]{2,1,0:T(8,128)(2,1)S(1)}, u32[]{:S(2)}, u32[]{:S(2)}) collective-permute-start(bf16[6,64,512]{2,1,0:T(8,128)(2,1)S(1)} %get-tuple-element.80), channel_id=1, source_target_pairs={{0,3},{1,0},{2,1},{3,2},{4,7},{5,4},{6,5},{7,6},{8,11},{9,8},{10,9... | collective-permute-start | bytes 1179656 | tf_op jit(solution)/shard_map/ppermute | solution.py:33
  65.9 14.1 %collective-permute-start.16 = (bf16[6,64,512]{2,1,0:T(8,128)(2,1)S(1)}, bf16[6,64,512]{2,1,0:T(8,128)(2,1)S(1)}, u32[]{:S(2)}, u32[]{:S(2)}) collective-permute-start(bf16[6,64,512]{2,1,0:T(8,128)(2,1)S(1)} %get-tuple-element.89), channel_id=1, source_target_pairs={{0,1},{1,2},{2,3},{3,0},{4,5},{5,6},{6,7},{7,4},{8,9},{9,10},{10,1... | collective-permute-start | bytes 1179656 | tf_op jit(solution)/shard_map/ppermute | solution.py:33
  67.4 15.2 %collective-permute-start.14 = (bf16[1,512,640]{2,1,0:T(8,128)(2,1)S(1)}, bf16[1,512,640]{2,1,0:T(8,128)(2,1)S(1)}, u32[]{:S(2)}, u32[]{:S(2)}) collective-permute-start(bf16[1,512,640]{2,1,0:T(8,128)(2,1)S(1)} %get-tuple-element.100), channel_id=1, source_target_pairs={{0,16},{8,24},{16,32},{24,40},{32,48},{40,56},{48,64},{56,72},{64,... | collective-permute-start | bytes 1966088 | tf_op jit(solution)/shard_map/ppermute | solution.py:28
  69.8 13.9 %collective-permute-start.15 = (bf16[1,512,640]{2,1,0:T(8,128)(2,1)S(1)}, bf16[1,512,640]{2,1,0:T(8,128)(2,1)S(1)}, u32[]{:S(2)}, u32[]{:S(2)}) collective-permute-start(bf16[1,512,640]{2,1,0:T(8,128)(2,1)S(1)} %get-tuple-element.101), channel_id=1, source_target_pairs={{0,112},{8,120},{16,0},{24,8},{32,16},{40,24},{48,32},{56,40},{64,... | collective-permute-start | bytes 1966088 | tf_op jit(solution)/shard_map/ppermute | solution.py:28
  72.4 10.2 %collective-permute-start.17 = (bf16[6,64,512]{2,1,0:T(8,128)(2,1)S(1)}, bf16[6,64,512]{2,1,0:T(8,128)(2,1)S(1)}, u32[]{:S(2)}, u32[]{:S(2)}) collective-permute-start(bf16[6,64,512]{2,1,0:T(8,128)(2,1)S(1)} %get-tuple-element.90), channel_id=1, source_target_pairs={{0,3},{1,0},{2,1},{3,2},{4,7},{5,4},{6,5},{7,6},{8,11},{9,8},{10,9... | collective-permute-start | bytes 1179656 | tf_op jit(solution)/shard_map/ppermute | solution.py:33
  77.9 16.6 %collective-permute-start.10 = (bf16[2,4,64,512]{3,2,1,0:T(8,128)(2,1)S(1)}, bf16[2,4,64,512]{3,2,1,0:T(8,128)(2,1)S(1)}, u32[]{:S(2)}, u32[]{:S(2)}) collective-permute-start(bf16[2,4,64,512]{3,2,1,0:T(8,128)(2,1)S(1)} %get-tuple-element.94), channel_id=1, source_target_pairs={{0,1},{1,2},{2,3},{3,0},{4,5},{5,6},{6,7},{7,4},{8,9},{9,10},{10,1... | collective-permute-start | bytes 1572872 | tf_op jit(solution)/shard_map/ppermute | solution.py:33
  80.0 14.9 %collective-permute-start.11 = (bf16[2,4,64,512]{3,2,1,0:T(8,128)(2,1)S(1)}, bf16[2,4,64,512]{3,2,1,0:T(8,128)(2,1)S(1)}, u32[]{:S(2)}, u32[]{:S(2)}) collective-permute-start(bf16[2,4,64,512]{3,2,1,0:T(8,128)(2,1)S(1)} %get-tuple-element.95), channel_id=1, source_target_pairs={{0,3},{1,0},{2,1},{3,2},{4,7},{5,4},{6,5},{7,6},{8,11},{9,8},{10,9... | collective-permute-start | bytes 1572872 | tf_op jit(solution)/shard_map/ppermute | solution.py:33
  85.9 13.3 %collective-permute-start.18 = (bf16[2,2,64,512]{3,2,1,0:T(8,128)(2,1)S(1)}, bf16[2,2,64,512]{3,2,1,0:T(8,128)(2,1)S(1)}, u32[]{:S(2)}, u32[]{:S(2)}) collective-permute-start(bf16[2,2,64,512]{3,2,1,0:T(8,128)(2,1)S(1)} %get-tuple-element.105), channel_id=1, source_target_pairs={{0,1},{1,2},{2,3},{3,0},{4,5},{5,6},{6,7},{7,4},{8,9},{9,10},{10,1... | collective-permute-start | bytes 786440 | tf_op jit(solution)/shard_map/ppermute | solution.py:33
  87.5 13.0 %collective-permute-start.19 = (bf16[2,2,64,512]{3,2,1,0:T(8,128)(2,1)S(1)}, bf16[2,2,64,512]{3,2,1,0:T(8,128)(2,1)S(1)}, u32[]{:S(2)}, u32[]{:S(2)}) collective-permute-start(bf16[2,2,64,512]{3,2,1,0:T(8,128)(2,1)S(1)} %get-tuple-element.106), channel_id=1, source_target_pairs={{0,3},{1,0},{2,1},{3,2},{4,7},{5,4},{6,5},{7,6},{8,11},{9,8},{10,9... | collective-permute-start | bytes 786440 | tf_op jit(solution)/shard_map/ppermute | solution.py:33
  90.8 21.2 %collective-permute-start.23 = (bf16[12,64,512]{2,1,0:T(8,128)(2,1)S(1)}, bf16[12,64,512]{2,1,0:T(8,128)(2,1)S(1)}, u32[]{:S(2)}, u32[]{:S(2)}) collective-permute-start(bf16[12,64,512]{2,1,0:T(8,128)(2,1)S(1)} %get-tuple-element.120), channel_id=1, source_target_pairs={{0,4},{1,5},{2,6},{3,7},{4,0},{5,1},{6,2},{7,3},{8,12},{9,13},{10,... | collective-permute-start | bytes 2359304 | tf_op jit(solution)/shard_map/ppermute | solution.py:37
  95.1 9.3 %collective-permute-start.12 = (bf16[4,64,512]{2,1,0:T(8,128)(2,1)S(1)}, bf16[4,64,512]{2,1,0:T(8,128)(2,1)S(1)}, u32[]{:S(2)}, u32[]{:S(2)}) collective-permute-start(bf16[4,64,512]{2,1,0:T(8,128)(2,1)S(1)} %get-tuple-element.98), channel_id=1, source_target_pairs={{0,1},{1,2},{2,3},{3,0},{4,5},{5,6},{6,7},{7,4},{8,9},{9,10},{10,1... | collective-permute-start | bytes 786440 | tf_op jit(solution)/shard_map/ppermute | solution.py:33
  95.2 9.3 %collective-permute-start.13 = (bf16[4,64,512]{2,1,0:T(8,128)(2,1)S(1)}, bf16[4,64,512]{2,1,0:T(8,128)(2,1)S(1)}, u32[]{:S(2)}, u32[]{:S(2)}) collective-permute-start(bf16[4,64,512]{2,1,0:T(8,128)(2,1)S(1)} %get-tuple-element.99), channel_id=1, source_target_pairs={{0,3},{1,0},{2,1},{3,2},{4,7},{5,4},{6,5},{7,6},{8,11},{9,8},{10,9... | collective-permute-start | bytes 786440 | tf_op jit(solution)/shard_map/ppermute | solution.py:33
  100.6 6.7 %collective-permute-start.20 = (bf16[2,64,512]{2,1,0:T(8,128)(2,1)S(1)}, bf16[2,64,512]{2,1,0:T(8,128)(2,1)S(1)}, u32[]{:S(2)}, u32[]{:S(2)}) collective-permute-start(bf16[2,64,512]{2,1,0:T(8,128)(2,1)S(1)} %get-tuple-element.109), channel_id=1, source_target_pairs={{0,1},{1,2},{2,3},{3,0},{4,5},{5,6},{6,7},{7,4},{8,9},{9,10},{10,1... | collective-permute-start | bytes 393224 | tf_op jit(solution)/shard_map/ppermute | solution.py:33
  100.7 6.6 %collective-permute-start.21 = (bf16[2,64,512]{2,1,0:T(8,128)(2,1)S(1)}, bf16[2,64,512]{2,1,0:T(8,128)(2,1)S(1)}, u32[]{:S(2)}, u32[]{:S(2)}) collective-permute-start(bf16[2,64,512]{2,1,0:T(8,128)(2,1)S(1)} %get-tuple-element.110), channel_id=1, source_target_pairs={{0,3},{1,0},{2,1},{3,2},{4,7},{5,4},{6,5},{7,6},{8,11},{9,8},{10,9... | collective-permute-start | bytes 393224 | tf_op jit(solution)/shard_map/ppermute | solution.py:33
  108.4 9.4 %collective-permute-start.22 = (bf16[6,64,512]{2,1,0:T(8,128)(2,1)S(1)}, bf16[6,64,512]{2,1,0:T(8,128)(2,1)S(1)}, u32[]{:S(2)}, u32[]{:S(2)}) collective-permute-start(bf16[6,64,512]{2,1,0:T(8,128)(2,1)S(1)} %get-tuple-element.112), channel_id=1, source_target_pairs={{0,4},{1,5},{2,6},{3,7},{4,0},{5,1},{6,2},{7,3},{8,12},{9,13},{10,... | collective-permute-start | bytes 1179656 | tf_op jit(solution)/shard_map/ppermute | solution.py:37
  119.4 24.8 %all-to-all-start = ((bf16[8,9,64,128]{3,2,1,0:T(8,128)(2,1)}), bf16[8,9,64,128]{3,2,1,0:T(8,128)(2,1)S(1)}, u32[]{:S(2)}, u32[]{:S(2)}) async-start(bf16[8,9,64,128]{3,2,1,0:T(8,128)(2,1)} %get-tuple-element.122), calls=%async_computation | async-start | bytes 2359296 | tf_op jit(solution)/shard_map/all_to_all | solution.py:41
  127.1 4.7 %collective-permute-start.24 = (bf16[3,64,512]{2,1,0:T(8,128)(2,1)S(1)}, bf16[3,64,512]{2,1,0:T(8,128)(2,1)S(1)}, u32[]{:S(2)}, u32[]{:S(2)}) collective-permute-start(bf16[3,64,512]{2,1,0:T(8,128)(2,1)S(1)} %get-tuple-element.124), channel_id=1, source_target_pairs={{0,120},{8,0},{16,8},{24,16},{32,24},{40,32},{48,40},{56,48},{64,5... | collective-permute-start | bytes 589832 | tf_op jit(solution)/shard_map/ppermute | solution.py:28
  127.1 5.7 %collective-permute-start.25 = (bf16[3,64,512]{2,1,0:T(8,128)(2,1)S(1)}, bf16[3,64,512]{2,1,0:T(8,128)(2,1)S(1)}, u32[]{:S(2)}, u32[]{:S(2)}) collective-permute-start(bf16[3,64,512]{2,1,0:T(8,128)(2,1)S(1)} %get-tuple-element.125), channel_id=1, source_target_pairs={{0,8},{8,16},{16,24},{24,32},{32,40},{40,48},{48,56},{56,64},{64,7... | collective-permute-start | bytes 589832 | tf_op jit(solution)/shard_map/ppermute | solution.py:28
  127.6 14.2 %collective-permute-start.26 = (bf16[3,64,512]{2,1,0:T(8,128)(2,1)S(1)}, bf16[3,64,512]{2,1,0:T(8,128)(2,1)S(1)}, u32[]{:S(2)}, u32[]{:S(2)}) collective-permute-start(bf16[3,64,512]{2,1,0:T(8,128)(2,1)S(1)} %get-tuple-element.126), channel_id=1, source_target_pairs={{0,112},{8,120},{16,0},{24,8},{32,16},{40,24},{48,32},{56,40},{64,... | collective-permute-start | bytes 589832 | tf_op jit(solution)/shard_map/ppermute | solution.py:28
  128.1 13.7 %collective-permute-start.27 = (bf16[3,64,512]{2,1,0:T(8,128)(2,1)S(1)}, bf16[3,64,512]{2,1,0:T(8,128)(2,1)S(1)}, u32[]{:S(2)}, u32[]{:S(2)}) collective-permute-start(bf16[3,64,512]{2,1,0:T(8,128)(2,1)S(1)} %get-tuple-element.127), channel_id=1, source_target_pairs={{0,16},{8,24},{16,32},{24,40},{32,48},{40,56},{48,64},{56,72},{64,... | collective-permute-start | bytes 589832 | tf_op jit(solution)/shard_map/ppermute | solution.py:28

commit v6 on v5

--- a/solution.py
+++ b/solution.py
@@ -79,7 +79,7 @@
         in_specs=[smem, smem, smem],
         out_specs=smem,
         compiler_params=params(),
-        cost_estimate=pl.CostEstimate(flops=2300000001, bytes_accessed=6000001, transcendentals=0),
+        cost_estimate=pl.CostEstimate(flops=3450000001, bytes_accessed=9000001, transcendentals=0),
         name="make_table",
     )(place, pairs, owner)
 
@@ -105,54 +105,58 @@
         out_specs=[pl.BlockSpec(memory_space=pltpu.VMEM)] * 2,
         scratch_shapes=[pltpu.SemaphoreType.DMA((2 * each,))],
         compiler_params=params(),
-        cost_estimate=pl.CostEstimate(flops=115000001, bytes_accessed=300001, transcendentals=0),
+        cost_estimate=pl.CostEstimate(flops=1150000001, bytes_accessed=3000001, transcendentals=0),
         name="select",
     )(table, blocks)
 
 
-def products_kernel(count, table_ref, right_ref, coulomb_ref, *refs):
+def products_kernel(start, count, table_ref, blocks_ref, coulomb_ref, *refs):
     lefts, (own_ref, up_add_ref, down_add_ref, up_ref, down_ref, weighted_ref) = refs[:-6], refs[-6:]
-    each = count // len(lefts)
+    each = count // max(len(lefts), 1)
     y = table_ref[YAT]
-    for at, left_ref in enumerate(lefts):
-
-        @pl.when(pl.program_id(0) // each == at)
-        def _():
-            for dy in range(NY):
-                for z in range(NZ):
-                    to = (dy * NZ + z) * ROWS
-                    source = z * (NY * ROWS) + ((y + dy) & (NY - 1)) * ROWS
-                    rows = left_ref[0, pl.ds(pl.multiple_of(source, ROWS), ROWS), :]
-                    weighted_ref[to : to + ROWS, :] = (rows.astype(jnp.float32) * coulomb_ref[...]).astype(jnp.bfloat16)
-
-    part = lax.dot_general(
-        weighted_ref[...], right_ref[0], (((1,), (1,)), ((), ())), preferred_element_type=jnp.float32
-    ).reshape(NY, NZ, 1, ROWS, BLK)
-    own_ref[...] = part[0]
-    up_add_ref[...] = part[1, 0]
-    up_ref[0] = part[2, 0].astype(jnp.bfloat16)
-    up_ref[1] = part[1, 1].astype(jnp.bfloat16)
-    down_ref[0] = part[3, 0].astype(jnp.bfloat16)
-    down_ref[1] = part[2, 1].astype(jnp.bfloat16)
-    down_add_ref[...] = part[3, 1]
+
+    def pair(i, left_ref, left_at):
+        for dy in range(NY):
+            for z in range(NZ):
+                to = (dy * NZ + z) * ROWS
+                source = z * (NY * ROWS) + ((y + dy) & (NY - 1)) * ROWS
+                rows = left_ref[left_at, pl.ds(pl.multiple_of(source, ROWS), ROWS), :]
+                weighted_ref[to : to + ROWS, :] = (rows.astype(jnp.float32) * coulomb_ref[...]).astype(jnp.bfloat16)
+        part = lax.dot_general(
+            weighted_ref[...],
+            blocks_ref[table_ref[SECOND + start + i]],
+            (((1,), (1,)), ((), ())),
+            preferred_element_type=jnp.float32,
+        ).reshape(NY, NZ, ROWS, BLK)
+        own_ref[0, i] = part[0, 0]
+        own_ref[1, i] = part[0, 1]
+        up_add_ref[i] = part[1, 0]
+        up_ref[0, i] = part[2, 0].astype(jnp.bfloat16)
+        up_ref[1, i] = part[1, 1].astype(jnp.bfloat16)
+        down_ref[0, i] = part[3, 0].astype(jnp.bfloat16)
+        down_ref[1, i] = part[2, 1].astype(jnp.bfloat16)
+        down_add_ref[i] = part[3, 1]
+
+    if lefts:
+        for at, left_ref in enumerate(lefts):
+
+            @pl.loop(0, each)
+            def _(j):
+                pair(at * each + j, left_ref, j)
+    else:
+
+        @pl.loop(0, count)
+        def _(i):
+            pair(i, blocks_ref, table_ref[FIRST + start + i])
 
 
 def products(table, blocks, coulomb, lefts, start, count):
     width = blocks.shape[2]
-    each = count // len(lefts)
-    if lefts[0].shape[0] == STORED:
-        left_specs = [pl.BlockSpec((1, BLK, width), lambda i, table: (table[FIRST + start + i], 0, 0))]
-    else:
-        left_specs = [
-            pl.BlockSpec((1, BLK, width), lambda i, table, at=at: (jnp.clip(i - at * each, 0, each - 1), 0, 0))
-            for at in range(len(lefts))
-        ]
     half = (count, ROWS, BLK)
-    half_spec = pl.BlockSpec((1, ROWS, BLK), lambda i, table: (i, 0, 0))
     whole = (NZ, count, ROWS, BLK)
-    whole_spec = pl.BlockSpec((NZ, 1, ROWS, BLK), lambda i, table: (0, i, 0, 0))
-    return pl.pallas_call(
-        lambda *refs: products_kernel(count, *refs),
+    vmem = pl.BlockSpec(memory_space=pltpu.VMEM)
+    return pl.pallas_call(
+        lambda *refs: products_kernel(start, count, *refs),
         out_shape=[
             jax.ShapeDtypeStruct(whole, jnp.float32),
             jax.ShapeDtypeStruct(half, jnp.float32),
@@ -160,19 +164,11 @@
             jax.ShapeDtypeStruct(whole, jnp.bfloat16),
             jax.ShapeDtypeStruct(whole, jnp.bfloat16),
         ],
-        grid_spec=pltpu.PrefetchScalarGridSpec(
-            num_scalar_prefetch=1,
-            grid=(count,),
-            in_specs=[
-                pl.BlockSpec((1, BLK, width), lambda i, table: (table[SECOND + start + i], 0, 0)),
-                pl.BlockSpec((1, width), lambda i, table: (0, 0)),
-                *left_specs,
-            ],
-            out_specs=[whole_spec, half_spec, half_spec, whole_spec, whole_spec],
-            scratch_shapes=[pltpu.VMEM((BLK, width), jnp.bfloat16)],
-        ),
-        compiler_params=params(),
-        cost_estimate=pl.CostEstimate(flops=115000001, bytes_accessed=300001, transcendentals=0),
+        in_specs=[pl.BlockSpec(memory_space=pltpu.SMEM)] + [vmem] * (2 + len(lefts)),
+        out_specs=[vmem] * 5,
+        scratch_shapes=[pltpu.VMEM((BLK, width), jnp.bfloat16)],
+        compiler_params=params(),
+        cost_estimate=pl.CostEstimate(flops=1150000001, bytes_accessed=3000001, transcendentals=0),
         name="products",
     )(table, blocks, coulomb, *lefts)
 
@@ -198,7 +194,7 @@
         ],
         out_specs=[half, half],
         compiler_params=params(),
-        cost_estimate=pl.CostEstimate(flops=115000001, bytes_accessed=300001, transcendentals=0),
+        cost_estimate=pl.CostEstimate(flops=1150000001, bytes_accessed=3000001, transcendentals=0),
         name="passed_on",
     )(up_add, down_add, up_got, down_got)
 
@@ -247,7 +243,7 @@
             out_specs=[pl.BlockSpec((each, ROWS, BLK), lambda i, table: (i, 0, 0))] * 2,
         ),
         compiler_params=params(),
-        cost_estimate=pl.CostEstimate(flops=115000001, bytes_accessed=300001, transcendentals=0),
+        cost_estimate=pl.CostEstimate(flops=1150000001, bytes_accessed=3000001, transcendentals=0),
         name="plane_sums",
     )(table, *[part for group in groups for part in group])
 
@@ -283,7 +279,7 @@
         + [pl.BlockSpec((NPW, 1, ROWS, 2 * ROWS), lambda i: (0, at // 2 + i, 0, 0))],
         input_output_aliases={2: len(outs)} if carried else {},
         compiler_params=params(),
-        cost_estimate=pl.CostEstimate(flops=115000001, bytes_accessed=300001, transcendentals=0),
+        cost_estimate=pl.CostEstimate(flops=1150000001, bytes_accessed=3000001, transcendentals=0),
         name="totals",
     )(keep, got, *carried)
 
@@ -330,7 +326,7 @@
             pltpu.SemaphoreType.DMA((2 * LISTED,)),
         ],
         compiler_params=params(),
-        cost_estimate=pl.CostEstimate(flops=115000001, bytes_accessed=300001, transcendentals=0),
+        cost_estimate=pl.CostEstimate(flops=1150000001, bytes_accessed=3000001, transcendentals=0),
         name="finish",
     )(table, cut, *results)
 
@@ -357,7 +353,7 @@
     near = select(NEAR_AT, 3, table, blocks)
     (ready,) = after((table,), near)
     near = [shifted(send, step) for step, send in zip((1, -1), near)]
-    local = begin([blocks], 0, LOCAL, ready)
+    local = begin([], 0, LOCAL, ready)
     (ready,) = after((ready,), local[:1])
     far, last = select(FAR_AT, 2, ready, blocks), select(LAST_AT, 1, ready, blocks)
     own, up_add, down_add, up, down = local

time: 150 us -> 151 us (level); the launches traced: 147 us -> 150 us
  waiting for transfers between devices: 60.4 us -> 69.6 us
  Pallas kernels: 32.8 us -> 29.6 us
  starting transfers between devices: 50.9 us -> 47.9 us
    all_to_all x1, waiting for transfers between devices: 2.32 us -> 7 us  [exchanged(): return lax.all_to_all(value, 'pw', split_axis=0, concat_axis=0, tiled=True)]
    ppermute x10, waiting for transfers between devices: 12.4 us -> 16.7 us  [shifted(): return lax.ppermute(value, 'trans', pairs)]
    pallas_call x4, Pallas kernels: 16.4 us -> 13.3 us  [products(): pl.pallas_call(lambda *refs: products_kernel(start, count, *refs), out_sh...]
    ppermute x2, waiting for transfers between devices: 3.23 us -> 5.33 us  [across_z(): lax.ppermute(value, 'pw', [(source, (source + NY) % NPW) for source in ra...]
    ppermute x16, waiting for transfers between devices: 42.5 us -> 40.6 us  [along_y(): return lax.ppermute(value, 'pw', pairs)]
    ppermute x16, starting transfers between devices: 24.9 us -> 23.1 us  [along_y(): return lax.ppermute(value, 'pw', pairs)]
  transfers between devices with their start and end apart: 29 -> 29, of which waited for: 13 -> 18; matrix products, arithmetic and copies ran while one was open for 0% -> 0% of each run, Pallas kernels for 17% -> 14%
where the time goes in v6:
time: 151 us; the launch traced here: 150 us
  waiting for transfers between devices  69.6 us (46%)
  starting transfers between devices  47.9 us (32%)
  Pallas kernels  29.6 us (20%)
  local copies, waits for them, and re-layouts  2.1 us (1%)
    ppermute x16, waiting for transfers between devices, along_y(): return lax.ppermute(value, 'pw', pairs)  40.6 us
    ppermute x16, starting transfers between devices, along_y(): return lax.ppermute(value, 'pw', pairs)  23.1 us
    ppermute x10, waiting for transfers between devices, shifted(): return lax.ppermute(value, 'trans', pairs)  16.7 us
    pallas_call x4, Pallas kernels, products(): pl.pallas_call(lambda *refs: products_kernel(start, count, *refs), out_sh...  13.3 us
    ppermute x10, starting transfers between devices, shifted(): return lax.ppermute(value, 'trans', pairs)  10.6 us
    ppermute x2, starting transfers between devices, across_z(): lax.ppermute(value, 'pw', [(source, (source + NY) % NPW) for source in ra...  7.58 us
    all_to_all x1, waiting for transfers between devices, exchanged(): return lax.all_to_all(value, 'pw', split_axis=0, concat_axis=0, tiled=True)  7 us
    all_to_all x1, starting transfers between devices, exchanged(): return lax.all_to_all(value, 'pw', split_axis=0, concat_axis=0, tiled=True)  6.7 us
  transfers between devices with their start and end apart: 29, of which 18 were waited for; matrix products, arithmetic and copies ran while one was open for 0% of the time, Pallas kernels for 14%

profile of v6, /device:TPU:6, one launch (start us, length us, event | category | flops | bytes accessed | tf_op | source)
XLA Modules:
  0.0 150.3 jit_solution(9203473225149208097)
XLA Ops:
  0.6 0.1 pad_add_fusion.place_ref
  0.7 0.7 copy-done.1
  1.4 0.7 copy-done.2
  2.1 1.7 %make_table.1.refs_0_.table_ref = s32[56]{0:T(128)S(1)} custom-call(s32[2]{0:T(128)S(1)} %pad_add_fusion.place_ref, s32[2,288]{1,0:T(2,128)S(1)} %bitcast.13, s32[128]{0:T(128)S(1)} %copy-done.2), custom_call_target="tpu_custom_call" | custom-call | flops 3450000128 | bytes 9000001 | tf_op jit(solution)/shard_map/make_table/pallas_call | solution.py:76
  3.8 0.8 copy-done
  4.5 1.9 %select.3 = (bf16[3,512,640]{2,1,0:T(8,128)(2,1)S(1)}, bf16[3,512,640]{2,1,0:T(8,128)(2,1)S(1)}) custom-call(s32[56]{0:T(128)S(1)} %make_table.1.refs_0_.table_ref, bf16[8,512,640]{2,1,0:T(8,128)(2,1)S(1)} %bitcast.6), custom_call_target="tpu_custom_call" | custom-call | flops 1150000000 | bytes 3000001 | tf_op jit(solution)/shard_map/select/pallas_call | solution.py:101
  6.5 1.7 %collective-permute-start.1 = (bf16[3,512,640]{2,1,0:T(8,128)(2,1)S(1)}, bf16[3,512,640]{2,1,0:T(8,128)(2,1)S(1)}, u32[]{:S(2)}, u32[]{:S(2)}) collective-permute-start(bf16[3,512,640]{2,1,0:T(8,128)(2,1)S(1)} %get-tuple-element.67), channel_id=1, source_target_pairs={{0,120},{8,0},{16,8},{24,16},{32,24},{40,32},{48,40},{56,48},{64,5... | collective-permute-start | bytes 5898248 | tf_op jit(solution)/shard_map/ppermute | solution.py:28
  8.2 4.3 %products.4 = (f32[2,6,64,512]{3,2,1,0:T(8,128)S(1)}, f32[6,64,512]{2,1,0:T(8,128)S(1)}, f32[6,64,512]{2,1,0:T(8,128)S(1)}, bf16[2,6,64,512]{3,2,1,0:T(8,128)(2,1)S(1)}, bf16[2,6,64,512]{3,2,1,0:T(8,128)(2,1)S(1)}) custom-call(s32[56]{0:T(128)S(1)} %make_table.1.refs_0_.table_ref, bf16[8,512,640]{2,1,0:T(8,128)(2,1)S(1)} %bitcast.7, ...), custom_call_target="tpu_custom_call" | custom-call | flops 1150000000 | bytes 3000001 | tf_op jit(solution)/shard_map/products/pallas_call | solution.py:158
  12.5 1.6 %collective-permute-start.2 = (bf16[2,6,64,512]{3,2,1,0:T(8,128)(2,1)S(1)}, bf16[2,6,64,512]{3,2,1,0:T(8,128)(2,1)S(1)}, u32[]{:S(2)}, u32[]{:S(2)}) collective-permute-start(bf16[2,6,64,512]{3,2,1,0:T(8,128)(2,1)S(1)} %get-tuple-element.77), channel_id=1, source_target_pairs={{0,1},{1,2},{2,3},{3,0},{4,5},{5,6},{6,7},{7,4},{8,9},{9,10},{10,1... | collective-permute-start | bytes 2359304 | tf_op jit(solution)/shard_map/ppermute | solution.py:33
  14.2 1.7 %collective-permute-start.3 = (bf16[2,6,64,512]{3,2,1,0:T(8,128)(2,1)S(1)}, bf16[2,6,64,512]{3,2,1,0:T(8,128)(2,1)S(1)}, u32[]{:S(2)}, u32[]{:S(2)}) collective-permute-start(bf16[2,6,64,512]{3,2,1,0:T(8,128)(2,1)S(1)} %get-tuple-element.78), channel_id=1, source_target_pairs={{0,3},{1,0},{2,1},{3,2},{4,7},{5,4},{6,5},{7,6},{8,11},{9,8},{10,9... | collective-permute-start | bytes 2359304 | tf_op jit(solution)/shard_map/ppermute | solution.py:33
  15.8 1.0 select.5
  16.8 1.4 select.4
  18.3 15.3 %collective-permute-done.2.up_got_ref.refs_2_ = bf16[2,6,64,512]{3,2,1,0:T(8,128)(2,1)S(1)} collective-permute-done((bf16[2,6,64,512]{3,2,1,0:T(8,128)(2,1)S(1)}, bf16[2,6,64,512]{3,2,1,0:T(8,128)(2,1)S(1)}, u32[]{:S(2)}, u32[]{:S(2)}) %collective-permute-start.2) | collective-permute-done | bytes 786464 | tf_op jit(solution)/shard_map/ppermute | solution.py:33
  33.6 0.2 passed_on.4
  33.8 1.6 %collective-permute-start.4 = (bf16[2,512,640]{2,1,0:T(8,128)(2,1)S(1)}, bf16[2,512,640]{2,1,0:T(8,128)(2,1)S(1)}, u32[]{:S(2)}, u32[]{:S(2)}) collective-permute-start(bf16[2,512,640]{2,1,0:T(8,128)(2,1)S(1)} %get-tuple-element.83), channel_id=1, source_target_pairs={{0,16},{8,24},{16,32},{24,40},{32,48},{40,56},{48,64},{56,72},{64,... | collective-permute-start | bytes 3932168 | tf_op jit(solution)/shard_map/ppermute | solution.py:28
  35.4 0.5 collective-permute-start.5
  35.9 4.3 %products.5 = (f32[2,6,64,512]{3,2,1,0:T(8,128)S(1)}, f32[6,64,512]{2,1,0:T(8,128)S(1)}, f32[6,64,512]{2,1,0:T(8,128)S(1)}, bf16[2,6,64,512]{3,2,1,0:T(8,128)(2,1)S(1)}, bf16[2,6,64,512]{3,2,1,0:T(8,128)(2,1)S(1)}) custom-call(s32[56]{0:T(128)S(1)} %make_table.1.refs_0_.table_ref, bf16[8,512,640]{2,1,0:T(8,128)(2,1)S(1)} %bitcast.10, ...), custom_call_target="tpu_custom_call" | custom-call | flops 1150000000 | bytes 3000001 | tf_op jit(solution)/shard_map/products/pallas_call | solution.py:158
  40.2 1.7 %collective-permute-start.6 = (bf16[2,6,64,512]{3,2,1,0:T(8,128)(2,1)S(1)}, bf16[2,6,64,512]{3,2,1,0:T(8,128)(2,1)S(1)}, u32[]{:S(2)}, u32[]{:S(2)}) collective-permute-start(bf16[2,6,64,512]{3,2,1,0:T(8,128)(2,1)S(1)} %get-tuple-element.87), channel_id=1, source_target_pairs={{0,1},{1,2},{2,3},{3,0},{4,5},{5,6},{6,7},{7,4},{8,9},{9,10},{10,1... | collective-permute-start | bytes 2359304 | tf_op jit(solution)/shard_map/ppermute | solution.py:33
  41.9 1.7 %collective-permute-start.7 = (bf16[2,6,64,512]{3,2,1,0:T(8,128)(2,1)S(1)}, bf16[2,6,64,512]{3,2,1,0:T(8,128)(2,1)S(1)}, u32[]{:S(2)}, u32[]{:S(2)}) collective-permute-start(bf16[2,6,64,512]{3,2,1,0:T(8,128)(2,1)S(1)} %get-tuple-element.88), channel_id=1, source_target_pairs={{0,3},{1,0},{2,1},{3,2},{4,7},{5,4},{6,5},{7,6},{8,11},{9,8},{10,9... | collective-permute-start | bytes 2359304 | tf_op jit(solution)/shard_map/ppermute | solution.py:33
  43.5 0.4 collective-permute-start.8
  43.9 18.0 %collective-permute-done.6.up_got_ref.refs_7_ = bf16[2,6,64,512]{3,2,1,0:T(8,128)(2,1)S(1)} collective-permute-done((bf16[2,6,64,512]{3,2,1,0:T(8,128)(2,1)S(1)}, bf16[2,6,64,512]{3,2,1,0:T(8,128)(2,1)S(1)}, u32[]{:S(2)}, u32[]{:S(2)}) %collective-permute-start.6) | collective-permute-done | bytes 786464 | tf_op jit(solution)/shard_map/ppermute | solution.py:33
  61.9 1.8 %collective-permute-start.9 = (bf16[6,64,512]{2,1,0:T(8,128)(2,1)S(1)}, bf16[6,64,512]{2,1,0:T(8,128)(2,1)S(1)}, u32[]{:S(2)}, u32[]{:S(2)}) collective-permute-start(bf16[6,64,512]{2,1,0:T(8,128)(2,1)S(1)} %get-tuple-element.80), channel_id=1, source_target_pairs={{0,3},{1,0},{2,1},{3,2},{4,7},{5,4},{6,5},{7,6},{8,11},{9,8},{10,9... | collective-permute-start | bytes 1179656 | tf_op jit(solution)/shard_map/ppermute | solution.py:33
  63.7 0.2 passed_on.5
  63.9 0.3 collective-permute-start.16
  64.2 1.1 collective-permute-done.4.refs_3_
  65.3 2.1 %collective-permute-done.5.refs_4_ = bf16[2,512,640]{2,1,0:T(8,128)(2,1)S(1)} collective-permute-done((bf16[2,512,640]{2,1,0:T(8,128)(2,1)S(1)}, bf16[2,512,640]{2,1,0:T(8,128)(2,1)S(1)}, u32[]{:S(2)}, u32[]{:S(2)}) %collective-permute-start.5) | collective-permute-done | bytes 1310752 | tf_op jit(solution)/shard_map/ppermute | solution.py:28
  67.4 0.5 collective-permute-start.14
  67.9 1.5 %collective-permute-start.15 = (bf16[1,512,640]{2,1,0:T(8,128)(2,1)S(1)}, bf16[1,512,640]{2,1,0:T(8,128)(2,1)S(1)}, u32[]{:S(2)}, u32[]{:S(2)}) collective-permute-start(bf16[1,512,640]{2,1,0:T(8,128)(2,1)S(1)} %get-tuple-element.101), channel_id=1, source_target_pairs={{0,112},{8,120},{16,0},{24,8},{32,16},{40,24},{48,32},{56,40},{64,... | collective-permute-start | bytes 1966088 | tf_op jit(solution)/shard_map/ppermute | solution.py:28
  69.4 0.9 collective-permute-done.8.refs_4_
  70.3 2.1 %collective-permute-start.17 = (bf16[6,64,512]{2,1,0:T(8,128)(2,1)S(1)}, bf16[6,64,512]{2,1,0:T(8,128)(2,1)S(1)}, u32[]{:S(2)}, u32[]{:S(2)}) collective-permute-start(bf16[6,64,512]{2,1,0:T(8,128)(2,1)S(1)} %get-tuple-element.90), channel_id=1, source_target_pairs={{0,3},{1,0},{2,1},{3,2},{4,7},{5,4},{6,5},{7,6},{8,11},{9,8},{10,9... | collective-permute-start | bytes 1179656 | tf_op jit(solution)/shard_map/ppermute | solution.py:33
  72.4 3.1 %products.6 = (f32[2,4,64,512]{3,2,1,0:T(8,128)S(1)}, f32[4,64,512]{2,1,0:T(8,128)S(1)}, f32[4,64,512]{2,1,0:T(8,128)S(1)}, bf16[2,4,64,512]{3,2,1,0:T(8,128)(2,1)S(1)}, bf16[2,4,64,512]{3,2,1,0:T(8,128)(2,1)S(1)}) custom-call(s32[56]{0:T(128)S(1)} %make_table.1.refs_0_.table_ref, bf16[8,512,640]{2,1,0:T(8,128)(2,1)S(1)} %bitcast.11, ...), custom_call_target="tpu_custom_call" | custom-call | flops 1150000000 | bytes 3000001 | tf_op jit(solution)/shard_map/products/pallas_call | solution.py:158
  75.5 0.1 collective-permute-start.10
  75.6 3.0 %collective-permute-done.16.refs_9_ = bf16[6,64,512]{2,1,0:T(8,128)(2,1)S(1)} collective-permute-done((bf16[6,64,512]{2,1,0:T(8,128)(2,1)S(1)}, bf16[6,64,512]{2,1,0:T(8,128)(2,1)S(1)}, u32[]{:S(2)}, u32[]{:S(2)}) %collective-permute-start.16) | collective-permute-done | bytes 393248 | tf_op jit(solution)/shard_map/ppermute | solution.py:33
  78.6 1.9 %collective-permute-start.11 = (bf16[2,4,64,512]{3,2,1,0:T(8,128)(2,1)S(1)}, bf16[2,4,64,512]{3,2,1,0:T(8,128)(2,1)S(1)}, u32[]{:S(2)}, u32[]{:S(2)}) collective-permute-start(bf16[2,4,64,512]{3,2,1,0:T(8,128)(2,1)S(1)} %get-tuple-element.95), channel_id=1, source_target_pairs={{0,3},{1,0},{2,1},{3,2},{4,7},{5,4},{6,5},{7,6},{8,11},{9,8},{10,9... | collective-permute-start | bytes 1572872 | tf_op jit(solution)/shard_map/ppermute | solution.py:33
  80.5 1.8 %collective-permute-done.14.refs_3_ = bf16[1,512,640]{2,1,0:T(8,128)(2,1)S(1)} collective-permute-done((bf16[1,512,640]{2,1,0:T(8,128)(2,1)S(1)}, bf16[1,512,640]{2,1,0:T(8,128)(2,1)S(1)}, u32[]{:S(2)}, u32[]{:S(2)}) %collective-permute-start.14) | collective-permute-done | bytes 655392 | tf_op jit(solution)/shard_map/ppermute | solution.py:28
  82.3 2.4 %collective-permute-done.15.refs_4_ = bf16[1,512,640]{2,1,0:T(8,128)(2,1)S(1)} collective-permute-done((bf16[1,512,640]{2,1,0:T(8,128)(2,1)S(1)}, bf16[1,512,640]{2,1,0:T(8,128)(2,1)S(1)}, u32[]{:S(2)}, u32[]{:S(2)}) %collective-permute-start.15) | collective-permute-done | bytes 655392 | tf_op jit(solution)/shard_map/ppermute | solution.py:28
  84.7 1.6 %products.7 = (f32[2,2,64,512]{3,2,1,0:T(8,128)S(1)}, f32[2,64,512]{2,1,0:T(8,128)S(1)}, f32[2,64,512]{2,1,0:T(8,128)S(1)}, bf16[2,2,64,512]{3,2,1,0:T(8,128)(2,1)S(1)}, bf16[2,2,64,512]{3,2,1,0:T(8,128)(2,1)S(1)}) custom-call(s32[56]{0:T(128)S(1)} %make_table.1.refs_0_.table_ref, bf16[8,512,640]{2,1,0:T(8,128)(2,1)S(1)} %bitcast.12, ...), custom_call_target="tpu_custom_call" | custom-call | flops 1150000000 | bytes 3000001 | tf_op jit(solution)/shard_map/products/pallas_call | solution.py:158
  86.3 1.6 %collective-permute-start.18 = (bf16[2,2,64,512]{3,2,1,0:T(8,128)(2,1)S(1)}, bf16[2,2,64,512]{3,2,1,0:T(8,128)(2,1)S(1)}, u32[]{:S(2)}, u32[]{:S(2)}) collective-permute-start(bf16[2,2,64,512]{3,2,1,0:T(8,128)(2,1)S(1)} %get-tuple-element.105), channel_id=1, source_target_pairs={{0,1},{1,2},{2,3},{3,0},{4,5},{5,6},{6,7},{7,4},{8,9},{9,10},{10,1... | collective-permute-start | bytes 786440 | tf_op jit(solution)/shard_map/ppermute | solution.py:33
  88.0 1.7 %collective-permute-start.19 = (bf16[2,2,64,512]{3,2,1,0:T(8,128)(2,1)S(1)}, bf16[2,2,64,512]{3,2,1,0:T(8,128)(2,1)S(1)}, u32[]{:S(2)}, u32[]{:S(2)}) collective-permute-start(bf16[2,2,64,512]{3,2,1,0:T(8,128)(2,1)S(1)} %get-tuple-element.106), channel_id=1, source_target_pairs={{0,3},{1,0},{2,1},{3,2},{4,7},{5,4},{6,5},{7,6},{8,11},{9,8},{10,9... | collective-permute-start | bytes 786440 | tf_op jit(solution)/shard_map/ppermute | solution.py:33
  89.6 1.6 %plane_sums.3 = (f32[12,64,512]{2,1,0:T(8,128)S(1)}, bf16[12,64,512]{2,1,0:T(8,128)(2,1)S(1)}) custom-call(s32[56]{0:T(128)S(1)} %make_table.1.refs_0_.table_ref, f32[2,6,64,512]{3,2,1,0:T(8,128)S(1)} %get-tuple-element.113.refs_1_, bf16[2,6,64,512]{3,2,1,0:T(8,128)(2,1)S(1)} %collective-permute-done.2.up_got_ref.refs_2_, ...), custom_call_target="tpu_custom_call" | custom-call | flops 1150000000 | bytes 3000001 | tf_op jit(solution)/shard_map/plane_sums/pallas_call | solution.py:233
  91.2 3.8 %collective-permute-start.23 = (bf16[12,64,512]{2,1,0:T(8,128)(2,1)S(1)}, bf16[12,64,512]{2,1,0:T(8,128)(2,1)S(1)}, u32[]{:S(2)}, u32[]{:S(2)}) collective-permute-start(bf16[12,64,512]{2,1,0:T(8,128)(2,1)S(1)} %get-tuple-element.120), channel_id=1, source_target_pairs={{0,4},{1,5},{2,6},{3,7},{4,0},{5,1},{6,2},{7,3},{8,12},{9,13},{10,... | collective-permute-start | bytes 2359304 | tf_op jit(solution)/shard_map/ppermute | solution.py:37
  95.1 0.2 passed_on.6
  95.3 0.4 collective-permute-start.12
  95.7 2.9 %collective-permute-start.13 = (bf16[4,64,512]{2,1,0:T(8,128)(2,1)S(1)}, bf16[4,64,512]{2,1,0:T(8,128)(2,1)S(1)}, u32[]{:S(2)}, u32[]{:S(2)}) collective-permute-start(bf16[4,64,512]{2,1,0:T(8,128)(2,1)S(1)} %get-tuple-element.99), channel_id=1, source_target_pairs={{0,3},{1,0},{2,1},{3,2},{4,7},{5,4},{6,5},{7,6},{8,11},{9,8},{10,9... | collective-permute-start | bytes 786440 | tf_op jit(solution)/shard_map/ppermute | solution.py:33
  98.6 0.1 collective-permute-done.19.down_got_ref.refs_8_
  98.8 0.1 collective-permute-start.20
  98.8 3.2 %collective-permute-start.21 = (bf16[2,64,512]{2,1,0:T(8,128)(2,1)S(1)}, bf16[2,64,512]{2,1,0:T(8,128)(2,1)S(1)}, u32[]{:S(2)}, u32[]{:S(2)}) collective-permute-start(bf16[2,64,512]{2,1,0:T(8,128)(2,1)S(1)} %get-tuple-element.110), channel_id=1, source_target_pairs={{0,3},{1,0},{2,1},{3,2},{4,7},{5,4},{6,5},{7,6},{8,11},{9,8},{10,9... | collective-permute-start | bytes 393224 | tf_op jit(solution)/shard_map/ppermute | solution.py:33
  102.1 1.0 collective-permute-done.12.refs_4_
  103.0 0.9 collective-permute-done.13.refs_5_
  103.9 1.1 collective-permute-done.20.refs_9_
  105.0 0.3 collective-permute-done.21.refs_10_
  105.3 1.1 plane_sums.2
  106.4 3.7 %collective-permute-start.22 = (bf16[6,64,512]{2,1,0:T(8,128)(2,1)S(1)}, bf16[6,64,512]{2,1,0:T(8,128)(2,1)S(1)}, u32[]{:S(2)}, u32[]{:S(2)}) collective-permute-start(bf16[6,64,512]{2,1,0:T(8,128)(2,1)S(1)} %get-tuple-element.112), channel_id=1, source_target_pairs={{0,4},{1,5},{2,6},{3,7},{4,0},{5,1},{6,2},{7,3},{8,12},{9,13},{10,... | collective-permute-start | bytes 1179656 | tf_op jit(solution)/shard_map/ppermute | solution.py:37
  110.1 0.1 collective-permute-done.23.refs_1_
  110.2 2.5 %totals.2 = (f32[6,64,512]{2,1,0:T(8,128)S(1)}, bf16[3,64,512]{2,1,0:T(8,128)(2,1)S(1)}, bf16[3,64,512]{2,1,0:T(8,128)(2,1)S(1)}, bf16[8,9,64,128]{3,2,1,0:T(8,128)(2,1)}) custom-call(f32[12,64,512]{2,1,0:T(8,128)S(1)} %get-tuple-element.119.refs_0_, bf16[12,64,512]{2,1,0:T(8,128)(2,1)S(1)} %collective-permute-done.23.refs_1_), custom_call_target="tpu_custom_call" | custom-call | flops 1150000000 | bytes 3000001 | tf_op jit(solution)/shard_map/totals/pallas_call | solution.py:273
  112.8 5.2 %collective-permute-done.22.refs_1_ = bf16[6,64,512]{2,1,0:T(8,128)(2,1)S(1)} collective-permute-done((bf16[6,64,512]{2,1,0:T(8,128)(2,1)S(1)}, bf16[6,64,512]{2,1,0:T(8,128)(2,1)S(1)}, u32[]{:S(2)}, u32[]{:S(2)}) %collective-permute-start.22) | collective-permute-done | bytes 393248 | tf_op jit(solution)/shard_map/ppermute | solution.py:37
  118.0 1.6 %totals.3 = (bf16[3,64,512]{2,1,0:T(8,128)(2,1)S(1)}, bf16[3,64,512]{2,1,0:T(8,128)(2,1)S(1)}, bf16[8,9,64,128]{3,2,1,0:T(8,128)(2,1)}) custom-call(f32[6,64,512]{2,1,0:T(8,128)S(1)} %get-tuple-element.111.refs_0_, bf16[6,64,512]{2,1,0:T(8,128)(2,1)S(1)} %collective-permute-done.22.refs_1_, ...), custom_call_target="tpu_custom_call", output_to_operand_aliasing={{2}: (2, {})} | custom-call | flops 1150000000 | bytes 3000001 | tf_op jit(solution)/shard_map/totals/pallas_call | solution.py:273
  119.6 6.7 %all-to-all-start = ((bf16[8,9,64,128]{3,2,1,0:T(8,128)(2,1)}), bf16[8,9,64,128]{3,2,1,0:T(8,128)(2,1)S(1)}, u32[]{:S(2)}, u32[]{:S(2)}) async-start(bf16[8,9,64,128]{3,2,1,0:T(8,128)(2,1)} %get-tuple-element.122), calls=%async_computation | async-start | bytes 2359296 | tf_op jit(solution)/shard_map/all_to_all | solution.py:41
  126.3 0.5 collective-permute-start.25
  126.8 4.1 %collective-permute-start.27 = (bf16[3,64,512]{2,1,0:T(8,128)(2,1)S(1)}, bf16[3,64,512]{2,1,0:T(8,128)(2,1)S(1)}, u32[]{:S(2)}, u32[]{:S(2)}) collective-permute-start(bf16[3,64,512]{2,1,0:T(8,128)(2,1)S(1)} %get-tuple-element.127), channel_id=1, source_target_pairs={{0,16},{8,24},{16,32},{24,40},{32,48},{40,56},{48,64},{56,72},{64,... | collective-permute-start | bytes 589832 | tf_op jit(solution)/shard_map/ppermute | solution.py:28
  130.9 1.6 %collective-permute-done.25.refs_2_ = bf16[3,64,512]{2,1,0:T(8,128)(2,1)S(1)} collective-permute-done((bf16[3,64,512]{2,1,0:T(8,128)(2,1)S(1)}, bf16[3,64,512]{2,1,0:T(8,128)(2,1)S(1)}, u32[]{:S(2)}, u32[]{:S(2)}) %collective-permute-start.25) | collective-permute-done | bytes 196640 | tf_op jit(solution)/shard_map/ppermute | solution.py:28
  132.5 7.6 %collective-permute-done.26.refs_3_ = bf16[3,64,512]{2,1,0:T(8,128)(2,1)S(1)} collective-permute-done((bf16[3,64,512]{2,1,0:T(8,128)(2,1)S(1)}, bf16[3,64,512]{2,1,0:T(8,128)(2,1)S(1)}, u32[]{:S(2)}, u32[]{:S(2)}) %collective-permute-start.26) | collective-permute-done | bytes 196640 | tf_op jit(solution)/shard_map/ppermute | solution.py:28
  140.2 7.0 %all-to-all-done.cut_ref = bf16[8,9,64,128]{3,2,1,0:T(8,128)(2,1)S(1)} async-done(((bf16[8,9,64,128]{3,2,1,0:T(8,128)(2,1)}), bf16[8,9,64,128]{3,2,1,0:T(8,128)(2,1)S(1)}, u32[]{:S(2)}, u32[]{:S(2)}) %all-to-all-start) | async-done | bytes 1179680 | tf_op jit(solution)/shard_map/all_to_all | solution.py:41
  147.2 3.0 %finish.1 = (f32[18,64,512]{2,1,0:T(8,128)}, f32[18,64,512]{2,1,0:T(8,128)}) custom-call(s32[56]{0:T(128)S(1)} %make_table.1.refs_0_.table_ref, bf16[8,9,64,128]{3,2,1,0:T(8,128)(2,1)S(1)} %all-to-all-done.cut_ref, f32[6,64,512]{2,1,0:T(8,128)S(1)} %get-tuple-element.123.refs_0_, bf16[3,64,512]{2,1,0:T(8,128)(2,1)S(1)} %collective-permute-done.24.refs_1_, ...), custom_call_target="tpu_custom_call" | custom-call | flops 1150000000 | bytes 3000001 | tf_op jit(solution)/shard_map/finish/pallas_call | solution.py:319
  (21 shorter events, 0.2 us)
Async XLA Ops:
  0.7 0.7 copy-start.1
  1.4 0.7 copy-start.2
  2.0 2.5 %copy-start = (bf16[4096,640]{1,0:T(8,128)(2,1)S(1)}, bf16[4096,640]{1,0:T(8,128)(2,1)}, u32[]{:S(2)}) copy-start(bf16[4096,640]{1,0:T(8,128)(2,1)} %param.4) | copy-start | bytes 15728644
  4.5 3.7 %copy-start.3 = (f32[640]{0:T(1024)S(1)}, f32[640]{0:T(1024)}, u32[]{:S(2)}) copy-start(f32[640]{0:T(1024)} %param.5) | copy-start | bytes 7684
  6.4 27.4 %collective-permute-start = (bf16[3,512,640]{2,1,0:T(8,128)(2,1)S(1)}, bf16[3,512,640]{2,1,0:T(8,128)(2,1)S(1)}, u32[]{:S(2)}, u32[]{:S(2)}) collective-permute-start(bf16[3,512,640]{2,1,0:T(8,128)(2,1)S(1)} %get-tuple-element.66), channel_id=1, source_target_pairs={{0,8},{8,16},{16,24},{24,32},{32,40},{40,48},{48,56},{56,64},{64,7... | collective-permute-start | bytes 5898248 | tf_op jit(solution)/shard_map/ppermute | solution.py:28
  6.5 27.3 %collective-permute-start.1 = (bf16[3,512,640]{2,1,0:T(8,128)(2,1)S(1)}, bf16[3,512,640]{2,1,0:T(8,128)(2,1)S(1)}, u32[]{:S(2)}, u32[]{:S(2)}) collective-permute-start(bf16[3,512,640]{2,1,0:T(8,128)(2,1)S(1)} %get-tuple-element.67), channel_id=1, source_target_pairs={{0,120},{8,0},{16,8},{24,16},{32,24},{40,32},{48,40},{56,48},{64,5... | collective-permute-start | bytes 5898248 | tf_op jit(solution)/shard_map/ppermute | solution.py:28
  12.5 21.0 %collective-permute-start.2 = (bf16[2,6,64,512]{3,2,1,0:T(8,128)(2,1)S(1)}, bf16[2,6,64,512]{3,2,1,0:T(8,128)(2,1)S(1)}, u32[]{:S(2)}, u32[]{:S(2)}) collective-permute-start(bf16[2,6,64,512]{3,2,1,0:T(8,128)(2,1)S(1)} %get-tuple-element.77), channel_id=1, source_target_pairs={{0,1},{1,2},{2,3},{3,0},{4,5},{5,6},{6,7},{7,4},{8,9},{9,10},{10,1... | collective-permute-start | bytes 2359304 | tf_op jit(solution)/shard_map/ppermute | solution.py:33
  14.2 19.4 %collective-permute-start.3 = (bf16[2,6,64,512]{3,2,1,0:T(8,128)(2,1)S(1)}, bf16[2,6,64,512]{3,2,1,0:T(8,128)(2,1)S(1)}, u32[]{:S(2)}, u32[]{:S(2)}) collective-permute-start(bf16[2,6,64,512]{3,2,1,0:T(8,128)(2,1)S(1)} %get-tuple-element.78), channel_id=1, source_target_pairs={{0,3},{1,0},{2,1},{3,2},{4,7},{5,4},{6,5},{7,6},{8,11},{9,8},{10,9... | collective-permute-start | bytes 2359304 | tf_op jit(solution)/shard_map/ppermute | solution.py:33
  33.8 31.5 %collective-permute-start.4 = (bf16[2,512,640]{2,1,0:T(8,128)(2,1)S(1)}, bf16[2,512,640]{2,1,0:T(8,128)(2,1)S(1)}, u32[]{:S(2)}, u32[]{:S(2)}) collective-permute-start(bf16[2,512,640]{2,1,0:T(8,128)(2,1)S(1)} %get-tuple-element.83), channel_id=1, source_target_pairs={{0,16},{8,24},{16,32},{24,40},{32,48},{40,56},{48,64},{56,72},{64,... | collective-permute-start | bytes 3932168 | tf_op jit(solution)/shard_map/ppermute | solution.py:28
  35.4 32.0 %collective-permute-start.5 = (bf16[2,512,640]{2,1,0:T(8,128)(2,1)S(1)}, bf16[2,512,640]{2,1,0:T(8,128)(2,1)S(1)}, u32[]{:S(2)}, u32[]{:S(2)}) collective-permute-start(bf16[2,512,640]{2,1,0:T(8,128)(2,1)S(1)} %get-tuple-element.84), channel_id=1, source_target_pairs={{0,112},{8,120},{16,0},{24,8},{32,16},{40,24},{48,32},{56,40},{64,... | collective-permute-start | bytes 3932168 | tf_op jit(solution)/shard_map/ppermute | solution.py:28
  40.2 21.7 %collective-permute-start.6 = (bf16[2,6,64,512]{3,2,1,0:T(8,128)(2,1)S(1)}, bf16[2,6,64,512]{3,2,1,0:T(8,128)(2,1)S(1)}, u32[]{:S(2)}, u32[]{:S(2)}) collective-permute-start(bf16[2,6,64,512]{3,2,1,0:T(8,128)(2,1)S(1)} %get-tuple-element.87), channel_id=1, source_target_pairs={{0,1},{1,2},{2,3},{3,0},{4,5},{5,6},{6,7},{7,4},{8,9},{9,10},{10,1... | collective-permute-start | bytes 2359304 | tf_op jit(solution)/shard_map/ppermute | solution.py:33
  41.9 21.8 %collective-permute-start.7 = (bf16[2,6,64,512]{3,2,1,0:T(8,128)(2,1)S(1)}, bf16[2,6,64,512]{3,2,1,0:T(8,128)(2,1)S(1)}, u32[]{:S(2)}, u32[]{:S(2)}) collective-permute-start(bf16[2,6,64,512]{3,2,1,0:T(8,128)(2,1)S(1)} %get-tuple-element.88), channel_id=1, source_target_pairs={{0,3},{1,0},{2,1},{3,2},{4,7},{5,4},{6,5},{7,6},{8,11},{9,8},{10,9... | collective-permute-start | bytes 2359304 | tf_op jit(solution)/shard_map/ppermute | solution.py:33
  43.5 26.8 %collective-permute-start.8 = (bf16[6,64,512]{2,1,0:T(8,128)(2,1)S(1)}, bf16[6,64,512]{2,1,0:T(8,128)(2,1)S(1)}, u32[]{:S(2)}, u32[]{:S(2)}) collective-permute-start(bf16[6,64,512]{2,1,0:T(8,128)(2,1)S(1)} %get-tuple-element.79), channel_id=1, source_target_pairs={{0,1},{1,2},{2,3},{3,0},{4,5},{5,6},{6,7},{7,4},{8,9},{9,10},{10,1... | collective-permute-start | bytes 1179656 | tf_op jit(solution)/shard_map/ppermute | solution.py:33
  61.9 10.6 %collective-permute-start.9 = (bf16[6,64,512]{2,1,0:T(8,128)(2,1)S(1)}, bf16[6,64,512]{2,1,0:T(8,128)(2,1)S(1)}, u32[]{:S(2)}, u32[]{:S(2)}) collective-permute-start(bf16[6,64,512]{2,1,0:T(8,128)(2,1)S(1)} %get-tuple-element.80), channel_id=1, source_target_pairs={{0,3},{1,0},{2,1},{3,2},{4,7},{5,4},{6,5},{7,6},{8,11},{9,8},{10,9... | collective-permute-start | bytes 1179656 | tf_op jit(solution)/shard_map/ppermute | solution.py:33
  63.9 14.7 %collective-permute-start.16 = (bf16[6,64,512]{2,1,0:T(8,128)(2,1)S(1)}, bf16[6,64,512]{2,1,0:T(8,128)(2,1)S(1)}, u32[]{:S(2)}, u32[]{:S(2)}) collective-permute-start(bf16[6,64,512]{2,1,0:T(8,128)(2,1)S(1)} %get-tuple-element.89), channel_id=1, source_target_pairs={{0,1},{1,2},{2,3},{3,0},{4,5},{5,6},{6,7},{7,4},{8,9},{9,10},{10,1... | collective-permute-start | bytes 1179656 | tf_op jit(solution)/shard_map/ppermute | solution.py:33
  67.4 14.9 %collective-permute-start.14 = (bf16[1,512,640]{2,1,0:T(8,128)(2,1)S(1)}, bf16[1,512,640]{2,1,0:T(8,128)(2,1)S(1)}, u32[]{:S(2)}, u32[]{:S(2)}) collective-permute-start(bf16[1,512,640]{2,1,0:T(8,128)(2,1)S(1)} %get-tuple-element.100), channel_id=1, source_target_pairs={{0,16},{8,24},{16,32},{24,40},{32,48},{40,56},{48,64},{56,72},{64,... | collective-permute-start | bytes 1966088 | tf_op jit(solution)/shard_map/ppermute | solution.py:28
  67.9 16.8 %collective-permute-start.15 = (bf16[1,512,640]{2,1,0:T(8,128)(2,1)S(1)}, bf16[1,512,640]{2,1,0:T(8,128)(2,1)S(1)}, u32[]{:S(2)}, u32[]{:S(2)}) collective-permute-start(bf16[1,512,640]{2,1,0:T(8,128)(2,1)S(1)} %get-tuple-element.101), channel_id=1, source_target_pairs={{0,112},{8,120},{16,0},{24,8},{32,16},{40,24},{48,32},{56,40},{64,... | collective-permute-start | bytes 1966088 | tf_op jit(solution)/shard_map/ppermute | solution.py:28
  70.3 10.2 %collective-permute-start.17 = (bf16[6,64,512]{2,1,0:T(8,128)(2,1)S(1)}, bf16[6,64,512]{2,1,0:T(8,128)(2,1)S(1)}, u32[]{:S(2)}, u32[]{:S(2)}) collective-permute-start(bf16[6,64,512]{2,1,0:T(8,128)(2,1)S(1)} %get-tuple-element.90), channel_id=1, source_target_pairs={{0,3},{1,0},{2,1},{3,2},{4,7},{5,4},{6,5},{7,6},{8,11},{9,8},{10,9... | collective-permute-start | bytes 1179656 | tf_op jit(solution)/shard_map/ppermute | solution.py:33
  75.5 19.6 %collective-permute-start.10 = (bf16[2,4,64,512]{3,2,1,0:T(8,128)(2,1)S(1)}, bf16[2,4,64,512]{3,2,1,0:T(8,128)(2,1)S(1)}, u32[]{:S(2)}, u32[]{:S(2)}) collective-permute-start(bf16[2,4,64,512]{3,2,1,0:T(8,128)(2,1)S(1)} %get-tuple-element.94), channel_id=1, source_target_pairs={{0,1},{1,2},{2,3},{3,0},{4,5},{5,6},{6,7},{7,4},{8,9},{9,10},{10,1... | collective-permute-start | bytes 1572872 | tf_op jit(solution)/shard_map/ppermute | solution.py:33
  78.6 16.5 %collective-permute-start.11 = (bf16[2,4,64,512]{3,2,1,0:T(8,128)(2,1)S(1)}, bf16[2,4,64,512]{3,2,1,0:T(8,128)(2,1)S(1)}, u32[]{:S(2)}, u32[]{:S(2)}) collective-permute-start(bf16[2,4,64,512]{3,2,1,0:T(8,128)(2,1)S(1)} %get-tuple-element.95), channel_id=1, source_target_pairs={{0,3},{1,0},{2,1},{3,2},{4,7},{5,4},{6,5},{7,6},{8,11},{9,8},{10,9... | collective-permute-start | bytes 1572872 | tf_op jit(solution)/shard_map/ppermute | solution.py:33
  86.3 12.2 %collective-permute-start.18 = (bf16[2,2,64,512]{3,2,1,0:T(8,128)(2,1)S(1)}, bf16[2,2,64,512]{3,2,1,0:T(8,128)(2,1)S(1)}, u32[]{:S(2)}, u32[]{:S(2)}) collective-permute-start(bf16[2,2,64,512]{3,2,1,0:T(8,128)(2,1)S(1)} %get-tuple-element.105), channel_id=1, source_target_pairs={{0,1},{1,2},{2,3},{3,0},{4,5},{5,6},{6,7},{7,4},{8,9},{9,10},{10,1... | collective-permute-start | bytes 786440 | tf_op jit(solution)/shard_map/ppermute | solution.py:33
  88.0 10.7 %collective-permute-start.19 = (bf16[2,2,64,512]{3,2,1,0:T(8,128)(2,1)S(1)}, bf16[2,2,64,512]{3,2,1,0:T(8,128)(2,1)S(1)}, u32[]{:S(2)}, u32[]{:S(2)}) collective-permute-start(bf16[2,2,64,512]{3,2,1,0:T(8,128)(2,1)S(1)} %get-tuple-element.106), channel_id=1, source_target_pairs={{0,3},{1,0},{2,1},{3,2},{4,7},{5,4},{6,5},{7,6},{8,11},{9,8},{10,9... | collective-permute-start | bytes 786440 | tf_op jit(solution)/shard_map/ppermute | solution.py:33
  91.2 19.0 %collective-permute-start.23 = (bf16[12,64,512]{2,1,0:T(8,128)(2,1)S(1)}, bf16[12,64,512]{2,1,0:T(8,128)(2,1)S(1)}, u32[]{:S(2)}, u32[]{:S(2)}) collective-permute-start(bf16[12,64,512]{2,1,0:T(8,128)(2,1)S(1)} %get-tuple-element.120), channel_id=1, source_target_pairs={{0,4},{1,5},{2,6},{3,7},{4,0},{5,1},{6,2},{7,3},{8,12},{9,13},{10,... | collective-permute-start | bytes 2359304 | tf_op jit(solution)/shard_map/ppermute | solution.py:37
  95.3 7.7 %collective-permute-start.12 = (bf16[4,64,512]{2,1,0:T(8,128)(2,1)S(1)}, bf16[4,64,512]{2,1,0:T(8,128)(2,1)S(1)}, u32[]{:S(2)}, u32[]{:S(2)}) collective-permute-start(bf16[4,64,512]{2,1,0:T(8,128)(2,1)S(1)} %get-tuple-element.98), channel_id=1, source_target_pairs={{0,1},{1,2},{2,3},{3,0},{4,5},{5,6},{6,7},{7,4},{8,9},{9,10},{10,1... | collective-permute-start | bytes 786440 | tf_op jit(solution)/shard_map/ppermute | solution.py:33
  95.7 8.2 %collective-permute-start.13 = (bf16[4,64,512]{2,1,0:T(8,128)(2,1)S(1)}, bf16[4,64,512]{2,1,0:T(8,128)(2,1)S(1)}, u32[]{:S(2)}, u32[]{:S(2)}) collective-permute-start(bf16[4,64,512]{2,1,0:T(8,128)(2,1)S(1)} %get-tuple-element.99), channel_id=1, source_target_pairs={{0,3},{1,0},{2,1},{3,2},{4,7},{5,4},{6,5},{7,6},{8,11},{9,8},{10,9... | collective-permute-start | bytes 786440 | tf_op jit(solution)/shard_map/ppermute | solution.py:33
  98.8 6.2 %collective-permute-start.20 = (bf16[2,64,512]{2,1,0:T(8,128)(2,1)S(1)}, bf16[2,64,512]{2,1,0:T(8,128)(2,1)S(1)}, u32[]{:S(2)}, u32[]{:S(2)}) collective-permute-start(bf16[2,64,512]{2,1,0:T(8,128)(2,1)S(1)} %get-tuple-element.109), channel_id=1, source_target_pairs={{0,1},{1,2},{2,3},{3,0},{4,5},{5,6},{6,7},{7,4},{8,9},{9,10},{10,1... | collective-permute-start | bytes 393224 | tf_op jit(solution)/shard_map/ppermute | solution.py:33
  98.8 6.5 %collective-permute-start.21 = (bf16[2,64,512]{2,1,0:T(8,128)(2,1)S(1)}, bf16[2,64,512]{2,1,0:T(8,128)(2,1)S(1)}, u32[]{:S(2)}, u32[]{:S(2)}) collective-permute-start(bf16[2,64,512]{2,1,0:T(8,128)(2,1)S(1)} %get-tuple-element.110), channel_id=1, source_target_pairs={{0,3},{1,0},{2,1},{3,2},{4,7},{5,4},{6,5},{7,6},{8,11},{9,8},{10,9... | collective-permute-start | bytes 393224 | tf_op jit(solution)/shard_map/ppermute | solution.py:33
  106.4 11.6 %collective-permute-start.22 = (bf16[6,64,512]{2,1,0:T(8,128)(2,1)S(1)}, bf16[6,64,512]{2,1,0:T(8,128)(2,1)S(1)}, u32[]{:S(2)}, u32[]{:S(2)}) collective-permute-start(bf16[6,64,512]{2,1,0:T(8,128)(2,1)S(1)} %get-tuple-element.112), channel_id=1, source_target_pairs={{0,4},{1,5},{2,6},{3,7},{4,0},{5,1},{6,2},{7,3},{8,12},{9,13},{10,... | collective-permute-start | bytes 1179656 | tf_op jit(solution)/shard_map/ppermute | solution.py:37
  119.6 27.6 %all-to-all-start = ((bf16[8,9,64,128]{3,2,1,0:T(8,128)(2,1)}), bf16[8,9,64,128]{3,2,1,0:T(8,128)(2,1)S(1)}, u32[]{:S(2)}, u32[]{:S(2)}) async-start(bf16[8,9,64,128]{3,2,1,0:T(8,128)(2,1)} %get-tuple-element.122), calls=%async_computation | async-start | bytes 2359296 | tf_op jit(solution)/shard_map/all_to_all | solution.py:41
  126.3 4.7 %collective-permute-start.24 = (bf16[3,64,512]{2,1,0:T(8,128)(2,1)S(1)}, bf16[3,64,512]{2,1,0:T(8,128)(2,1)S(1)}, u32[]{:S(2)}, u32[]{:S(2)}) collective-permute-start(bf16[3,64,512]{2,1,0:T(8,128)(2,1)S(1)} %get-tuple-element.124), channel_id=1, source_target_pairs={{0,120},{8,0},{16,8},{24,16},{32,24},{40,32},{48,40},{56,48},{64,5... | collective-permute-start | bytes 589832 | tf_op jit(solution)/shard_map/ppermute | solution.py:28
  126.3 6.3 %collective-permute-start.25 = (bf16[3,64,512]{2,1,0:T(8,128)(2,1)S(1)}, bf16[3,64,512]{2,1,0:T(8,128)(2,1)S(1)}, u32[]{:S(2)}, u32[]{:S(2)}) collective-permute-start(bf16[3,64,512]{2,1,0:T(8,128)(2,1)S(1)} %get-tuple-element.125), channel_id=1, source_target_pairs={{0,8},{8,16},{16,24},{24,32},{32,40},{40,48},{48,56},{56,64},{64,7... | collective-permute-start | bytes 589832 | tf_op jit(solution)/shard_map/ppermute | solution.py:28
  126.8 13.4 %collective-permute-start.26 = (bf16[3,64,512]{2,1,0:T(8,128)(2,1)S(1)}, bf16[3,64,512]{2,1,0:T(8,128)(2,1)S(1)}, u32[]{:S(2)}, u32[]{:S(2)}) collective-permute-start(bf16[3,64,512]{2,1,0:T(8,128)(2,1)S(1)} %get-tuple-element.126), channel_id=1, source_target_pairs={{0,112},{8,120},{16,0},{24,8},{32,16},{40,24},{48,32},{56,40},{64,... | collective-permute-start | bytes 589832 | tf_op jit(solution)/shard_map/ppermute | solution.py:28
  126.8 13.4 %collective-permute-start.27 = (bf16[3,64,512]{2,1,0:T(8,128)(2,1)S(1)}, bf16[3,64,512]{2,1,0:T(8,128)(2,1)S(1)}, u32[]{:S(2)}, u32[]{:S(2)}) collective-permute-start(bf16[3,64,512]{2,1,0:T(8,128)(2,1)S(1)} %get-tuple-element.127), channel_id=1, source_target_pairs={{0,16},{8,24},{16,32},{24,40},{32,48},{40,56},{48,64},{56,72},{64,... | collective-permute-start | bytes 589832 | tf_op jit(solution)/shard_map/ppermute | solution.py:28

commit v7 on v6

--- a/solution.py
+++ b/solution.py
@@ -300,8 +300,9 @@
             even = cut_ref[2 * pair, couple].astype(jnp.float32)
             odd = cut_ref[2 * pair + 1, couple].astype(jnp.float32)
             lanes = pl.ds(2 * ROWS * pair, 2 * ROWS)
-            held[2 * couple, :, lanes] = jnp.where(low, even, pltpu.roll(odd, ROWS, 1))
-            held[2 * couple + 1, :, lanes] = jnp.where(low, pltpu.roll(even, ROWS, 1), odd)
+            moved = pltpu.roll(jnp.where(low, odd, even), ROWS, 1)
+            held[2 * couple, :, lanes] = jnp.where(low, even, moved)
+            held[2 * couple + 1, :, lanes] = jnp.where(low, moved, odd)
         for at in (2 * couple, 2 * couple + 1):
             send(held.at[at], kernel_t_ref, at)
     for places, arrived_ref in zip(RESULTS[1:], results[1:]):

time: 151 us -> 151 us (level)
  no operation moved by 1% of the time
where the time goes in v7:
time: 151 us; the launch traced here: 150 us
  waiting for transfers between devices  69.6 us (46%)
  starting transfers between devices  47.9 us (32%)
  Pallas kernels  29.6 us (20%)
  local copies, waits for them, and re-layouts  2.1 us (1%)
    ppermute x16, waiting for transfers between devices, along_y(): return lax.ppermute(value, 'pw', pairs)  40.6 us
    ppermute x16, starting transfers between devices, along_y(): return lax.ppermute(value, 'pw', pairs)  23.1 us
    ppermute x10, waiting for transfers between devices, shifted(): return lax.ppermute(value, 'trans', pairs)  16.7 us
    pallas_call x4, Pallas kernels, products(): pl.pallas_call(lambda *refs: products_kernel(start, count, *refs), out_sh...  13.3 us
    ppermute x10, starting transfers between devices, shifted(): return lax.ppermute(value, 'trans', pairs)  10.6 us
    ppermute x2, starting transfers between devices, across_z(): lax.ppermute(value, 'pw', [(source, (source + NY) % NPW) for source in ra...  7.58 us
    all_to_all x1, waiting for transfers between devices, exchanged(): return lax.all_to_all(value, 'pw', split_axis=0, concat_axis=0, tiled=True)  7 us
    all_to_all x1, starting transfers between devices, exchanged(): return lax.all_to_all(value, 'pw', split_axis=0, concat_axis=0, tiled=True)  6.7 us
  transfers between devices with their start and end apart: 29, of which 18 were waited for; matrix products, arithmetic and copies ran while one was open for 0% of the time, Pallas kernels for 14%

profile of v7, /device:TPU:6, one launch (start us, length us, event | category | flops | bytes accessed | tf_op | source)
XLA Modules:
  0.0 150.3 jit_solution(13278044768371506750)
XLA Ops:
  0.6 0.1 pad_add_fusion.place_ref
  0.7 0.7 copy-done.1
  1.4 0.7 copy-done.2
  2.1 1.7 %make_table.1.refs_0_.table_ref = s32[56]{0:T(128)S(1)} custom-call(s32[2]{0:T(128)S(1)} %pad_add_fusion.place_ref, s32[2,288]{1,0:T(2,128)S(1)} %bitcast.13, s32[128]{0:T(128)S(1)} %copy-done.2), custom_call_target="tpu_custom_call" | custom-call | flops 3450000128 | bytes 9000001 | tf_op jit(solution)/shard_map/make_table/pallas_call | solution.py:76
  3.8 0.8 copy-done
  4.5 1.9 %select.3 = (bf16[3,512,640]{2,1,0:T(8,128)(2,1)S(1)}, bf16[3,512,640]{2,1,0:T(8,128)(2,1)S(1)}) custom-call(s32[56]{0:T(128)S(1)} %make_table.1.refs_0_.table_ref, bf16[8,512,640]{2,1,0:T(8,128)(2,1)S(1)} %bitcast.6), custom_call_target="tpu_custom_call" | custom-call | flops 1150000000 | bytes 3000001 | tf_op jit(solution)/shard_map/select/pallas_call | solution.py:101
  6.5 1.7 %collective-permute-start.1 = (bf16[3,512,640]{2,1,0:T(8,128)(2,1)S(1)}, bf16[3,512,640]{2,1,0:T(8,128)(2,1)S(1)}, u32[]{:S(2)}, u32[]{:S(2)}) collective-permute-start(bf16[3,512,640]{2,1,0:T(8,128)(2,1)S(1)} %get-tuple-element.67), channel_id=1, source_target_pairs={{0,120},{8,0},{16,8},{24,16},{32,24},{40,32},{48,40},{56,48},{64,5... | collective-permute-start | bytes 5898248 | tf_op jit(solution)/shard_map/ppermute | solution.py:28
  8.2 4.3 %products.4 = (f32[2,6,64,512]{3,2,1,0:T(8,128)S(1)}, f32[6,64,512]{2,1,0:T(8,128)S(1)}, f32[6,64,512]{2,1,0:T(8,128)S(1)}, bf16[2,6,64,512]{3,2,1,0:T(8,128)(2,1)S(1)}, bf16[2,6,64,512]{3,2,1,0:T(8,128)(2,1)S(1)}) custom-call(s32[56]{0:T(128)S(1)} %make_table.1.refs_0_.table_ref, bf16[8,512,640]{2,1,0:T(8,128)(2,1)S(1)} %bitcast.7, ...), custom_call_target="tpu_custom_call" | custom-call | flops 1150000000 | bytes 3000001 | tf_op jit(solution)/shard_map/products/pallas_call | solution.py:158
  12.5 1.6 %collective-permute-start.2 = (bf16[2,6,64,512]{3,2,1,0:T(8,128)(2,1)S(1)}, bf16[2,6,64,512]{3,2,1,0:T(8,128)(2,1)S(1)}, u32[]{:S(2)}, u32[]{:S(2)}) collective-permute-start(bf16[2,6,64,512]{3,2,1,0:T(8,128)(2,1)S(1)} %get-tuple-element.77), channel_id=1, source_target_pairs={{0,1},{1,2},{2,3},{3,0},{4,5},{5,6},{6,7},{7,4},{8,9},{9,10},{10,1... | collective-permute-start | bytes 2359304 | tf_op jit(solution)/shard_map/ppermute | solution.py:33
  14.2 1.7 %collective-permute-start.3 = (bf16[2,6,64,512]{3,2,1,0:T(8,128)(2,1)S(1)}, bf16[2,6,64,512]{3,2,1,0:T(8,128)(2,1)S(1)}, u32[]{:S(2)}, u32[]{:S(2)}) collective-permute-start(bf16[2,6,64,512]{3,2,1,0:T(8,128)(2,1)S(1)} %get-tuple-element.78), channel_id=1, source_target_pairs={{0,3},{1,0},{2,1},{3,2},{4,7},{5,4},{6,5},{7,6},{8,11},{9,8},{10,9... | collective-permute-start | bytes 2359304 | tf_op jit(solution)/shard_map/ppermute | solution.py:33
  15.8 1.0 select.5
  16.8 1.4 select.4
  18.3 15.3 %collective-permute-done.2.up_got_ref.refs_2_ = bf16[2,6,64,512]{3,2,1,0:T(8,128)(2,1)S(1)} collective-permute-done((bf16[2,6,64,512]{3,2,1,0:T(8,128)(2,1)S(1)}, bf16[2,6,64,512]{3,2,1,0:T(8,128)(2,1)S(1)}, u32[]{:S(2)}, u32[]{:S(2)}) %collective-permute-start.2) | collective-permute-done | bytes 786464 | tf_op jit(solution)/shard_map/ppermute | solution.py:33
  33.6 0.2 passed_on.4
  33.8 1.6 %collective-permute-start.4 = (bf16[2,512,640]{2,1,0:T(8,128)(2,1)S(1)}, bf16[2,512,640]{2,1,0:T(8,128)(2,1)S(1)}, u32[]{:S(2)}, u32[]{:S(2)}) collective-permute-start(bf16[2,512,640]{2,1,0:T(8,128)(2,1)S(1)} %get-tuple-element.83), channel_id=1, source_target_pairs={{0,16},{8,24},{16,32},{24,40},{32,48},{40,56},{48,64},{56,72},{64,... | collective-permute-start | bytes 3932168 | tf_op jit(solution)/shard_map/ppermute | solution.py:28
  35.4 0.5 collective-permute-start.5
  35.9 4.3 %products.5 = (f32[2,6,64,512]{3,2,1,0:T(8,128)S(1)}, f32[6,64,512]{2,1,0:T(8,128)S(1)}, f32[6,64,512]{2,1,0:T(8,128)S(1)}, bf16[2,6,64,512]{3,2,1,0:T(8,128)(2,1)S(1)}, bf16[2,6,64,512]{3,2,1,0:T(8,128)(2,1)S(1)}) custom-call(s32[56]{0:T(128)S(1)} %make_table.1.refs_0_.table_ref, bf16[8,512,640]{2,1,0:T(8,128)(2,1)S(1)} %bitcast.10, ...), custom_call_target="tpu_custom_call" | custom-call | flops 1150000000 | bytes 3000001 | tf_op jit(solution)/shard_map/products/pallas_call | solution.py:158
  40.2 1.7 %collective-permute-start.6 = (bf16[2,6,64,512]{3,2,1,0:T(8,128)(2,1)S(1)}, bf16[2,6,64,512]{3,2,1,0:T(8,128)(2,1)S(1)}, u32[]{:S(2)}, u32[]{:S(2)}) collective-permute-start(bf16[2,6,64,512]{3,2,1,0:T(8,128)(2,1)S(1)} %get-tuple-element.87), channel_id=1, source_target_pairs={{0,1},{1,2},{2,3},{3,0},{4,5},{5,6},{6,7},{7,4},{8,9},{9,10},{10,1... | collective-permute-start | bytes 2359304 | tf_op jit(solution)/shard_map/ppermute | solution.py:33
  41.9 1.7 %collective-permute-start.7 = (bf16[2,6,64,512]{3,2,1,0:T(8,128)(2,1)S(1)}, bf16[2,6,64,512]{3,2,1,0:T(8,128)(2,1)S(1)}, u32[]{:S(2)}, u32[]{:S(2)}) collective-permute-start(bf16[2,6,64,512]{3,2,1,0:T(8,128)(2,1)S(1)} %get-tuple-element.88), channel_id=1, source_target_pairs={{0,3},{1,0},{2,1},{3,2},{4,7},{5,4},{6,5},{7,6},{8,11},{9,8},{10,9... | collective-permute-start | bytes 2359304 | tf_op jit(solution)/shard_map/ppermute | solution.py:33
  43.5 0.4 collective-permute-start.8
  43.9 18.0 %collective-permute-done.6.up_got_ref.refs_7_ = bf16[2,6,64,512]{3,2,1,0:T(8,128)(2,1)S(1)} collective-permute-done((bf16[2,6,64,512]{3,2,1,0:T(8,128)(2,1)S(1)}, bf16[2,6,64,512]{3,2,1,0:T(8,128)(2,1)S(1)}, u32[]{:S(2)}, u32[]{:S(2)}) %collective-permute-start.6) | collective-permute-done | bytes 786464 | tf_op jit(solution)/shard_map/ppermute | solution.py:33
  61.9 1.8 %collective-permute-start.9 = (bf16[6,64,512]{2,1,0:T(8,128)(2,1)S(1)}, bf16[6,64,512]{2,1,0:T(8,128)(2,1)S(1)}, u32[]{:S(2)}, u32[]{:S(2)}) collective-permute-start(bf16[6,64,512]{2,1,0:T(8,128)(2,1)S(1)} %get-tuple-element.80), channel_id=1, source_target_pairs={{0,3},{1,0},{2,1},{3,2},{4,7},{5,4},{6,5},{7,6},{8,11},{9,8},{10,9... | collective-permute-start | bytes 1179656 | tf_op jit(solution)/shard_map/ppermute | solution.py:33
  63.7 0.2 passed_on.5
  63.9 0.3 collective-permute-start.16
  64.2 1.1 collective-permute-done.4.refs_3_
  65.3 2.1 %collective-permute-done.5.refs_4_ = bf16[2,512,640]{2,1,0:T(8,128)(2,1)S(1)} collective-permute-done((bf16[2,512,640]{2,1,0:T(8,128)(2,1)S(1)}, bf16[2,512,640]{2,1,0:T(8,128)(2,1)S(1)}, u32[]{:S(2)}, u32[]{:S(2)}) %collective-permute-start.5) | collective-permute-done | bytes 1310752 | tf_op jit(solution)/shard_map/ppermute | solution.py:28
  67.4 0.5 collective-permute-start.14
  67.9 1.5 %collective-permute-start.15 = (bf16[1,512,640]{2,1,0:T(8,128)(2,1)S(1)}, bf16[1,512,640]{2,1,0:T(8,128)(2,1)S(1)}, u32[]{:S(2)}, u32[]{:S(2)}) collective-permute-start(bf16[1,512,640]{2,1,0:T(8,128)(2,1)S(1)} %get-tuple-element.101), channel_id=1, source_target_pairs={{0,112},{8,120},{16,0},{24,8},{32,16},{40,24},{48,32},{56,40},{64,... | collective-permute-start | bytes 1966088 | tf_op jit(solution)/shard_map/ppermute | solution.py:28
  69.4 0.9 collective-permute-done.8.refs_4_
  70.3 2.1 %collective-permute-start.17 = (bf16[6,64,512]{2,1,0:T(8,128)(2,1)S(1)}, bf16[6,64,512]{2,1,0:T(8,128)(2,1)S(1)}, u32[]{:S(2)}, u32[]{:S(2)}) collective-permute-start(bf16[6,64,512]{2,1,0:T(8,128)(2,1)S(1)} %get-tuple-element.90), channel_id=1, source_target_pairs={{0,3},{1,0},{2,1},{3,2},{4,7},{5,4},{6,5},{7,6},{8,11},{9,8},{10,9... | collective-permute-start | bytes 1179656 | tf_op jit(solution)/shard_map/ppermute | solution.py:33
  72.4 3.1 %products.6 = (f32[2,4,64,512]{3,2,1,0:T(8,128)S(1)}, f32[4,64,512]{2,1,0:T(8,128)S(1)}, f32[4,64,512]{2,1,0:T(8,128)S(1)}, bf16[2,4,64,512]{3,2,1,0:T(8,128)(2,1)S(1)}, bf16[2,4,64,512]{3,2,1,0:T(8,128)(2,1)S(1)}) custom-call(s32[56]{0:T(128)S(1)} %make_table.1.refs_0_.table_ref, bf16[8,512,640]{2,1,0:T(8,128)(2,1)S(1)} %bitcast.11, ...), custom_call_target="tpu_custom_call" | custom-call | flops 1150000000 | bytes 3000001 | tf_op jit(solution)/shard_map/products/pallas_call | solution.py:158
  75.5 0.1 collective-permute-start.10
  75.6 3.0 %collective-permute-done.16.refs_9_ = bf16[6,64,512]{2,1,0:T(8,128)(2,1)S(1)} collective-permute-done((bf16[6,64,512]{2,1,0:T(8,128)(2,1)S(1)}, bf16[6,64,512]{2,1,0:T(8,128)(2,1)S(1)}, u32[]{:S(2)}, u32[]{:S(2)}) %collective-permute-start.16) | collective-permute-done | bytes 393248 | tf_op jit(solution)/shard_map/ppermute | solution.py:33
  78.6 1.9 %collective-permute-start.11 = (bf16[2,4,64,512]{3,2,1,0:T(8,128)(2,1)S(1)}, bf16[2,4,64,512]{3,2,1,0:T(8,128)(2,1)S(1)}, u32[]{:S(2)}, u32[]{:S(2)}) collective-permute-start(bf16[2,4,64,512]{3,2,1,0:T(8,128)(2,1)S(1)} %get-tuple-element.95), channel_id=1, source_target_pairs={{0,3},{1,0},{2,1},{3,2},{4,7},{5,4},{6,5},{7,6},{8,11},{9,8},{10,9... | collective-permute-start | bytes 1572872 | tf_op jit(solution)/shard_map/ppermute | solution.py:33
  80.5 1.8 %collective-permute-done.14.refs_3_ = bf16[1,512,640]{2,1,0:T(8,128)(2,1)S(1)} collective-permute-done((bf16[1,512,640]{2,1,0:T(8,128)(2,1)S(1)}, bf16[1,512,640]{2,1,0:T(8,128)(2,1)S(1)}, u32[]{:S(2)}, u32[]{:S(2)}) %collective-permute-start.14) | collective-permute-done | bytes 655392 | tf_op jit(solution)/shard_map/ppermute | solution.py:28
  82.3 2.4 %collective-permute-done.15.refs_4_ = bf16[1,512,640]{2,1,0:T(8,128)(2,1)S(1)} collective-permute-done((bf16[1,512,640]{2,1,0:T(8,128)(2,1)S(1)}, bf16[1,512,640]{2,1,0:T(8,128)(2,1)S(1)}, u32[]{:S(2)}, u32[]{:S(2)}) %collective-permute-start.15) | collective-permute-done | bytes 655392 | tf_op jit(solution)/shard_map/ppermute | solution.py:28
  84.7 1.6 %products.7 = (f32[2,2,64,512]{3,2,1,0:T(8,128)S(1)}, f32[2,64,512]{2,1,0:T(8,128)S(1)}, f32[2,64,512]{2,1,0:T(8,128)S(1)}, bf16[2,2,64,512]{3,2,1,0:T(8,128)(2,1)S(1)}, bf16[2,2,64,512]{3,2,1,0:T(8,128)(2,1)S(1)}) custom-call(s32[56]{0:T(128)S(1)} %make_table.1.refs_0_.table_ref, bf16[8,512,640]{2,1,0:T(8,128)(2,1)S(1)} %bitcast.12, ...), custom_call_target="tpu_custom_call" | custom-call | flops 1150000000 | bytes 3000001 | tf_op jit(solution)/shard_map/products/pallas_call | solution.py:158
  86.3 1.6 %collective-permute-start.18 = (bf16[2,2,64,512]{3,2,1,0:T(8,128)(2,1)S(1)}, bf16[2,2,64,512]{3,2,1,0:T(8,128)(2,1)S(1)}, u32[]{:S(2)}, u32[]{:S(2)}) collective-permute-start(bf16[2,2,64,512]{3,2,1,0:T(8,128)(2,1)S(1)} %get-tuple-element.105), channel_id=1, source_target_pairs={{0,1},{1,2},{2,3},{3,0},{4,5},{5,6},{6,7},{7,4},{8,9},{9,10},{10,1... | collective-permute-start | bytes 786440 | tf_op jit(solution)/shard_map/ppermute | solution.py:33
  88.0 1.7 %collective-permute-start.19 = (bf16[2,2,64,512]{3,2,1,0:T(8,128)(2,1)S(1)}, bf16[2,2,64,512]{3,2,1,0:T(8,128)(2,1)S(1)}, u32[]{:S(2)}, u32[]{:S(2)}) collective-permute-start(bf16[2,2,64,512]{3,2,1,0:T(8,128)(2,1)S(1)} %get-tuple-element.106), channel_id=1, source_target_pairs={{0,3},{1,0},{2,1},{3,2},{4,7},{5,4},{6,5},{7,6},{8,11},{9,8},{10,9... | collective-permute-start | bytes 786440 | tf_op jit(solution)/shard_map/ppermute | solution.py:33
  89.6 1.6 %plane_sums.3 = (f32[12,64,512]{2,1,0:T(8,128)S(1)}, bf16[12,64,512]{2,1,0:T(8,128)(2,1)S(1)}) custom-call(s32[56]{0:T(128)S(1)} %make_table.1.refs_0_.table_ref, f32[2,6,64,512]{3,2,1,0:T(8,128)S(1)} %get-tuple-element.113.refs_1_, bf16[2,6,64,512]{3,2,1,0:T(8,128)(2,1)S(1)} %collective-permute-done.2.up_got_ref.refs_2_, ...), custom_call_target="tpu_custom_call" | custom-call | flops 1150000000 | bytes 3000001 | tf_op jit(solution)/shard_map/plane_sums/pallas_call | solution.py:233
  91.2 3.8 %collective-permute-start.23 = (bf16[12,64,512]{2,1,0:T(8,128)(2,1)S(1)}, bf16[12,64,512]{2,1,0:T(8,128)(2,1)S(1)}, u32[]{:S(2)}, u32[]{:S(2)}) collective-permute-start(bf16[12,64,512]{2,1,0:T(8,128)(2,1)S(1)} %get-tuple-element.120), channel_id=1, source_target_pairs={{0,4},{1,5},{2,6},{3,7},{4,0},{5,1},{6,2},{7,3},{8,12},{9,13},{10,... | collective-permute-start | bytes 2359304 | tf_op jit(solution)/shard_map/ppermute | solution.py:37
  95.1 0.2 passed_on.6
  95.3 0.4 collective-permute-start.12
  95.7 2.9 %collective-permute-start.13 = (bf16[4,64,512]{2,1,0:T(8,128)(2,1)S(1)}, bf16[4,64,512]{2,1,0:T(8,128)(2,1)S(1)}, u32[]{:S(2)}, u32[]{:S(2)}) collective-permute-start(bf16[4,64,512]{2,1,0:T(8,128)(2,1)S(1)} %get-tuple-element.99), channel_id=1, source_target_pairs={{0,3},{1,0},{2,1},{3,2},{4,7},{5,4},{6,5},{7,6},{8,11},{9,8},{10,9... | collective-permute-start | bytes 786440 | tf_op jit(solution)/shard_map/ppermute | solution.py:33
  98.6 0.1 collective-permute-done.19.down_got_ref.refs_8_
  98.8 0.1 collective-permute-start.20
  98.8 3.2 %collective-permute-start.21 = (bf16[2,64,512]{2,1,0:T(8,128)(2,1)S(1)}, bf16[2,64,512]{2,1,0:T(8,128)(2,1)S(1)}, u32[]{:S(2)}, u32[]{:S(2)}) collective-permute-start(bf16[2,64,512]{2,1,0:T(8,128)(2,1)S(1)} %get-tuple-element.110), channel_id=1, source_target_pairs={{0,3},{1,0},{2,1},{3,2},{4,7},{5,4},{6,5},{7,6},{8,11},{9,8},{10,9... | collective-permute-start | bytes 393224 | tf_op jit(solution)/shard_map/ppermute | solution.py:33
  102.1 1.0 collective-permute-done.12.refs_4_
  103.0 0.9 collective-permute-done.13.refs_5_
  103.9 1.1 collective-permute-done.20.refs_9_
  105.0 0.3 collective-permute-done.21.refs_10_
  105.3 1.1 plane_sums.2
  106.4 3.7 %collective-permute-start.22 = (bf16[6,64,512]{2,1,0:T(8,128)(2,1)S(1)}, bf16[6,64,512]{2,1,0:T(8,128)(2,1)S(1)}, u32[]{:S(2)}, u32[]{:S(2)}) collective-permute-start(bf16[6,64,512]{2,1,0:T(8,128)(2,1)S(1)} %get-tuple-element.112), channel_id=1, source_target_pairs={{0,4},{1,5},{2,6},{3,7},{4,0},{5,1},{6,2},{7,3},{8,12},{9,13},{10,... | collective-permute-start | bytes 1179656 | tf_op jit(solution)/shard_map/ppermute | solution.py:37
  110.1 0.1 collective-permute-done.23.refs_1_
  110.2 2.5 %totals.2 = (f32[6,64,512]{2,1,0:T(8,128)S(1)}, bf16[3,64,512]{2,1,0:T(8,128)(2,1)S(1)}, bf16[3,64,512]{2,1,0:T(8,128)(2,1)S(1)}, bf16[8,9,64,128]{3,2,1,0:T(8,128)(2,1)}) custom-call(f32[12,64,512]{2,1,0:T(8,128)S(1)} %get-tuple-element.119.refs_0_, bf16[12,64,512]{2,1,0:T(8,128)(2,1)S(1)} %collective-permute-done.23.refs_1_), custom_call_target="tpu_custom_call" | custom-call | flops 1150000000 | bytes 3000001 | tf_op jit(solution)/shard_map/totals/pallas_call | solution.py:273
  112.8 5.2 %collective-permute-done.22.refs_1_ = bf16[6,64,512]{2,1,0:T(8,128)(2,1)S(1)} collective-permute-done((bf16[6,64,512]{2,1,0:T(8,128)(2,1)S(1)}, bf16[6,64,512]{2,1,0:T(8,128)(2,1)S(1)}, u32[]{:S(2)}, u32[]{:S(2)}) %collective-permute-start.22) | collective-permute-done | bytes 393248 | tf_op jit(solution)/shard_map/ppermute | solution.py:37
  118.0 1.6 %totals.3 = (bf16[3,64,512]{2,1,0:T(8,128)(2,1)S(1)}, bf16[3,64,512]{2,1,0:T(8,128)(2,1)S(1)}, bf16[8,9,64,128]{3,2,1,0:T(8,128)(2,1)}) custom-call(f32[6,64,512]{2,1,0:T(8,128)S(1)} %get-tuple-element.111.refs_0_, bf16[6,64,512]{2,1,0:T(8,128)(2,1)S(1)} %collective-permute-done.22.refs_1_, ...), custom_call_target="tpu_custom_call", output_to_operand_aliasing={{2}: (2, {})} | custom-call | flops 1150000000 | bytes 3000001 | tf_op jit(solution)/shard_map/totals/pallas_call | solution.py:273
  119.6 6.7 %all-to-all-start = ((bf16[8,9,64,128]{3,2,1,0:T(8,128)(2,1)}), bf16[8,9,64,128]{3,2,1,0:T(8,128)(2,1)S(1)}, u32[]{:S(2)}, u32[]{:S(2)}) async-start(bf16[8,9,64,128]{3,2,1,0:T(8,128)(2,1)} %get-tuple-element.122), calls=%async_computation | async-start | bytes 2359296 | tf_op jit(solution)/shard_map/all_to_all | solution.py:41
  126.3 0.5 collective-permute-start.25
  126.8 4.1 %collective-permute-start.27 = (bf16[3,64,512]{2,1,0:T(8,128)(2,1)S(1)}, bf16[3,64,512]{2,1,0:T(8,128)(2,1)S(1)}, u32[]{:S(2)}, u32[]{:S(2)}) collective-permute-start(bf16[3,64,512]{2,1,0:T(8,128)(2,1)S(1)} %get-tuple-element.127), channel_id=1, source_target_pairs={{0,16},{8,24},{16,32},{24,40},{32,48},{40,56},{48,64},{56,72},{64,... | collective-permute-start | bytes 589832 | tf_op jit(solution)/shard_map/ppermute | solution.py:28
  130.9 1.6 %collective-permute-done.25.refs_2_ = bf16[3,64,512]{2,1,0:T(8,128)(2,1)S(1)} collective-permute-done((bf16[3,64,512]{2,1,0:T(8,128)(2,1)S(1)}, bf16[3,64,512]{2,1,0:T(8,128)(2,1)S(1)}, u32[]{:S(2)}, u32[]{:S(2)}) %collective-permute-start.25) | collective-permute-done | bytes 196640 | tf_op jit(solution)/shard_map/ppermute | solution.py:28
  132.5 7.6 %collective-permute-done.26.refs_3_ = bf16[3,64,512]{2,1,0:T(8,128)(2,1)S(1)} collective-permute-done((bf16[3,64,512]{2,1,0:T(8,128)(2,1)S(1)}, bf16[3,64,512]{2,1,0:T(8,128)(2,1)S(1)}, u32[]{:S(2)}, u32[]{:S(2)}) %collective-permute-start.26) | collective-permute-done | bytes 196640 | tf_op jit(solution)/shard_map/ppermute | solution.py:28
  140.2 7.0 %all-to-all-done.cut_ref = bf16[8,9,64,128]{3,2,1,0:T(8,128)(2,1)S(1)} async-done(((bf16[8,9,64,128]{3,2,1,0:T(8,128)(2,1)}), bf16[8,9,64,128]{3,2,1,0:T(8,128)(2,1)S(1)}, u32[]{:S(2)}, u32[]{:S(2)}) %all-to-all-start) | async-done | bytes 1179680 | tf_op jit(solution)/shard_map/all_to_all | solution.py:41
  147.2 3.0 %finish.1 = (f32[18,64,512]{2,1,0:T(8,128)}, f32[18,64,512]{2,1,0:T(8,128)}) custom-call(s32[56]{0:T(128)S(1)} %make_table.1.refs_0_.table_ref, bf16[8,9,64,128]{3,2,1,0:T(8,128)(2,1)S(1)} %all-to-all-done.cut_ref, f32[6,64,512]{2,1,0:T(8,128)S(1)} %get-tuple-element.123.refs_0_, bf16[3,64,512]{2,1,0:T(8,128)(2,1)S(1)} %collective-permute-done.24.refs_1_, ...), custom_call_target="tpu_custom_call" | custom-call | flops 1150000000 | bytes 3000001 | tf_op jit(solution)/shard_map/finish/pallas_call | solution.py:320
  (21 shorter events, 0.2 us)
Async XLA Ops:
  0.7 0.7 copy-start.1
  1.4 0.7 copy-start.2
  2.0 2.5 %copy-start = (bf16[4096,640]{1,0:T(8,128)(2,1)S(1)}, bf16[4096,640]{1,0:T(8,128)(2,1)}, u32[]{:S(2)}) copy-start(bf16[4096,640]{1,0:T(8,128)(2,1)} %param.4) | copy-start | bytes 15728644
  4.5 3.7 %copy-start.3 = (f32[640]{0:T(1024)S(1)}, f32[640]{0:T(1024)}, u32[]{:S(2)}) copy-start(f32[640]{0:T(1024)} %param.5) | copy-start | bytes 7684
  6.4 27.4 %collective-permute-start = (bf16[3,512,640]{2,1,0:T(8,128)(2,1)S(1)}, bf16[3,512,640]{2,1,0:T(8,128)(2,1)S(1)}, u32[]{:S(2)}, u32[]{:S(2)}) collective-permute-start(bf16[3,512,640]{2,1,0:T(8,128)(2,1)S(1)} %get-tuple-element.66), channel_id=1, source_target_pairs={{0,8},{8,16},{16,24},{24,32},{32,40},{40,48},{48,56},{56,64},{64,7... | collective-permute-start | bytes 5898248 | tf_op jit(solution)/shard_map/ppermute | solution.py:28
  6.5 27.3 %collective-permute-start.1 = (bf16[3,512,640]{2,1,0:T(8,128)(2,1)S(1)}, bf16[3,512,640]{2,1,0:T(8,128)(2,1)S(1)}, u32[]{:S(2)}, u32[]{:S(2)}) collective-permute-start(bf16[3,512,640]{2,1,0:T(8,128)(2,1)S(1)} %get-tuple-element.67), channel_id=1, source_target_pairs={{0,120},{8,0},{16,8},{24,16},{32,24},{40,32},{48,40},{56,48},{64,5... | collective-permute-start | bytes 5898248 | tf_op jit(solution)/shard_map/ppermute | solution.py:28
  12.5 21.0 %collective-permute-start.2 = (bf16[2,6,64,512]{3,2,1,0:T(8,128)(2,1)S(1)}, bf16[2,6,64,512]{3,2,1,0:T(8,128)(2,1)S(1)}, u32[]{:S(2)}, u32[]{:S(2)}) collective-permute-start(bf16[2,6,64,512]{3,2,1,0:T(8,128)(2,1)S(1)} %get-tuple-element.77), channel_id=1, source_target_pairs={{0,1},{1,2},{2,3},{3,0},{4,5},{5,6},{6,7},{7,4},{8,9},{9,10},{10,1... | collective-permute-start | bytes 2359304 | tf_op jit(solution)/shard_map/ppermute | solution.py:33
  14.2 19.4 %collective-permute-start.3 = (bf16[2,6,64,512]{3,2,1,0:T(8,128)(2,1)S(1)}, bf16[2,6,64,512]{3,2,1,0:T(8,128)(2,1)S(1)}, u32[]{:S(2)}, u32[]{:S(2)}) collective-permute-start(bf16[2,6,64,512]{3,2,1,0:T(8,128)(2,1)S(1)} %get-tuple-element.78), channel_id=1, source_target_pairs={{0,3},{1,0},{2,1},{3,2},{4,7},{5,4},{6,5},{7,6},{8,11},{9,8},{10,9... | collective-permute-start | bytes 2359304 | tf_op jit(solution)/shard_map/ppermute | solution.py:33
  33.8 31.5 %collective-permute-start.4 = (bf16[2,512,640]{2,1,0:T(8,128)(2,1)S(1)}, bf16[2,512,640]{2,1,0:T(8,128)(2,1)S(1)}, u32[]{:S(2)}, u32[]{:S(2)}) collective-permute-start(bf16[2,512,640]{2,1,0:T(8,128)(2,1)S(1)} %get-tuple-element.83), channel_id=1, source_target_pairs={{0,16},{8,24},{16,32},{24,40},{32,48},{40,56},{48,64},{56,72},{64,... | collective-permute-start | bytes 3932168 | tf_op jit(solution)/shard_map/ppermute | solution.py:28
  35.4 32.0 %collective-permute-start.5 = (bf16[2,512,640]{2,1,0:T(8,128)(2,1)S(1)}, bf16[2,512,640]{2,1,0:T(8,128)(2,1)S(1)}, u32[]{:S(2)}, u32[]{:S(2)}) collective-permute-start(bf16[2,512,640]{2,1,0:T(8,128)(2,1)S(1)} %get-tuple-element.84), channel_id=1, source_target_pairs={{0,112},{8,120},{16,0},{24,8},{32,16},{40,24},{48,32},{56,40},{64,... | collective-permute-start | bytes 3932168 | tf_op jit(solution)/shard_map/ppermute | solution.py:28
  40.2 21.7 %collective-permute-start.6 = (bf16[2,6,64,512]{3,2,1,0:T(8,128)(2,1)S(1)}, bf16[2,6,64,512]{3,2,1,0:T(8,128)(2,1)S(1)}, u32[]{:S(2)}, u32[]{:S(2)}) collective-permute-start(bf16[2,6,64,512]{3,2,1,0:T(8,128)(2,1)S(1)} %get-tuple-element.87), channel_id=1, source_target_pairs={{0,1},{1,2},{2,3},{3,0},{4,5},{5,6},{6,7},{7,4},{8,9},{9,10},{10,1... | collective-permute-start | bytes 2359304 | tf_op jit(solution)/shard_map/ppermute | solution.py:33
  41.9 21.8 %collective-permute-start.7 = (bf16[2,6,64,512]{3,2,1,0:T(8,128)(2,1)S(1)}, bf16[2,6,64,512]{3,2,1,0:T(8,128)(2,1)S(1)}, u32[]{:S(2)}, u32[]{:S(2)}) collective-permute-start(bf16[2,6,64,512]{3,2,1,0:T(8,128)(2,1)S(1)} %get-tuple-element.88), channel_id=1, source_target_pairs={{0,3},{1,0},{2,1},{3,2},{4,7},{5,4},{6,5},{7,6},{8,11},{9,8},{10,9... | collective-permute-start | bytes 2359304 | tf_op jit(solution)/shard_map/ppermute | solution.py:33
  43.5 26.8 %collective-permute-start.8 = (bf16[6,64,512]{2,1,0:T(8,128)(2,1)S(1)}, bf16[6,64,512]{2,1,0:T(8,128)(2,1)S(1)}, u32[]{:S(2)}, u32[]{:S(2)}) collective-permute-start(bf16[6,64,512]{2,1,0:T(8,128)(2,1)S(1)} %get-tuple-element.79), channel_id=1, source_target_pairs={{0,1},{1,2},{2,3},{3,0},{4,5},{5,6},{6,7},{7,4},{8,9},{9,10},{10,1... | collective-permute-start | bytes 1179656 | tf_op jit(solution)/shard_map/ppermute | solution.py:33
  61.9 10.6 %collective-permute-start.9 = (bf16[6,64,512]{2,1,0:T(8,128)(2,1)S(1)}, bf16[6,64,512]{2,1,0:T(8,128)(2,1)S(1)}, u32[]{:S(2)}, u32[]{:S(2)}) collective-permute-start(bf16[6,64,512]{2,1,0:T(8,128)(2,1)S(1)} %get-tuple-element.80), channel_id=1, source_target_pairs={{0,3},{1,0},{2,1},{3,2},{4,7},{5,4},{6,5},{7,6},{8,11},{9,8},{10,9... | collective-permute-start | bytes 1179656 | tf_op jit(solution)/shard_map/ppermute | solution.py:33
  63.9 14.7 %collective-permute-start.16 = (bf16[6,64,512]{2,1,0:T(8,128)(2,1)S(1)}, bf16[6,64,512]{2,1,0:T(8,128)(2,1)S(1)}, u32[]{:S(2)}, u32[]{:S(2)}) collective-permute-start(bf16[6,64,512]{2,1,0:T(8,128)(2,1)S(1)} %get-tuple-element.89), channel_id=1, source_target_pairs={{0,1},{1,2},{2,3},{3,0},{4,5},{5,6},{6,7},{7,4},{8,9},{9,10},{10,1... | collective-permute-start | bytes 1179656 | tf_op jit(solution)/shard_map/ppermute | solution.py:33
  67.4 14.9 %collective-permute-start.14 = (bf16[1,512,640]{2,1,0:T(8,128)(2,1)S(1)}, bf16[1,512,640]{2,1,0:T(8,128)(2,1)S(1)}, u32[]{:S(2)}, u32[]{:S(2)}) collective-permute-start(bf16[1,512,640]{2,1,0:T(8,128)(2,1)S(1)} %get-tuple-element.100), channel_id=1, source_target_pairs={{0,16},{8,24},{16,32},{24,40},{32,48},{40,56},{48,64},{56,72},{64,... | collective-permute-start | bytes 1966088 | tf_op jit(solution)/shard_map/ppermute | solution.py:28
  67.9 16.8 %collective-permute-start.15 = (bf16[1,512,640]{2,1,0:T(8,128)(2,1)S(1)}, bf16[1,512,640]{2,1,0:T(8,128)(2,1)S(1)}, u32[]{:S(2)}, u32[]{:S(2)}) collective-permute-start(bf16[1,512,640]{2,1,0:T(8,128)(2,1)S(1)} %get-tuple-element.101), channel_id=1, source_target_pairs={{0,112},{8,120},{16,0},{24,8},{32,16},{40,24},{48,32},{56,40},{64,... | collective-permute-start | bytes 1966088 | tf_op jit(solution)/shard_map/ppermute | solution.py:28
  70.3 10.2 %collective-permute-start.17 = (bf16[6,64,512]{2,1,0:T(8,128)(2,1)S(1)}, bf16[6,64,512]{2,1,0:T(8,128)(2,1)S(1)}, u32[]{:S(2)}, u32[]{:S(2)}) collective-permute-start(bf16[6,64,512]{2,1,0:T(8,128)(2,1)S(1)} %get-tuple-element.90), channel_id=1, source_target_pairs={{0,3},{1,0},{2,1},{3,2},{4,7},{5,4},{6,5},{7,6},{8,11},{9,8},{10,9... | collective-permute-start | bytes 1179656 | tf_op jit(solution)/shard_map/ppermute | solution.py:33
  75.5 19.6 %collective-permute-start.10 = (bf16[2,4,64,512]{3,2,1,0:T(8,128)(2,1)S(1)}, bf16[2,4,64,512]{3,2,1,0:T(8,128)(2,1)S(1)}, u32[]{:S(2)}, u32[]{:S(2)}) collective-permute-start(bf16[2,4,64,512]{3,2,1,0:T(8,128)(2,1)S(1)} %get-tuple-element.94), channel_id=1, source_target_pairs={{0,1},{1,2},{2,3},{3,0},{4,5},{5,6},{6,7},{7,4},{8,9},{9,10},{10,1... | collective-permute-start | bytes 1572872 | tf_op jit(solution)/shard_map/ppermute | solution.py:33
  78.6 16.5 %collective-permute-start.11 = (bf16[2,4,64,512]{3,2,1,0:T(8,128)(2,1)S(1)}, bf16[2,4,64,512]{3,2,1,0:T(8,128)(2,1)S(1)}, u32[]{:S(2)}, u32[]{:S(2)}) collective-permute-start(bf16[2,4,64,512]{3,2,1,0:T(8,128)(2,1)S(1)} %get-tuple-element.95), channel_id=1, source_target_pairs={{0,3},{1,0},{2,1},{3,2},{4,7},{5,4},{6,5},{7,6},{8,11},{9,8},{10,9... | collective-permute-start | bytes 1572872 | tf_op jit(solution)/shard_map/ppermute | solution.py:33
  86.3 12.2 %collective-permute-start.18 = (bf16[2,2,64,512]{3,2,1,0:T(8,128)(2,1)S(1)}, bf16[2,2,64,512]{3,2,1,0:T(8,128)(2,1)S(1)}, u32[]{:S(2)}, u32[]{:S(2)}) collective-permute-start(bf16[2,2,64,512]{3,2,1,0:T(8,128)(2,1)S(1)} %get-tuple-element.105), channel_id=1, source_target_pairs={{0,1},{1,2},{2,3},{3,0},{4,5},{5,6},{6,7},{7,4},{8,9},{9,10},{10,1... | collective-permute-start | bytes 786440 | tf_op jit(solution)/shard_map/ppermute | solution.py:33
  88.0 10.7 %collective-permute-start.19 = (bf16[2,2,64,512]{3,2,1,0:T(8,128)(2,1)S(1)}, bf16[2,2,64,512]{3,2,1,0:T(8,128)(2,1)S(1)}, u32[]{:S(2)}, u32[]{:S(2)}) collective-permute-start(bf16[2,2,64,512]{3,2,1,0:T(8,128)(2,1)S(1)} %get-tuple-element.106), channel_id=1, source_target_pairs={{0,3},{1,0},{2,1},{3,2},{4,7},{5,4},{6,5},{7,6},{8,11},{9,8},{10,9... | collective-permute-start | bytes 786440 | tf_op jit(solution)/shard_map/ppermute | solution.py:33
  91.2 19.0 %collective-permute-start.23 = (bf16[12,64,512]{2,1,0:T(8,128)(2,1)S(1)}, bf16[12,64,512]{2,1,0:T(8,128)(2,1)S(1)}, u32[]{:S(2)}, u32[]{:S(2)}) collective-permute-start(bf16[12,64,512]{2,1,0:T(8,128)(2,1)S(1)} %get-tuple-element.120), channel_id=1, source_target_pairs={{0,4},{1,5},{2,6},{3,7},{4,0},{5,1},{6,2},{7,3},{8,12},{9,13},{10,... | collective-permute-start | bytes 2359304 | tf_op jit(solution)/shard_map/ppermute | solution.py:37
  95.3 7.7 %collective-permute-start.12 = (bf16[4,64,512]{2,1,0:T(8,128)(2,1)S(1)}, bf16[4,64,512]{2,1,0:T(8,128)(2,1)S(1)}, u32[]{:S(2)}, u32[]{:S(2)}) collective-permute-start(bf16[4,64,512]{2,1,0:T(8,128)(2,1)S(1)} %get-tuple-element.98), channel_id=1, source_target_pairs={{0,1},{1,2},{2,3},{3,0},{4,5},{5,6},{6,7},{7,4},{8,9},{9,10},{10,1... | collective-permute-start | bytes 786440 | tf_op jit(solution)/shard_map/ppermute | solution.py:33
  95.7 8.2 %collective-permute-start.13 = (bf16[4,64,512]{2,1,0:T(8,128)(2,1)S(1)}, bf16[4,64,512]{2,1,0:T(8,128)(2,1)S(1)}, u32[]{:S(2)}, u32[]{:S(2)}) collective-permute-start(bf16[4,64,512]{2,1,0:T(8,128)(2,1)S(1)} %get-tuple-element.99), channel_id=1, source_target_pairs={{0,3},{1,0},{2,1},{3,2},{4,7},{5,4},{6,5},{7,6},{8,11},{9,8},{10,9... | collective-permute-start | bytes 786440 | tf_op jit(solution)/shard_map/ppermute | solution.py:33
  98.8 6.2 %collective-permute-start.20 = (bf16[2,64,512]{2,1,0:T(8,128)(2,1)S(1)}, bf16[2,64,512]{2,1,0:T(8,128)(2,1)S(1)}, u32[]{:S(2)}, u32[]{:S(2)}) collective-permute-start(bf16[2,64,512]{2,1,0:T(8,128)(2,1)S(1)} %get-tuple-element.109), channel_id=1, source_target_pairs={{0,1},{1,2},{2,3},{3,0},{4,5},{5,6},{6,7},{7,4},{8,9},{9,10},{10,1... | collective-permute-start | bytes 393224 | tf_op jit(solution)/shard_map/ppermute | solution.py:33
  98.8 6.5 %collective-permute-start.21 = (bf16[2,64,512]{2,1,0:T(8,128)(2,1)S(1)}, bf16[2,64,512]{2,1,0:T(8,128)(2,1)S(1)}, u32[]{:S(2)}, u32[]{:S(2)}) collective-permute-start(bf16[2,64,512]{2,1,0:T(8,128)(2,1)S(1)} %get-tuple-element.110), channel_id=1, source_target_pairs={{0,3},{1,0},{2,1},{3,2},{4,7},{5,4},{6,5},{7,6},{8,11},{9,8},{10,9... | collective-permute-start | bytes 393224 | tf_op jit(solution)/shard_map/ppermute | solution.py:33
  106.4 11.6 %collective-permute-start.22 = (bf16[6,64,512]{2,1,0:T(8,128)(2,1)S(1)}, bf16[6,64,512]{2,1,0:T(8,128)(2,1)S(1)}, u32[]{:S(2)}, u32[]{:S(2)}) collective-permute-start(bf16[6,64,512]{2,1,0:T(8,128)(2,1)S(1)} %get-tuple-element.112), channel_id=1, source_target_pairs={{0,4},{1,5},{2,6},{3,7},{4,0},{5,1},{6,2},{7,3},{8,12},{9,13},{10,... | collective-permute-start | bytes 1179656 | tf_op jit(solution)/shard_map/ppermute | solution.py:37
  119.6 27.6 %all-to-all-start = ((bf16[8,9,64,128]{3,2,1,0:T(8,128)(2,1)}), bf16[8,9,64,128]{3,2,1,0:T(8,128)(2,1)S(1)}, u32[]{:S(2)}, u32[]{:S(2)}) async-start(bf16[8,9,64,128]{3,2,1,0:T(8,128)(2,1)} %get-tuple-element.122), calls=%async_computation | async-start | bytes 2359296 | tf_op jit(solution)/shard_map/all_to_all | solution.py:41
  126.3 4.7 %collective-permute-start.24 = (bf16[3,64,512]{2,1,0:T(8,128)(2,1)S(1)}, bf16[3,64,512]{2,1,0:T(8,128)(2,1)S(1)}, u32[]{:S(2)}, u32[]{:S(2)}) collective-permute-start(bf16[3,64,512]{2,1,0:T(8,128)(2,1)S(1)} %get-tuple-element.124), channel_id=1, source_target_pairs={{0,120},{8,0},{16,8},{24,16},{32,24},{40,32},{48,40},{56,48},{64,5... | collective-permute-start | bytes 589832 | tf_op jit(solution)/shard_map/ppermute | solution.py:28
  126.3 6.3 %collective-permute-start.25 = (bf16[3,64,512]{2,1,0:T(8,128)(2,1)S(1)}, bf16[3,64,512]{2,1,0:T(8,128)(2,1)S(1)}, u32[]{:S(2)}, u32[]{:S(2)}) collective-permute-start(bf16[3,64,512]{2,1,0:T(8,128)(2,1)S(1)} %get-tuple-element.125), channel_id=1, source_target_pairs={{0,8},{8,16},{16,24},{24,32},{32,40},{40,48},{48,56},{56,64},{64,7... | collective-permute-start | bytes 589832 | tf_op jit(solution)/shard_map/ppermute | solution.py:28
  126.8 13.4 %collective-permute-start.26 = (bf16[3,64,512]{2,1,0:T(8,128)(2,1)S(1)}, bf16[3,64,512]{2,1,0:T(8,128)(2,1)S(1)}, u32[]{:S(2)}, u32[]{:S(2)}) collective-permute-start(bf16[3,64,512]{2,1,0:T(8,128)(2,1)S(1)} %get-tuple-element.126), channel_id=1, source_target_pairs={{0,112},{8,120},{16,0},{24,8},{32,16},{40,24},{48,32},{56,40},{64,... | collective-permute-start | bytes 589832 | tf_op jit(solution)/shard_map/ppermute | solution.py:28
  126.8 13.4 %collective-permute-start.27 = (bf16[3,64,512]{2,1,0:T(8,128)(2,1)S(1)}, bf16[3,64,512]{2,1,0:T(8,128)(2,1)S(1)}, u32[]{:S(2)}, u32[]{:S(2)}) collective-permute-start(bf16[3,64,512]{2,1,0:T(8,128)(2,1)S(1)} %get-tuple-element.127), channel_id=1, source_target_pairs={{0,16},{8,24},{16,32},{24,40},{32,48},{40,56},{48,64},{56,72},{64,... | collective-permute-start | bytes 589832 | tf_op jit(solution)/shard_map/ppermute | solution.py:28
